TPU v7x, 32 devices: a whole 2x2x4 slice. The times are simulated.
32 devices in a mesh: ep: 8 (over z, x), dp: 4 (over y, core).
Axes of the slice: x: 2, y: 2, z: 4, core: 2. Of those that a mesh axis runs over, the one named last changes fastest.
Arguments:
- tokens: bfloat16 [2048, 2048], P(('dp', 'ep')), parts along dimension 0, may hold values from -6 to 6
- gates: float32 [2048, 2], P(('dp', 'ep')), parts along dimension 0, may hold values from 0.05 to 1
- expert_ids: int32 [2048, 2], P(('dp', 'ep')), parts along dimension 0, may hold values from 0 to 1, all different within a row; in each aligned block of 64 rows (0 to 63, 64 to 127, ...) at most 64 rows name the same one
- slot_expert: int32 [8], P('dp'), parts along dimension 0, may hold values from 0 to 1, each once
- w_in: bfloat16 [32, 2, 192, 2048], P(('dp', 'ep')), parts along dimension 0, may hold values from -0.125 to 0.125
- w_out: bfloat16 [32, 192, 2048], P(('dp', 'ep')), parts along dimension 0, may hold values from -0.21875 to 0.21875
Outputs:
- mixed: bfloat16 [2048, 2048], P(('dp', 'ep')), parts along dimension 0
There are 4 independent parts, one for each index of `dp`. A program takes and returns all parts, laid end to end along the dimension named above; each array names one. Nothing has to cross between parts.
All inputs are finite; a program needn't handle non-finite values.
Results may differ from a plain program's by a relative error of at most 0.0058.
Values may be sent and summed in bfloat16 or wider, within the bound.
No kernel may reach another device: no remote copies, remote signals or barrier semaphores. Data moves between devices by JAX's collectives and lax.ppermute only.
A program may use at most 64 MiB of HBM per device.

v0:
```python
import jax
import jax.numpy as jnp
from jax import lax
from jax.sharding import PartitionSpec as P

GROUP = 4
BLOCK = 128


def from_partner(block, axis, apart):
    count = lax.axis_size(axis)
    route = []
    for low in range(count):
        high = low | 1 << apart
        if high != low and high < count:
            route += [(low, high), (high, low)]
    return lax.ppermute(block, axis, route)


def local(tokens, gates, expert_ids, slot_expert, w_in, w_out):
    members = lax.axis_size("ep")
    myself = lax.axis_index("ep")
    tok_rows, width = tokens.shape
    top_count = expert_ids.shape[1]
    experts = members // GROUP
    cap_expert = min(tok_rows, 5 * tok_rows * top_count // (4 * experts))
    cap_member = (cap_expert + GROUP - 1) // GROUP
    slot_total = members * cap_member
    block_limit = slot_total // BLOCK + 1
    expert_range = jnp.arange(experts, dtype=jnp.int32)
    home = jnp.sum(
        jnp.where(slot_expert[:, None] == expert_range[None, :], expert_range[:, None], 0), axis=0
    )
    pieces_in, pieces_out = (w_in, w_out)
    bit_order = (0, 1)
    for swap_bit in bit_order:
        other_in, other_out = from_partner((pieces_in, pieces_out), "ep", swap_bit)
        lower = myself // (1 << swap_bit) % 2 == 0
        pieces_in = jnp.where(
            lower,
            jnp.concatenate([pieces_in, other_in], axis=0),
            jnp.concatenate([other_in, pieces_in], axis=0),
        )
        pieces_out = jnp.where(
            lower,
            jnp.concatenate([pieces_out, other_out], axis=0),
            jnp.concatenate([other_out, pieces_out], axis=0),
        )
    flat_ids = expert_ids.reshape(-1)
    onehot = (flat_ids[:, None] == expert_range[None, :]).astype(jnp.int32)
    rank = jnp.sum(jnp.cumsum(onehot, axis=0) * onehot, axis=1) - 1
    group = jnp.sum(onehot * home[None, :], axis=1)
    member = rank // cap_member
    slot = rank % cap_member
    slot_index = (group * GROUP + member) * cap_member + slot
    repeated = jnp.repeat(tokens, top_count, axis=0)
    send_rows = jnp.zeros((slot_total, width), jnp.bfloat16).at[slot_index].set(repeated)
    send_flag = (
        jnp.zeros((slot_total,), jnp.bfloat16).at[slot_index].set(jnp.ones((), jnp.bfloat16))
    )
    recv_rows, recv_flag = (
        lax.all_to_all(send_rows, "ep", split_axis=0, concat_axis=0, tiled=True),
        lax.all_to_all(send_flag, "ep", split_axis=0, concat_axis=0, tiled=True),
    )
    valid = recv_flag > 0.5
    valid_count = jnp.sum(valid.astype(jnp.int32))
    blocks_total = (valid_count + BLOCK - 1) // BLOCK
    position = jnp.where(valid, jnp.cumsum(valid.astype(jnp.int32)) - 1, block_limit * BLOCK)
    compact = (
        jnp.zeros((block_limit * BLOCK, width), jnp.bfloat16)
        .at[position]
        .set(recv_rows, mode="drop")
    )
    gate_weights = pieces_in[:, 0]
    up_weights = pieces_in[:, 1]

    def compute_block(block, result):
        block_rows = lax.dynamic_slice_in_dim(compact, block * BLOCK, BLOCK, 0)
        gate_part = jnp.einsum(
            "rd,jfd->rjf", block_rows, gate_weights, preferred_element_type=jnp.float32
        )
        up_part = jnp.einsum(
            "rd,jfd->rjf", block_rows, up_weights, preferred_element_type=jnp.float32
        )
        hidden = (jax.nn.silu(gate_part) * up_part).astype(jnp.bfloat16)
        produced = jnp.einsum(
            "rjf,jfd->rd", hidden, pieces_out, preferred_element_type=jnp.float32
        ).astype(jnp.bfloat16)
        return lax.dynamic_update_slice_in_dim(result, produced, block * BLOCK, 0)

    computed = lax.fori_loop(
        0, blocks_total, compute_block, jnp.zeros((block_limit * BLOCK, width), jnp.bfloat16)
    )
    back_rows = jnp.where(
        valid[:, None],
        computed[jnp.minimum(position, block_limit * BLOCK - 1)],
        jnp.zeros((), jnp.bfloat16),
    )
    returned = lax.all_to_all(back_rows, "ep", split_axis=0, concat_axis=0, tiled=True)
    gathered = returned[slot_index].reshape(tok_rows, top_count, width)
    total = jnp.zeros((tok_rows, width), jnp.float32)
    for choice_index in range(top_count):
        total = total + gates[:, choice_index][:, None] * gathered[:, choice_index].astype(
            jnp.float32
        )
    return total.astype(jnp.bfloat16)


def solution(mesh):
    return jax.shard_map(
        local,
        mesh=mesh,
        in_specs=(
            P(("dp", "ep"), None),
            P(("dp", "ep"), None),
            P(("dp", "ep"), None),
            P("dp"),
            P(("dp", "ep"), None, None, None),
            P(("dp", "ep"), None, None),
        ),
        out_specs=P(("dp", "ep"), None),
        check_vma=False,
    )
```

profile of v0, /device:TPU:0, one launch (start us, length us, event | category | flops | bytes accessed | tf_op | source)
XLA Modules:
  0.0 211.1 jit_solution(5263734947999241226)
XLA Ops:
  0.0 2.9 %collective-permute-start = (bf16[1,2,192,2048]{3,2,0,1:T(8,128)(2,1)}, bf16[1,2,192,2048]{3,2,0,1:T(8,128)(2,1)S(1)}, u32[]{:S(2)}, u32[]{:S(2)}) collective-permute-start(bf16[1,2,192,2048]{3,2,0,1:T(8,128)(2,1)} %bitcast.61), channel_id=1, source_target_pairs={{0,4},{4,0},{8,12},{12,8},{16,20},{20,16},{24,28},{28,24},{1,5},{5... | collective-permute-start | bytes 4718600 | tf_op jit(solution)/shard_map/ppermute | solution.py:17
  2.9 34.6 %collective-permute-done = bf16[1,2,192,2048]{3,2,0,1:T(8,128)(2,1)S(1)} collective-permute-done((bf16[1,2,192,2048]{3,2,0,1:T(8,128)(2,1)}, bf16[1,2,192,2048]{3,2,0,1:T(8,128)(2,1)S(1)}, u32[]{:S(2)}, u32[]{:S(2)}) %collective-permute-start) | collective-permute-done | bytes 1572896 | tf_op jit(solution)/shard_map/ppermute | solution.py:17
  37.5 3.8 %maximum_select_fusion.1 = bf16[2,2,192,2048]{3,2,0,1:T(8,128)(2,1)} fusion(bf16[1,2,192,2048]{3,2,0,1:T(8,128)(2,1)S(1)} %collective-permute-done, bf16[1,2,192,2048]{3,2,0,1:T(8,128)(2,1)} %bitcast.62, pred[]{:T(512)S(6)} %eq.47), kind=kLoop, calls=%fused_computation.27 | loop fusion | flops 4718592 | bytes 6291457 | tf_op jit(solution)/shard_map/jit(_where)/select_n | solution.py:39
  41.4 1.8 collective-permute-start.1
  43.2 1.5 collective-permute-start.2
  44.7 0.1 copy.48
  44.8 0.1 eq.39
  44.9 16.4 %collective-permute-done.2 = bf16[1,192,2048]{2,1,0:T(8,128)(2,1)S(1)} collective-permute-done((bf16[1,192,2048]{2,1,0:T(8,128)(2,1)S(1)}, bf16[1,192,2048]{2,1,0:T(8,128)(2,1)S(1)}, u32[]{:S(2)}, u32[]{:S(2)}) %collective-permute-start.2) | collective-permute-done | bytes 786464 | tf_op jit(solution)/shard_map/ppermute | solution.py:17
  61.3 0.3 maximum_select_fusion.3
  61.6 0.6 collective-permute-start.3
  62.2 0.1 fusion.33
  62.3 0.2 reduce_window_sum.18
  62.4 0.1 fusion.37
  62.5 0.2 select_reduce_fusion
  62.7 0.1 copy.49
  62.8 0.1 copy.53
  63.0 0.2 fusion.34
  63.1 1.3 scatter_custom_fusion
  64.5 0.7 all_to_all.27
  65.2 5.7 %all-to-all-start = ((bf16[8,16,1]{1,2,0:T(2,128)(2,1)}), bf16[8,16,1]{1,2,0:T(2,128)(2,1)S(1)}, u32[]{:S(2)}, u32[]{:S(2)}) async-start(bf16[8,16,1]{1,2,0:T(2,128)(2,1)} %all_to_all.27), calls=%async_computation | async-start | bytes 8192 | tf_op jit(solution)/shard_map/all_to_all | solution.py:63
  70.9 0.3 broadcast_in_dim.58
  71.2 0.2 reshape.217
  71.4 2.1 %scatter_custom_fusion.1 = bf16[128,2048]{1,0:T(8,128)(2,1)} fusion(s32[128]{0:T(128)S(1)} %fusion.34, bf16[128,2048]{1,0:T(8,128)(2,1)S(1)} %reshape.217, bf16[]{:T(256)} %constant.106.clone.1), kind=kCustom, calls=%fused_computation.39 | custom fusion | bytes 524290 | tf_op jit(solution)/shard_map/scatter | solution.py:57
  73.6 73.9 %all-to-all-done = bf16[8,16,1]{1,2,0:T(2,128)(2,1)S(1)} async-done(((bf16[8,16,1]{1,2,0:T(2,128)(2,1)}), bf16[8,16,1]{1,2,0:T(2,128)(2,1)S(1)}, u32[]{:S(2)}, u32[]{:S(2)}) %all-to-all-start) | async-done | bytes 288 | tf_op jit(solution)/shard_map/all_to_all | solution.py:63
  147.5 3.5 %all-to-all-start.1 = ((bf16[8,16,2048]{2,1,0:T(8,128)(2,1)}), bf16[8,16,2048]{2,1,0:T(8,128)(2,1)S(1)}, u32[]{:S(2)}, u32[]{:S(2)}) async-start(bf16[8,16,2048]{2,1,0:T(8,128)(2,1)} %bitcast.6), calls=%async_computation.1 | async-start | bytes 1048576 | tf_op jit(solution)/shard_map/all_to_all | solution.py:62
  151.0 0.6 convert_reduce_fusion
  152.2 0.1 gt.34
  152.3 0.1 copy.57
  152.4 0.1 copy.56
  152.6 0.2 reduce-window.4
  152.7 0.1 fusion.30
  152.9 10.8 %all-to-all-done.1 = bf16[8,16,2048]{2,1,0:T(8,128)(2,1)S(1)} async-done(((bf16[8,16,2048]{2,1,0:T(8,128)(2,1)}), bf16[8,16,2048]{2,1,0:T(8,128)(2,1)S(1)}, u32[]{:S(2)}, u32[]{:S(2)}) %all-to-all-start.1) | async-done | bytes 524320 | tf_op jit(solution)/shard_map/all_to_all | solution.py:62
  163.6 2.4 %scatter_custom_fusion.2 = bf16[256,2048]{1,0:T(8,128)(2,1)} fusion(s32[128]{0:T(128)S(1)} %get-tuple-element.45, bf16[128,2048]{1,0:T(8,128)(2,1)S(1)} %bitcast.63, bf16[]{:T(256)} %constant.106.clone.1), kind=kCustom, calls=%fused_computation.34 | custom fusion | bytes 1048578 | tf_op jit(solution)/shard_map/scatter | solution.py:72
  166.1 3.1 %maximum_select_fusion.2 = bf16[4,192,2048]{2,1,0:T(8,128)(2,1)S(1)} fusion(bf16[2,192,2048]{2,1,0:T(8,128)(2,1)} %collective-permute-done.3, bf16[2,192,2048]{2,1,0:T(8,128)(2,1)} %copy-done, pred[]{:T(512)S(6)} %eq.46), kind=kLoop, calls=%fused_computation.28 | loop fusion | flops 4718592 | bytes 6291457 | tf_op jit(solution)/shard_map/jit(_where)/select_n | solution.py:44
  169.2 5.3 %maximum_select_fusion = bf16[4,2,192,2048]{3,2,0,1:T(8,128)(2,1)S(1)} fusion(bf16[2,2,192,2048]{3,2,0,1:T(8,128)(2,1)} %collective-permute-done.1, bf16[2,2,192,2048]{3,2,0,1:T(8,128)(2,1)} %maximum_select_fusion.1, pred[]{:T(512)S(6)} %eq.46), kind=kLoop, calls=%fused_computation.24 | loop fusion | flops 9437184 | bytes 12582913 | tf_op jit(solution)/shard_map/jit(_where)/select_n | solution.py:39
  174.5 3.2 %slice_bitcast_fusion = (bf16[4,192,2048]{2,1,0:T(8,128)(2,1)}, bf16[4,192,2048]{2,1,0:T(8,128)(2,1)}) fusion(bf16[4,2,192,2048]{3,2,0,1:T(8,128)(2,1)S(1)} %maximum_select_fusion), kind=kLoop, calls=%fused_computation.25 | loop fusion | bytes 12582912 | tf_op jit(solution)/shard_map/squeeze | solution.py:75
  177.7 1.1 broadcast.231
  178.9 8.1 %while.10 = (s32[]{:T(128)}, bf16[256,2048]{1,0:T(8,128)(2,1)}, s32[]{:T(128)}, bf16[256,2048]{1,0:T(8,128)(2,1)}, bf16[4,192,2048]{2,1,0:T(8,128)(2,1)}, /*inde...) while((s32[]{:T(128)}, bf16[256,2048]{1,0:T(8,128)(2,1)}, ...), condition=%wide.region_10.11_spmd, body=%wide.region_9.10_spmd.sunk | while | flops 1208811520 | bytes 11797663 | solution.py:91
  178.9 3.0 %fusion.56 = f32[128,4,192]{0,2,1:T(8,128)S(1)} fusion(bf16[4,192,2048]{2,1,0:T(8,128)(2,1)} %get-tuple-element.142, bf16[256,2048]{1,0:T(8,128)(2,1)} %get-tuple-element.141, s32[]{:T(128)S(6)} %select_n.199), kind=kOutput, calls=%fused_computation.11.clone.1 | convolution fusion | flops 402653184 | bytes 4063236 | tf_op jit(solution)/shard_map/while/body/rd,jfd->rjf/dot_general | solution.py:79
  181.9 5.1 %fusion.57 = bf16[256,2048]{1,0:T(8,128)(2,1)} fusion(bf16[256,2048]{1,0:T(8,128)(2,1)} %get-tuple-element.128, s32[]{:T(128)S(6)} %select_n.199, bf16[4,192,2048]{2,1,0:T(8,128)(2,1)S(1)} %get-tuple-element.144, bf16[4,192,2048]{2,1,0:T(8,128)(2,1)} %get-tuple-element.143, bf16[256,2048]{1,0:T(8,128)(2,1)} %get-tuple-element.141, ...), kind=kOutput, calls=%fused_computation.7.clone.1 | convolution fusion | flops 806158336 | bytes 7734272 | tf_op jit(solution)/shard_map/while/body/rjf,jfd->rd/dot_general | solution.py:86
  187.0 2.8 %gather_fusion = bf16[128,2048]{1,0:T(8,128)(2,1)S(1)} fusion(bf16[256,2048]{1,0:T(8,128)(2,1)} %get-tuple-element.43, s32[1024]{0:T(1024)S(1)} %pad_clamp_fusion.1), kind=kCustom, calls=%fused_computation | custom fusion | bytes 1049088 | tf_op jit(solution)/shard_map/gather | solution.py:96
  189.8 0.9 broadcast_select_fusion
  190.7 3.6 %all-to-all-start.2 = ((bf16[8,16,2048]{2,1,0:T(8,128)(2,1)}), bf16[8,16,2048]{2,1,0:T(8,128)(2,1)S(1)}, u32[]{:S(2)}, u32[]{:S(2)}) async-start(bf16[8,16,2048]{2,1,0:T(8,128)(2,1)} %broadcast_select_fusion), calls=%async_computation.2 | async-start | bytes 1048576 | tf_op jit(solution)/shard_map/all_to_all | solution.py:99
  194.4 13.6 %all-to-all-done.2 = bf16[8,16,2048]{2,1,0:T(8,128)(2,1)S(1)} async-done(((bf16[8,16,2048]{2,1,0:T(8,128)(2,1)}), bf16[8,16,2048]{2,1,0:T(8,128)(2,1)S(1)}, u32[]{:S(2)}, u32[]{:S(2)}) %all-to-all-start.2) | async-done | bytes 524320 | tf_op jit(solution)/shard_map/all_to_all | solution.py:99
  208.0 0.9 gather_fusion.1
  208.9 0.3 reshape.186
  209.3 0.7 fusion.40
  210.0 1.1 fusion.21
  (20 shorter events, 0.1 us)
Async XLA Ops:
  0.0 37.5 %collective-permute-start = (bf16[1,2,192,2048]{3,2,0,1:T(8,128)(2,1)}, bf16[1,2,192,2048]{3,2,0,1:T(8,128)(2,1)S(1)}, u32[]{:S(2)}, u32[]{:S(2)}) collective-permute-start(bf16[1,2,192,2048]{3,2,0,1:T(8,128)(2,1)} %bitcast.61), channel_id=1, source_target_pairs={{0,4},{4,0},{8,12},{12,8},{16,20},{20,16},{24,28},{28,24},{1,5},{5... | collective-permute-start | bytes 4718600 | tf_op jit(solution)/shard_map/ppermute | solution.py:17
  2.9 40.3 %copy-start.1 = (bf16[1,192,2048]{2,1,0:T(8,128)(2,1)S(1)}, bf16[1,192,2048]{2,1,0:T(8,128)(2,1)}, u32[]{:S(2)}) copy-start(bf16[1,192,2048]{2,1,0:T(8,128)(2,1)} %param.13) | copy-start | bytes 2359300
  2.9 41.8 %copy-start.3 = (s32[64,2]{0,1:T(2,128)S(1)}, s32[64,2]{0,1:T(2,128)}, u32[]{:S(2)}) copy-start(s32[64,2]{0,1:T(2,128)} %param.10) | copy-start | bytes 1540
  41.4 21.1 %copy-start.5 = (s32[2]{0:T(128)S(1)}, s32[2]{0:T(128)}, u32[]{:S(2)}) copy-start(s32[2]{0:T(128)} %param.11) | copy-start | bytes 28
  41.4 29.5 %copy-start.2 = (bf16[64,2048]{1,0:T(8,128)(2,1)S(1)}, bf16[64,2048]{1,0:T(8,128)(2,1)}, u32[]{:S(2)}) copy-start(bf16[64,2048]{1,0:T(8,128)(2,1)} %param.8) | copy-start | bytes 786436
  41.4 127.8 %collective-permute-start.1 = (bf16[2,2,192,2048]{3,2,0,1:T(8,128)(2,1)}, bf16[2,2,192,2048]{3,2,0,1:T(8,128)(2,1)}, u32[]{:S(2)}, u32[]{:S(2)}) collective-permute-start(bf16[2,2,192,2048]{3,2,0,1:T(8,128)(2,1)} %maximum_select_fusion.1), channel_id=1, source_target_pairs={{0,8},{8,0},{4,12},{12,4},{16,24},{24,16},{20,28},{28,20},{1,9},{9... | collective-permute-start | bytes 9437192 | tf_op jit(solution)/shard_map/ppermute | solution.py:17
  43.2 18.1 %collective-permute-start.2 = (bf16[1,192,2048]{2,1,0:T(8,128)(2,1)S(1)}, bf16[1,192,2048]{2,1,0:T(8,128)(2,1)S(1)}, u32[]{:S(2)}, u32[]{:S(2)}) collective-permute-start(bf16[1,192,2048]{2,1,0:T(8,128)(2,1)S(1)} %copy-done.1), channel_id=1, source_target_pairs={{0,4},{4,0},{8,12},{12,8},{16,20},{20,16},{24,28},{28,24},{1,5},{5... | collective-permute-start | bytes 2359304 | tf_op jit(solution)/shard_map/ppermute | solution.py:17
  61.6 104.5 %copy-start = (bf16[2,192,2048]{2,1,0:T(8,128)(2,1)}, bf16[2,192,2048]{2,1,0:T(8,128)(2,1)S(1)}, u32[]{:S(2)}) copy-start(bf16[2,192,2048]{2,1,0:T(8,128)(2,1)S(1)} %maximum_select_fusion.3) | copy-start | bytes 4718596
  61.6 104.5 %collective-permute-start.3 = (bf16[2,192,2048]{2,1,0:T(8,128)(2,1)S(1)}, bf16[2,192,2048]{2,1,0:T(8,128)(2,1)}, u32[]{:S(2)}, u32[]{:S(2)}) collective-permute-start(bf16[2,192,2048]{2,1,0:T(8,128)(2,1)S(1)} %maximum_select_fusion.3), channel_id=1, source_target_pairs={{0,8},{8,0},{4,12},{12,4},{16,24},{24,16},{20,28},{28,20},{1,9},{9... | collective-permute-start | bytes 4718600 | tf_op jit(solution)/shard_map/ppermute | solution.py:17
  65.2 82.3 %all-to-all-start = ((bf16[8,16,1]{1,2,0:T(2,128)(2,1)}), bf16[8,16,1]{1,2,0:T(2,128)(2,1)S(1)}, u32[]{:S(2)}, u32[]{:S(2)}) async-start(bf16[8,16,1]{1,2,0:T(2,128)(2,1)} %all_to_all.27), calls=%async_computation | async-start | bytes 8192 | tf_op jit(solution)/shard_map/all_to_all | solution.py:63
  147.5 16.1 %all-to-all-start.1 = ((bf16[8,16,2048]{2,1,0:T(8,128)(2,1)}), bf16[8,16,2048]{2,1,0:T(8,128)(2,1)S(1)}, u32[]{:S(2)}, u32[]{:S(2)}) async-start(bf16[8,16,2048]{2,1,0:T(8,128)(2,1)} %bitcast.6), calls=%async_computation.1 | async-start | bytes 1048576 | tf_op jit(solution)/shard_map/all_to_all | solution.py:62
  187.0 7.3 %copy-start.4 = (f32[64,2]{0,1:T(2,128)S(1)}, f32[64,2]{0,1:T(2,128)}, u32[]{:S(2)}) copy-start(f32[64,2]{0,1:T(2,128)} %param.9) | copy-start | bytes 1540
  190.7 17.3 %all-to-all-start.2 = ((bf16[8,16,2048]{2,1,0:T(8,128)(2,1)}), bf16[8,16,2048]{2,1,0:T(8,128)(2,1)S(1)}, u32[]{:S(2)}, u32[]{:S(2)}) async-start(bf16[8,16,2048]{2,1,0:T(8,128)(2,1)} %broadcast_select_fusion), calls=%async_computation.2 | async-start | bytes 1048576 | tf_op jit(solution)/shard_map/all_to_all | solution.py:99
where the time goes:
time: 212 us; the launch traced here: 211 us
  waiting for transfers between devices  149 us (70%)
  starting transfers between devices  19.7 us (9%)
  local copies, waits for them, and re-layouts  17.1 us (8%)
  other arithmetic  16.1 us (8%)
  matrix products  8.12 us (4%)
    all_to_all x1, waiting for transfers between devices, local(): lax.all_to_all(send_flag, 'ep', split_axis=0, concat_axis=0, tiled=True)  73.9 us
    ppermute x4, waiting for transfers between devices, from_partner(): return lax.ppermute(block, axis, route)  51 us
    all_to_all x1, waiting for transfers between devices, local(): lax.all_to_all(back_rows, 'ep', split_axis=0, concat_axis=0, tiled=True)  13.6 us
    all_to_all x1, waiting for transfers between devices, local(): lax.all_to_all(send_rows, 'ep', split_axis=0, concat_axis=0, tiled=True)  10.8 us
    select_n x2, other arithmetic, local(): jnp.where(lower, jnp.concatenate([pieces_in, other_in], axis=0), jnp.conc...  9.1 us
    ppermute x4, starting transfers between devices, from_partner(): return lax.ppermute(block, axis, route)  6.84 us
    all_to_all x1, starting transfers between devices, local(): lax.all_to_all(send_flag, 'ep', split_axis=0, concat_axis=0, tiled=True)  5.74 us
    dot_general x1, matrix products, compute_block(): jnp.einsum('rjf,jfd->rd', hidden, pieces_out, preferred_element_type=jnp....  5.08 us
  transfers between devices with their start and end apart: 7, of which 5 were waited for; matrix products, arithmetic and copies ran while one was open for 6% of the time, Pallas kernels for 0%

commit v1 on v0

--- a/solution.py
+++ b/solution.py
@@ -1,6 +1,10 @@
+import functools
+
 import jax
 import jax.numpy as jnp
 from jax import lax
+from jax.experimental import pallas as pl
+from jax.experimental.pallas import tpu as pltpu
 from jax.sharding import PartitionSpec as P
 
 GROUP = 4
@@ -17,7 +21,75 @@
     return lax.ppermute(block, axis, route)
 
 
-def local(tokens, gates, expert_ids, slot_expert, w_in, w_out):
+def from_member(block, apart):
+    count = lax.axis_size("ep")
+    return lax.ppermute(block, "ep", [(i, i ^ apart) for i in range(count)])
+
+
+def from_group(block, steps):
+    count = lax.axis_size("ep")
+    return lax.ppermute(block, "ep", [(i, (i - steps * GROUP) % count) for i in range(count)])
+
+
+def share_kernel(*refs):
+    n = (len(refs) - 2) // 2
+    w_in, w_out = refs[n], refs[n + 1]
+    rows = refs[0].shape[0]
+    x = jnp.concatenate([r[...] for r in refs[:n]], axis=0)
+    contract = (((1,), (1,)), ((), ()))
+    gate = lax.dot_general(x, w_in[0, 0], contract, preferred_element_type=jnp.float32)
+    up = lax.dot_general(x, w_in[0, 1], contract, preferred_element_type=jnp.float32)
+    hidden = (gate / (1.0 + jnp.exp(-gate)) * up).astype(jnp.bfloat16)
+    for i in range(n):
+        refs[n + 2 + i][...] = jnp.dot(
+            hidden[i * rows : (i + 1) * rows], w_out[0], preferred_element_type=jnp.float32
+        ).astype(jnp.bfloat16)
+
+
+def share(blocks, w_in, w_out):
+    rows, width = blocks[0].shape
+    units = w_out.shape[1]
+    n = len(blocks)
+    return pl.pallas_call(
+        share_kernel,
+        out_shape=[jax.ShapeDtypeStruct((rows, width), jnp.bfloat16)] * n,
+        in_specs=[pl.BlockSpec(memory_space=pltpu.VMEM)] * (n + 2),
+        out_specs=[pl.BlockSpec(memory_space=pltpu.VMEM)] * n,
+        compiler_params=pltpu.CompilerParams(vmem_limit_bytes=32 << 20),
+        cost_estimate=pl.CostEstimate(
+            flops=6 * n * rows * width * units,
+            bytes_accessed=2 * (2 * n * rows * width + 3 * units * width),
+            transcendentals=n * rows * units,
+        ),
+        name="share",
+    )(*blocks, w_in, w_out)
+
+
+def everywhere(tokens, gates, expert_ids, slot_expert, w_in, w_out):
+    experts = lax.axis_size("ep") // GROUP
+    my_group = lax.axis_index("ep") // GROUP
+    visitors = [from_group(tokens, s) for s in range(1, experts)]
+    held = [[tokens] + [from_member(tokens, m) for m in range(1, GROUP)]]
+    for rows in visitors:
+        held.append([rows] + [from_member(rows, m) for m in range(1, GROUP)])
+    sums = []
+    for blocks in held:
+        shares = share(blocks, w_in, w_out)
+        total = shares[0].astype(jnp.float32)
+        for m in range(1, GROUP):
+            total = total + from_member(shares[m], m).astype(jnp.float32)
+        sums.append(total.astype(jnp.bfloat16))
+    mixed = jnp.zeros(tokens.shape, jnp.float32)
+    for s in range(experts):
+        rows = sums[0] if s == 0 else from_group(sums[s], experts - s)
+        source = (my_group + (experts - s if s else 0)) % experts
+        named = lax.dynamic_index_in_dim(slot_expert, source, 0, keepdims=False)
+        weight = jnp.sum(jnp.where(expert_ids == named, gates, 0.0), axis=1, keepdims=True)
+        mixed = mixed + weight * rows.astype(jnp.float32)
+    return mixed.astype(jnp.bfloat16)
+
+
+def routed(tokens, gates, expert_ids, slot_expert, w_in, w_out):
     members = lax.axis_size("ep")
     myself = lax.axis_index("ep")
     tok_rows, width = tokens.shape
@@ -104,6 +176,11 @@
             jnp.float32
         )
     return total.astype(jnp.bfloat16)
+
+
+def local(tokens, gates, expert_ids, slot_expert, w_in, w_out):
+    plan = everywhere if expert_ids.shape[1] == slot_expert.shape[0] else routed
+    return plan(tokens, gates, expert_ids, slot_expert, w_in, w_out)
 
 
 def solution(mesh):

time: 212 us -> 71.1 us (0.34)
  waiting for transfers between devices: 149 us -> 42.3 us
  local copies, waits for them, and re-layouts: 17.1 us -> 3.15 us
  other arithmetic: 16.1 us -> 2.29 us
  matrix products: 8.12 us -> 0 us
  Pallas kernels: 0 us -> 2.75 us
    all_to_all x3 -> x0, waiting for transfers between devices: 98.3 us -> none  [the longest x1 73.9 us: local(): lax.all_to_all(send_flag, 'ep', split_axis=0, concat_axis=0, tiled=True)]
    select_n x7 -> x0, other arithmetic: 13.6 us -> none  [the longest x2 9.1 us: local(): jnp.where(lower, jnp.concatenate([pieces_in, other_in], axis=0), jnp.conc...]
    ppermute x4 -> x14, starting transfers between devices: 6.84 us -> 20.1 us  [the longest x12 14 us: from_member(): return lax.ppermute(block, 'ep', [(i, i ^ apart) for i in range(count)])]
    all_to_all x3 -> x0, starting transfers between devices: 12.8 us -> none  [the longest x1 5.74 us: local(): lax.all_to_all(send_flag, 'ep', split_axis=0, concat_axis=0, tiled=True)]
    ppermute x4 -> x14, waiting for transfers between devices: 51 us -> 42.3 us  [the longest x12 30.2 us: from_member(): return lax.ppermute(block, 'ep', [(i, i ^ apart) for i in range(count)])]
    dot_general x2 -> x0, matrix products: 8.12 us -> none  [the longest x1 5.08 us: compute_block(): jnp.einsum('rjf,jfd->rd', hidden, pieces_out, preferred_element_type=jnp....]
    scatter x3 -> x0, local copies, waits for them, and re-layouts: 5.93 us -> none  [the longest x1 2.44 us: local(): compact = jnp.zeros((block_limit * BLOCK, width), jnp.bfloat16).at[positi...]
    gather x2 -> x0, local copies, waits for them, and re-layouts: 3.75 us -> none  [the longest x1 2.81 us: local(): computed[jnp.minimum(position, block_limit * BLOCK - 1)]]
  transfers between devices with their start and end apart: 7 -> 14, of which waited for: 5 -> 8; matrix products, arithmetic and copies ran while one was open for 6% -> 3% of each run, Pallas kernels for 0% -> 4%
where the time goes in v1:
time: 71.1 us; the launch traced here: 70.7 us
  waiting for transfers between devices  42.3 us (59%)
  starting transfers between devices  20.1 us (28%)
  local copies, waits for them, and re-layouts  3.15 us (4%)
  Pallas kernels  2.75 us (4%)
  other arithmetic  2.29 us (3%)
    ppermute x12, waiting for transfers between devices, from_member(): return lax.ppermute(block, 'ep', [(i, i ^ apart) for i in range(count)])  30.2 us
    ppermute x12, starting transfers between devices, from_member(): return lax.ppermute(block, 'ep', [(i, i ^ apart) for i in range(count)])  14 us
    ppermute x2, waiting for transfers between devices, from_group(): lax.ppermute(block, 'ep', [(i, (i - steps * GROUP) % count) for i in rang...  12.1 us
    ppermute x2, starting transfers between devices, from_group(): lax.ppermute(block, 'ep', [(i, (i - steps * GROUP) % count) for i in rang...  6.08 us
    pallas_call x2, Pallas kernels, share(): pl.pallas_call(share_kernel, out_shape=[jax.ShapeDtypeStruct((rows, width...  2.75 us
    unnamed x16, local copies, waits for them, and re-layouts  2.56 us
  transfers between devices with their start and end apart: 14, of which 8 were waited for; matrix products, arithmetic and copies ran while one was open for 3% of the time, Pallas kernels for 4%

profile of v1, /device:TPU:0, one launch (start us, length us, event | category | flops | bytes accessed | tf_op | source)
XLA Modules:
  0.0 70.7 jit_solution(18445312154874969831)
XLA Ops:
  0.0 4.0 %collective-permute-start.6 = (bf16[64,2048]{1,0:T(8,128)(2,1)}, bf16[64,2048]{1,0:T(8,128)(2,1)S(1)}, u32[]{:S(2)}, u32[]{:S(2)}) collective-permute-start(bf16[64,2048]{1,0:T(8,128)(2,1)} %refs_0_.1), channel_id=1, source_target_pairs={{0,16},{4,20},{8,24},{12,28},{16,0},{20,4},{24,8},{28,12},{1,17},{... | collective-permute-start | bytes 786440 | tf_op jit(solution)/shard_map/ppermute | solution.py:31
  4.0 12.1 %collective-permute-done.6.refs_0_ = bf16[64,2048]{1,0:T(8,128)(2,1)S(1)} collective-permute-done((bf16[64,2048]{1,0:T(8,128)(2,1)}, bf16[64,2048]{1,0:T(8,128)(2,1)S(1)}, u32[]{:S(2)}, u32[]{:S(2)}) %collective-permute-start.6) | collective-permute-done | bytes 262176 | tf_op jit(solution)/shard_map/ppermute | solution.py:31
  16.2 1.5 %collective-permute-start.7 = (bf16[64,2048]{1,0:T(8,128)(2,1)S(1)}, bf16[64,2048]{1,0:T(8,128)(2,1)S(1)}, u32[]{:S(2)}, u32[]{:S(2)}) collective-permute-start(bf16[64,2048]{1,0:T(8,128)(2,1)S(1)} %collective-permute-done.6.refs_0_), channel_id=1, source_target_pairs={{0,4},{4,0},{8,12},{12,8},{16,20},{20,16},{24,28},{28,24},{1,5},{5... | collective-permute-start | bytes 786440 | tf_op jit(solution)/shard_map/ppermute | solution.py:26
  17.7 0.8 %collective-permute-start.8 = (bf16[64,2048]{1,0:T(8,128)(2,1)S(1)}, bf16[64,2048]{1,0:T(8,128)(2,1)S(1)}, u32[]{:S(2)}, u32[]{:S(2)}) collective-permute-start(bf16[64,2048]{1,0:T(8,128)(2,1)S(1)} %collective-permute-done.6.refs_0_), channel_id=1, source_target_pairs={{0,8},{4,12},{8,0},{12,4},{16,24},{20,28},{24,16},{28,20},{1,9},{5... | collective-permute-start | bytes 786440 | tf_op jit(solution)/shard_map/ppermute | solution.py:26
  18.5 1.2 %collective-permute-start.9 = (bf16[64,2048]{1,0:T(8,128)(2,1)S(1)}, bf16[64,2048]{1,0:T(8,128)(2,1)S(1)}, u32[]{:S(2)}, u32[]{:S(2)}) collective-permute-start(bf16[64,2048]{1,0:T(8,128)(2,1)S(1)} %collective-permute-done.6.refs_0_), channel_id=1, source_target_pairs={{0,12},{4,8},{8,4},{12,0},{16,28},{20,24},{24,20},{28,16},{1,13},{... | collective-permute-start | bytes 786440 | tf_op jit(solution)/shard_map/ppermute | solution.py:26
  19.7 1.5 %collective-permute-start = (bf16[64,2048]{1,0:T(8,128)(2,1)}, bf16[64,2048]{1,0:T(8,128)(2,1)S(1)}, u32[]{:S(2)}, u32[]{:S(2)}) collective-permute-start(bf16[64,2048]{1,0:T(8,128)(2,1)} %refs_0_.1), channel_id=1, source_target_pairs={{0,4},{4,0},{8,12},{12,8},{16,20},{20,16},{24,28},{28,24},{1,5},{5... | collective-permute-start | bytes 786440 | tf_op jit(solution)/shard_map/ppermute | solution.py:26
  21.2 0.8 %collective-permute-start.1 = (bf16[64,2048]{1,0:T(8,128)(2,1)}, bf16[64,2048]{1,0:T(8,128)(2,1)S(1)}, u32[]{:S(2)}, u32[]{:S(2)}) collective-permute-start(bf16[64,2048]{1,0:T(8,128)(2,1)} %refs_0_.1), channel_id=1, source_target_pairs={{0,8},{4,12},{8,0},{12,4},{16,24},{20,28},{24,16},{28,20},{1,9},{5... | collective-permute-start | bytes 786440 | tf_op jit(solution)/shard_map/ppermute | solution.py:26
  22.0 7.5 %collective-permute-done.7.refs_1_ = bf16[64,2048]{1,0:T(8,128)(2,1)S(1)} collective-permute-done((bf16[64,2048]{1,0:T(8,128)(2,1)S(1)}, bf16[64,2048]{1,0:T(8,128)(2,1)S(1)}, u32[]{:S(2)}, u32[]{:S(2)}) %collective-permute-start.7) | collective-permute-done | bytes 262176 | tf_op jit(solution)/shard_map/ppermute | solution.py:26
  29.5 0.0 collective-permute-start.2
  29.5 0.0 collective-permute-done.8.refs_2_
  29.5 3.0 %collective-permute-done.9.refs_3_ = bf16[64,2048]{1,0:T(8,128)(2,1)S(1)} collective-permute-done((bf16[64,2048]{1,0:T(8,128)(2,1)S(1)}, bf16[64,2048]{1,0:T(8,128)(2,1)S(1)}, u32[]{:S(2)}, u32[]{:S(2)}) %collective-permute-start.9) | collective-permute-done | bytes 262176 | tf_op jit(solution)/shard_map/ppermute | solution.py:26
  32.5 0.0 copy-start
  32.5 1.4 %copy-done = bf16[1,2,192,2048]{3,2,1,0:T(8,128)(2,1)S(1)} copy-done((bf16[1,2,192,2048]{3,2,1,0:T(8,128)(2,1)S(1)}, bf16[1,2,192,2048]{3,2,1,0:T(8,128)(2,1)}, u32[]{:S(2)}) %copy-start) | copy-done | bytes 1572888
  33.9 0.0 copy-start.2
  33.9 1.1 %copy-done.2 = bf16[1,192,2048]{2,1,0:T(8,128)(2,1)S(1)} copy-done((bf16[1,192,2048]{2,1,0:T(8,128)(2,1)S(1)}, bf16[1,192,2048]{2,1,0:T(8,128)(2,1)}, u32[]{:S(2)}) %copy-start.2) | copy-done | bytes 786456
  35.1 0.0 copy-start.1
  35.1 0.0 copy-start.3
  35.1 0.0 copy-start.4
  35.1 1.4 %share.3 = (bf16[64,2048]{1,0:T(8,128)(2,1)S(1)}, bf16[64,2048]{1,0:T(8,128)(2,1)S(1)}, bf16[64,2048]{1,0:T(8,128)(2,1)S(1)}, bf16[64,2048]{1,0:T(8,128)(2,1)S(1)}) custom-call(bf16[64,2048]{1,0:T(8,128)(2,1)S(1)} %collective-permute-done.6.refs_0_, bf16[64,2048]{1,0:T(8,128)(2,1)S(1)} %collective-permute-done.7.refs_1_, ...), custom_call_target="tpu_custom_call" | custom-call | flops 603979776 | bytes 4456448 | tf_op jit(solution)/shard_map/share/pallas_call | solution.py:53
  36.5 1.8 %collective-permute-start.12 = (bf16[64,2048]{1,0:T(8,128)(2,1)S(1)}, bf16[64,2048]{1,0:T(8,128)(2,1)S(1)}, u32[]{:S(2)}, u32[]{:S(2)}) collective-permute-start(bf16[64,2048]{1,0:T(8,128)(2,1)S(1)} %get-tuple-element.20), channel_id=1, source_target_pairs={{0,12},{4,8},{8,4},{12,0},{16,28},{20,24},{24,20},{28,16},{1,13},{... | collective-permute-start | bytes 786440 | tf_op jit(solution)/shard_map/ppermute | solution.py:26
  38.3 1.3 %collective-permute-start.11 = (bf16[64,2048]{1,0:T(8,128)(2,1)S(1)}, bf16[64,2048]{1,0:T(8,128)(2,1)S(1)}, u32[]{:S(2)}, u32[]{:S(2)}) collective-permute-start(bf16[64,2048]{1,0:T(8,128)(2,1)S(1)} %get-tuple-element.19), channel_id=1, source_target_pairs={{0,8},{4,12},{8,0},{12,4},{16,24},{20,28},{24,16},{28,20},{1,9},{5... | collective-permute-start | bytes 786440 | tf_op jit(solution)/shard_map/ppermute | solution.py:26
  39.5 0.0 collective-permute-done.refs_1_
  39.5 0.0 copy-start.5
  39.6 0.5 collective-permute-start.10
  40.1 0.0 collective-permute-done.1.refs_2_
  40.1 3.8 %collective-permute-done.2.refs_3_ = bf16[64,2048]{1,0:T(8,128)(2,1)S(1)} collective-permute-done((bf16[64,2048]{1,0:T(8,128)(2,1)}, bf16[64,2048]{1,0:T(8,128)(2,1)S(1)}, u32[]{:S(2)}, u32[]{:S(2)}) %collective-permute-start.2) | collective-permute-done | bytes 262176 | tf_op jit(solution)/shard_map/ppermute | solution.py:26
  43.9 0.0 copy-done.1
  43.9 0.0 copy-done.3
  43.9 0.0 copy-done.4
  43.9 1.4 %share.2 = (bf16[64,2048]{1,0:T(8,128)(2,1)S(1)}, bf16[64,2048]{1,0:T(8,128)(2,1)S(1)}, bf16[64,2048]{1,0:T(8,128)(2,1)S(1)}, bf16[64,2048]{1,0:T(8,128)(2,1)S(1)}) custom-call(bf16[64,2048]{1,0:T(8,128)(2,1)S(1)} %copy-done.4, bf16[64,2048]{1,0:T(8,128)(2,1)S(1)} %collective-permute-done.refs_1_, bf16[64,2048]{1,0:T(8,128)(2,1)S(1)} %collective-permute-done.1.refs_2_, ...), custom_call_target="tpu_custom_call" | custom-call | flops 603979776 | bytes 4456448 | tf_op jit(solution)/shard_map/share/pallas_call | solution.py:53
  45.3 1.8 %collective-permute-start.5 = (bf16[64,2048]{1,0:T(8,128)(2,1)S(1)}, bf16[64,2048]{1,0:T(8,128)(2,1)S(1)}, u32[]{:S(2)}, u32[]{:S(2)}) collective-permute-start(bf16[64,2048]{1,0:T(8,128)(2,1)S(1)} %get-tuple-element.16), channel_id=1, source_target_pairs={{0,12},{4,8},{8,4},{12,0},{16,28},{20,24},{24,20},{28,16},{1,13},{... | collective-permute-start | bytes 786440 | tf_op jit(solution)/shard_map/ppermute | solution.py:26
  47.1 1.3 %collective-permute-start.4 = (bf16[64,2048]{1,0:T(8,128)(2,1)S(1)}, bf16[64,2048]{1,0:T(8,128)(2,1)S(1)}, u32[]{:S(2)}, u32[]{:S(2)}) collective-permute-start(bf16[64,2048]{1,0:T(8,128)(2,1)S(1)} %get-tuple-element.15), channel_id=1, source_target_pairs={{0,8},{4,12},{8,0},{12,4},{16,24},{20,28},{24,16},{28,20},{1,9},{5... | collective-permute-start | bytes 786440 | tf_op jit(solution)/shard_map/ppermute | solution.py:26
  48.3 1.1 %collective-permute-done.12 = bf16[64,2048]{1,0:T(8,128)(2,1)S(1)} collective-permute-done((bf16[64,2048]{1,0:T(8,128)(2,1)S(1)}, bf16[64,2048]{1,0:T(8,128)(2,1)S(1)}, u32[]{:S(2)}, u32[]{:S(2)}) %collective-permute-start.12) | collective-permute-done | bytes 262176 | tf_op jit(solution)/shard_map/ppermute | solution.py:26
  49.4 1.5 %collective-permute-start.3 = (bf16[64,2048]{1,0:T(8,128)(2,1)S(1)}, bf16[64,2048]{1,0:T(8,128)(2,1)S(1)}, u32[]{:S(2)}, u32[]{:S(2)}) collective-permute-start(bf16[64,2048]{1,0:T(8,128)(2,1)S(1)} %get-tuple-element.14), channel_id=1, source_target_pairs={{0,4},{4,0},{8,12},{12,8},{16,20},{20,16},{24,28},{28,24},{1,5},{5... | collective-permute-start | bytes 786440 | tf_op jit(solution)/shard_map/ppermute | solution.py:26
  51.0 4.2 %collective-permute-done.11 = bf16[64,2048]{1,0:T(8,128)(2,1)S(1)} collective-permute-done((bf16[64,2048]{1,0:T(8,128)(2,1)S(1)}, bf16[64,2048]{1,0:T(8,128)(2,1)S(1)}, u32[]{:S(2)}, u32[]{:S(2)}) %collective-permute-start.11) | collective-permute-done | bytes 262176 | tf_op jit(solution)/shard_map/ppermute | solution.py:26
  55.1 0.0 collective-permute-done.10
  55.1 0.1 add_convert_fusion.1
  55.3 2.0 %collective-permute-start.13 = (bf16[64,2048]{1,0:T(8,128)(2,1)S(1)}, bf16[64,2048]{1,0:T(8,128)(2,1)S(1)}, u32[]{:S(2)}, u32[]{:S(2)}) collective-permute-start(bf16[64,2048]{1,0:T(8,128)(2,1)S(1)} %add_convert_fusion.1), channel_id=1, source_target_pairs={{0,16},{4,20},{8,24},{12,28},{16,0},{20,4},{24,8},{28,12},{1,17},{... | collective-permute-start | bytes 786440 | tf_op jit(solution)/shard_map/ppermute | solution.py:31
  57.3 0.0 copy-done.5
  57.3 0.6 fusion.2
  57.9 0.0 copy-done.6
  57.9 0.0 copy-done.7
  57.9 1.2 %fusion = (f32[64]{0:T(128)S(1)}, f32[64]{0:T(128)S(1)}) fusion(f32[64,2]{0,1:T(2,128)S(1)} %copy-done.6, s32[64,2]{0,1:T(2,128)S(1)} %copy-done.7, s32[]{:T(128)} %bitcast, s32[]{:T(128)} %bitcast.1), kind=kLoop, calls=%fused_computation.5 | loop fusion | flops 640 | bytes 1544 | tf_op jit(solution)/shard_map/reduce_sum | solution.py:87
  59.1 7.2 %collective-permute-done.5 = bf16[64,2048]{1,0:T(8,128)(2,1)S(1)} collective-permute-done((bf16[64,2048]{1,0:T(8,128)(2,1)S(1)}, bf16[64,2048]{1,0:T(8,128)(2,1)S(1)}, u32[]{:S(2)}, u32[]{:S(2)}) %collective-permute-start.5) | collective-permute-done | bytes 262176 | tf_op jit(solution)/shard_map/ppermute | solution.py:26
  66.3 3.4 %collective-permute-done.4 = bf16[64,2048]{1,0:T(8,128)(2,1)S(1)} collective-permute-done((bf16[64,2048]{1,0:T(8,128)(2,1)S(1)}, bf16[64,2048]{1,0:T(8,128)(2,1)S(1)}, u32[]{:S(2)}, u32[]{:S(2)}) %collective-permute-start.4) | collective-permute-done | bytes 262176 | tf_op jit(solution)/shard_map/ppermute | solution.py:26
  69.8 0.0 collective-permute-done.3
  69.8 0.0 collective-permute-done.13
  69.8 0.9 %add_convert_fusion = bf16[64,2048]{1,0:T(8,128)(2,1)} fusion(bf16[64,2048]{1,0:T(8,128)(2,1)S(1)} %collective-permute-done.13, bf16[64,2048]{1,0:T(8,128)(2,1)S(1)} %collective-permute-done.5, bf16[64,2048]{1,0:T(8,128)(2,1)S(1)} %collective-permute-done.4, bf16[64,2048]{1,0:T(8,128)(2,1)S(1)} %collective-permute-done.3, ...), kind=kLoop, calls=%fused_computation | loop fusion | flops 1835008 | bytes 1573376 | tf_op jit(solution)/shard_map/convert_element_type | solution.py:89
  (2 shorter events, 0.0 us)
Async XLA Ops:
  0.0 16.2 %collective-permute-start.6 = (bf16[64,2048]{1,0:T(8,128)(2,1)}, bf16[64,2048]{1,0:T(8,128)(2,1)S(1)}, u32[]{:S(2)}, u32[]{:S(2)}) collective-permute-start(bf16[64,2048]{1,0:T(8,128)(2,1)} %refs_0_.1), channel_id=1, source_target_pairs={{0,16},{4,20},{8,24},{12,28},{16,0},{20,4},{24,8},{28,12},{1,17},{... | collective-permute-start | bytes 786440 | tf_op jit(solution)/shard_map/ppermute | solution.py:31
  16.2 13.3 %collective-permute-start.7 = (bf16[64,2048]{1,0:T(8,128)(2,1)S(1)}, bf16[64,2048]{1,0:T(8,128)(2,1)S(1)}, u32[]{:S(2)}, u32[]{:S(2)}) collective-permute-start(bf16[64,2048]{1,0:T(8,128)(2,1)S(1)} %collective-permute-done.6.refs_0_), channel_id=1, source_target_pairs={{0,4},{4,0},{8,12},{12,8},{16,20},{20,16},{24,28},{28,24},{1,5},{5... | collective-permute-start | bytes 786440 | tf_op jit(solution)/shard_map/ppermute | solution.py:26
  17.7 11.8 %collective-permute-start.8 = (bf16[64,2048]{1,0:T(8,128)(2,1)S(1)}, bf16[64,2048]{1,0:T(8,128)(2,1)S(1)}, u32[]{:S(2)}, u32[]{:S(2)}) collective-permute-start(bf16[64,2048]{1,0:T(8,128)(2,1)S(1)} %collective-permute-done.6.refs_0_), channel_id=1, source_target_pairs={{0,8},{4,12},{8,0},{12,4},{16,24},{20,28},{24,16},{28,20},{1,9},{5... | collective-permute-start | bytes 786440 | tf_op jit(solution)/shard_map/ppermute | solution.py:26
  18.5 14.0 %collective-permute-start.9 = (bf16[64,2048]{1,0:T(8,128)(2,1)S(1)}, bf16[64,2048]{1,0:T(8,128)(2,1)S(1)}, u32[]{:S(2)}, u32[]{:S(2)}) collective-permute-start(bf16[64,2048]{1,0:T(8,128)(2,1)S(1)} %collective-permute-done.6.refs_0_), channel_id=1, source_target_pairs={{0,12},{4,8},{8,4},{12,0},{16,28},{20,24},{24,20},{28,16},{1,13},{... | collective-permute-start | bytes 786440 | tf_op jit(solution)/shard_map/ppermute | solution.py:26
  19.7 19.9 %collective-permute-start = (bf16[64,2048]{1,0:T(8,128)(2,1)}, bf16[64,2048]{1,0:T(8,128)(2,1)S(1)}, u32[]{:S(2)}, u32[]{:S(2)}) collective-permute-start(bf16[64,2048]{1,0:T(8,128)(2,1)} %refs_0_.1), channel_id=1, source_target_pairs={{0,4},{4,0},{8,12},{12,8},{16,20},{20,16},{24,28},{28,24},{1,5},{5... | collective-permute-start | bytes 786440 | tf_op jit(solution)/shard_map/ppermute | solution.py:26
  21.2 18.9 %collective-permute-start.1 = (bf16[64,2048]{1,0:T(8,128)(2,1)}, bf16[64,2048]{1,0:T(8,128)(2,1)S(1)}, u32[]{:S(2)}, u32[]{:S(2)}) collective-permute-start(bf16[64,2048]{1,0:T(8,128)(2,1)} %refs_0_.1), channel_id=1, source_target_pairs={{0,8},{4,12},{8,0},{12,4},{16,24},{20,28},{24,16},{28,20},{1,9},{5... | collective-permute-start | bytes 786440 | tf_op jit(solution)/shard_map/ppermute | solution.py:26
  29.5 14.4 %collective-permute-start.2 = (bf16[64,2048]{1,0:T(8,128)(2,1)}, bf16[64,2048]{1,0:T(8,128)(2,1)S(1)}, u32[]{:S(2)}, u32[]{:S(2)}) collective-permute-start(bf16[64,2048]{1,0:T(8,128)(2,1)} %refs_0_.1), channel_id=1, source_target_pairs={{0,12},{4,8},{8,4},{12,0},{16,28},{20,24},{24,20},{28,16},{1,13},{... | collective-permute-start | bytes 786440 | tf_op jit(solution)/shard_map/ppermute | solution.py:26
  32.5 1.4 %copy-start = (bf16[1,2,192,2048]{3,2,1,0:T(8,128)(2,1)S(1)}, bf16[1,2,192,2048]{3,2,1,0:T(8,128)(2,1)}, u32[]{:S(2)}) copy-start(bf16[1,2,192,2048]{3,2,1,0:T(8,128)(2,1)} %refs_4_.3) | copy-start | bytes 4718596
  33.9 1.1 %copy-start.2 = (bf16[1,192,2048]{2,1,0:T(8,128)(2,1)S(1)}, bf16[1,192,2048]{2,1,0:T(8,128)(2,1)}, u32[]{:S(2)}) copy-start(bf16[1,192,2048]{2,1,0:T(8,128)(2,1)} %refs_5_.3) | copy-start | bytes 2359300
  35.1 8.8 %copy-start.1 = (bf16[1,2,192,2048]{3,2,1,0:T(8,128)(2,1)S(1)}, bf16[1,2,192,2048]{3,2,1,0:T(8,128)(2,1)}, u32[]{:S(2)}) copy-start(bf16[1,2,192,2048]{3,2,1,0:T(8,128)(2,1)} %refs_4_.3) | copy-start | bytes 4718596
  35.1 8.8 %copy-start.3 = (bf16[1,192,2048]{2,1,0:T(8,128)(2,1)S(1)}, bf16[1,192,2048]{2,1,0:T(8,128)(2,1)}, u32[]{:S(2)}) copy-start(bf16[1,192,2048]{2,1,0:T(8,128)(2,1)} %refs_5_.3) | copy-start | bytes 2359300
  35.1 8.8 %copy-start.4 = (bf16[64,2048]{1,0:T(8,128)(2,1)S(1)}, bf16[64,2048]{1,0:T(8,128)(2,1)}, u32[]{:S(2)}) copy-start(bf16[64,2048]{1,0:T(8,128)(2,1)} %refs_0_.1) | copy-start | bytes 786436
  36.5 13.0 %collective-permute-start.12 = (bf16[64,2048]{1,0:T(8,128)(2,1)S(1)}, bf16[64,2048]{1,0:T(8,128)(2,1)S(1)}, u32[]{:S(2)}, u32[]{:S(2)}) collective-permute-start(bf16[64,2048]{1,0:T(8,128)(2,1)S(1)} %get-tuple-element.20), channel_id=1, source_target_pairs={{0,12},{4,8},{8,4},{12,0},{16,28},{20,24},{24,20},{28,16},{1,13},{... | collective-permute-start | bytes 786440 | tf_op jit(solution)/shard_map/ppermute | solution.py:26
  38.3 16.9 %collective-permute-start.11 = (bf16[64,2048]{1,0:T(8,128)(2,1)S(1)}, bf16[64,2048]{1,0:T(8,128)(2,1)S(1)}, u32[]{:S(2)}, u32[]{:S(2)}) collective-permute-start(bf16[64,2048]{1,0:T(8,128)(2,1)S(1)} %get-tuple-element.19), channel_id=1, source_target_pairs={{0,8},{4,12},{8,0},{12,4},{16,24},{20,28},{24,16},{28,20},{1,9},{5... | collective-permute-start | bytes 786440 | tf_op jit(solution)/shard_map/ppermute | solution.py:26
  39.5 17.8 %copy-start.5 = (s32[2]{0:T(128)S(1)}, s32[2]{0:T(128)}, u32[]{:S(2)}) copy-start(s32[2]{0:T(128)} %param.9) | copy-start | bytes 28
  39.5 18.4 %copy-start.6 = (f32[64,2]{0,1:T(2,128)S(1)}, f32[64,2]{0,1:T(2,128)}, u32[]{:S(2)}) copy-start(f32[64,2]{0,1:T(2,128)} %param.7) | copy-start | bytes 1540
  39.5 18.4 %copy-start.7 = (s32[64,2]{0,1:T(2,128)S(1)}, s32[64,2]{0,1:T(2,128)}, u32[]{:S(2)}) copy-start(s32[64,2]{0,1:T(2,128)} %param.8) | copy-start | bytes 1540
  39.6 15.6 %collective-permute-start.10 = (bf16[64,2048]{1,0:T(8,128)(2,1)S(1)}, bf16[64,2048]{1,0:T(8,128)(2,1)S(1)}, u32[]{:S(2)}, u32[]{:S(2)}) collective-permute-start(bf16[64,2048]{1,0:T(8,128)(2,1)S(1)} %get-tuple-element.18), channel_id=1, source_target_pairs={{0,4},{4,0},{8,12},{12,8},{16,20},{20,16},{24,28},{28,24},{1,5},{5... | collective-permute-start | bytes 786440 | tf_op jit(solution)/shard_map/ppermute | solution.py:26
  45.3 21.1 %collective-permute-start.5 = (bf16[64,2048]{1,0:T(8,128)(2,1)S(1)}, bf16[64,2048]{1,0:T(8,128)(2,1)S(1)}, u32[]{:S(2)}, u32[]{:S(2)}) collective-permute-start(bf16[64,2048]{1,0:T(8,128)(2,1)S(1)} %get-tuple-element.16), channel_id=1, source_target_pairs={{0,12},{4,8},{8,4},{12,0},{16,28},{20,24},{24,20},{28,16},{1,13},{... | collective-permute-start | bytes 786440 | tf_op jit(solution)/shard_map/ppermute | solution.py:26
  47.1 22.7 %collective-permute-start.4 = (bf16[64,2048]{1,0:T(8,128)(2,1)S(1)}, bf16[64,2048]{1,0:T(8,128)(2,1)S(1)}, u32[]{:S(2)}, u32[]{:S(2)}) collective-permute-start(bf16[64,2048]{1,0:T(8,128)(2,1)S(1)} %get-tuple-element.15), channel_id=1, source_target_pairs={{0,8},{4,12},{8,0},{12,4},{16,24},{20,28},{24,16},{28,20},{1,9},{5... | collective-permute-start | bytes 786440 | tf_op jit(solution)/shard_map/ppermute | solution.py:26
  49.4 20.3 %collective-permute-start.3 = (bf16[64,2048]{1,0:T(8,128)(2,1)S(1)}, bf16[64,2048]{1,0:T(8,128)(2,1)S(1)}, u32[]{:S(2)}, u32[]{:S(2)}) collective-permute-start(bf16[64,2048]{1,0:T(8,128)(2,1)S(1)} %get-tuple-element.14), channel_id=1, source_target_pairs={{0,4},{4,0},{8,12},{12,8},{16,20},{20,16},{24,28},{28,24},{1,5},{5... | collective-permute-start | bytes 786440 | tf_op jit(solution)/shard_map/ppermute | solution.py:26
  55.3 14.5 %collective-permute-start.13 = (bf16[64,2048]{1,0:T(8,128)(2,1)S(1)}, bf16[64,2048]{1,0:T(8,128)(2,1)S(1)}, u32[]{:S(2)}, u32[]{:S(2)}) collective-permute-start(bf16[64,2048]{1,0:T(8,128)(2,1)S(1)} %add_convert_fusion.1), channel_id=1, source_target_pairs={{0,16},{4,20},{8,24},{12,28},{16,0},{20,4},{24,8},{28,12},{1,17},{... | collective-permute-start | bytes 786440 | tf_op jit(solution)/shard_map/ppermute | solution.py:31

commit v2 on v1

--- a/solution.py
+++ b/solution.py
@@ -1,5 +1,3 @@
-import functools
-
 import jax
 import jax.numpy as jnp
 from jax import lax
@@ -21,14 +19,32 @@
     return lax.ppermute(block, axis, route)
 
 
-def from_member(block, apart):
-    count = lax.axis_size("ep")
-    return lax.ppermute(block, "ep", [(i, i ^ apart) for i in range(count)])
-
-
-def from_group(block, steps):
-    count = lax.axis_size("ep")
-    return lax.ppermute(block, "ep", [(i, (i - steps * GROUP) % count) for i in range(count)])
+def exchange(block, *apart):
+    replicas, count = lax.axis_size("dp"), lax.axis_size("ep")
+    route = []
+    for d in range(replicas):
+        bits = apart[d % len(apart)]
+        route += [(i * replicas + d, (i ^ bits) * replicas + d) for i in range(count)]
+    return lax.ppermute(block, ("ep", "dp"), route)
+
+
+def after(value, *others):
+    return lax.optimization_barrier((value, *others))[0]
+
+
+def touch_kernel(w_in, w_out, out):
+    out[...] = w_in[0, 0, :8, :128] + w_out[0, :8, :128]
+
+
+def touch(w_in, w_out):
+    return pl.pallas_call(
+        touch_kernel,
+        out_shape=jax.ShapeDtypeStruct((8, 128), jnp.bfloat16),
+        in_specs=[pl.BlockSpec(memory_space=pltpu.VMEM)] * 2,
+        out_specs=pl.BlockSpec(memory_space=pltpu.VMEM),
+        compiler_params=pltpu.CompilerParams(has_side_effects=True),
+        name="touch",
+    )(w_in, w_out)
 
 
 def share_kernel(*refs):
@@ -65,28 +81,43 @@
     )(*blocks, w_in, w_out)
 
 
+def summed(*shares):
+    total = shares[0].astype(jnp.float32)
+    for s in shares[1:]:
+        total = total + s.astype(jnp.float32)
+    return total.astype(jnp.bfloat16)
+
+
 def everywhere(tokens, gates, expert_ids, slot_expert, w_in, w_out):
-    experts = lax.axis_size("ep") // GROUP
+    first, second, across, group = (1, 2), (2, 1), (3, 3), (4, 4)
     my_group = lax.axis_index("ep") // GROUP
-    visitors = [from_group(tokens, s) for s in range(1, experts)]
-    held = [[tokens] + [from_member(tokens, m) for m in range(1, GROUP)]]
-    for rows in visitors:
-        held.append([rows] + [from_member(rows, m) for m in range(1, GROUP)])
-    sums = []
-    for blocks in held:
-        shares = share(blocks, w_in, w_out)
-        total = shares[0].astype(jnp.float32)
-        for m in range(1, GROUP):
-            total = total + from_member(shares[m], m).astype(jnp.float32)
-        sums.append(total.astype(jnp.bfloat16))
-    mixed = jnp.zeros(tokens.shape, jnp.float32)
-    for s in range(experts):
-        rows = sums[0] if s == 0 else from_group(sums[s], experts - s)
-        source = (my_group + (experts - s if s else 0)) % experts
-        named = lax.dynamic_index_in_dim(slot_expert, source, 0, keepdims=False)
-        weight = jnp.sum(jnp.where(expert_ids == named, gates, 0.0), axis=1, keepdims=True)
-        mixed = mixed + weight * rows.astype(jnp.float32)
-    return mixed.astype(jnp.bfloat16)
+    weights = []
+    for s in range(2):
+        named = lax.dynamic_index_in_dim(slot_expert, (my_group + s) % 2, 0, keepdims=False)
+        weights.append(jnp.sum(jnp.where(expert_ids == named, gates, 0.0), axis=1, keepdims=True))
+    theirs = exchange(tokens, *group)
+    ours_a = exchange(tokens, *first)
+    ours_b = exchange(tokens, *second)
+    ours_d = exchange(ours_a, *second)
+    theirs = after(theirs, touch(w_in, w_out), ours_a, ours_b, ours_d)
+    theirs_a = exchange(theirs, *first)
+    theirs_b = exchange(theirs, *second)
+    theirs_d = exchange(theirs, *across)
+    away = share([theirs, theirs_a, theirs_b, theirs_d], w_in, w_out)
+    away_d = exchange(away[3], *across)
+    away_a = exchange(away[1], *first)
+    away_b = exchange(away[2], *second)
+    home = share([after(tokens, away[0]), ours_a, ours_b, ours_d], w_in, w_out)
+    away_sum = summed(away[0], away_d, away_a, away_b)
+    other = exchange(away_sum, *group)
+    home = [after(h, away_d) for h in home]
+    home_d = exchange(home[3], *first)
+    home_a = exchange(home[1], *first)
+    home_b = exchange(summed(home[2], home_d), *second)
+    own = summed(home[0], home_a, home_b)
+    return (
+        weights[0] * own.astype(jnp.float32) + weights[1] * other.astype(jnp.float32)
+    ).astype(jnp.bfloat16)
 
 
 def routed(tokens, gates, expert_ids, slot_expert, w_in, w_out):
@@ -179,7 +210,7 @@
 
 
 def local(tokens, gates, expert_ids, slot_expert, w_in, w_out):
-    plan = everywhere if expert_ids.shape[1] == slot_expert.shape[0] else routed
+    plan = everywhere if expert_ids.shape[1] == slot_expert.shape[0] == 2 else routed
     return plan(tokens, gates, expert_ids, slot_expert, w_in, w_out)
 
 

time: 71.1 us -> 63 us (0.89)
  waiting for transfers between devices: 42.3 us -> 31.6 us
  Pallas kernels: 2.75 us -> 5.55 us
  local copies, waits for them, and re-layouts: 3.15 us -> 0.69 us
  starting transfers between devices: 20.1 us -> 22.4 us
    ppermute x14, waiting for transfers between devices: 42.3 us -> 31.6 us  [exchange(): return lax.ppermute(block, ('ep', 'dp'), route)]
    unnamed x16 -> x12, local copies, waits for them, and re-layouts: 2.56 us -> 0.02 us
    ppermute x14, starting transfers between devices: 20.1 us -> 22.4 us  [exchange(): return lax.ppermute(block, ('ep', 'dp'), route)]
    pallas_call x0 -> x1, Pallas kernels: none -> 2.19 us  [touch(): pl.pallas_call(touch_kernel, out_shape=jax.ShapeDtypeStruct((8, 128), jnp...]
  transfers between devices with their start and end apart: 14 -> 14, of which waited for: 8 -> 9; matrix products, arithmetic and copies ran while one was open for 3% -> 4% of each run, Pallas kernels for 4% -> 7%
where the time goes in v2:
time: 63 us; the launch traced here: 62.8 us
  waiting for transfers between devices  31.6 us (50%)
  starting transfers between devices  22.4 us (36%)
  Pallas kernels  5.55 us (9%)
  other arithmetic  2.47 us (4%)
  local copies, waits for them, and re-layouts  0.69 us (1%)
    ppermute x14, waiting for transfers between devices, exchange(): return lax.ppermute(block, ('ep', 'dp'), route)  31.6 us
    ppermute x14, starting transfers between devices, exchange(): return lax.ppermute(block, ('ep', 'dp'), route)  22.4 us
    pallas_call x2, Pallas kernels, share(): pl.pallas_call(share_kernel, out_shape=[jax.ShapeDtypeStruct((rows, width...  3.36 us
    pallas_call x1, Pallas kernels, touch(): pl.pallas_call(touch_kernel, out_shape=jax.ShapeDtypeStruct((8, 128), jnp...  2.19 us
    reduce_sum x1, other arithmetic, everywhere(): jnp.sum(jnp.where(expert_ids == named, gates, 0.0), axis=1, keepdims=True)  1.39 us
  transfers between devices with their start and end apart: 14, of which 9 were waited for; matrix products, arithmetic and copies ran while one was open for 4% of the time, Pallas kernels for 7%

profile of v2, /device:TPU:0, one launch (start us, length us, event | category | flops | bytes accessed | tf_op | source)
XLA Modules:
  0.0 62.8 jit_solution(4865765713427999629)
XLA Ops:
  0.0 0.0 copy-start
  0.0 0.0 copy-start.1
  0.0 2.9 %collective-permute-start.1 = (bf16[64,2048]{1,0:T(8,128)(2,1)}, bf16[64,2048]{1,0:T(8,128)(2,1)S(1)}, u32[]{:S(2)}, u32[]{:S(2)}) collective-permute-start(bf16[64,2048]{1,0:T(8,128)(2,1)} %refs_0_), channel_id=1, source_target_pairs={{0,4},{4,0},{8,12},{12,8},{16,20},{20,16},{24,28},{28,24},{1,9},{5... | collective-permute-start | bytes 786440 | tf_op jit(solution)/shard_map/ppermute | solution.py:28
  2.9 2.6 %collective-permute-start = (bf16[64,2048]{1,0:T(8,128)(2,1)}, bf16[64,2048]{1,0:T(8,128)(2,1)S(1)}, u32[]{:S(2)}, u32[]{:S(2)}) collective-permute-start(bf16[64,2048]{1,0:T(8,128)(2,1)} %refs_0_), channel_id=1, source_target_pairs={{0,16},{4,20},{8,24},{12,28},{16,0},{20,4},{24,8},{28,12},{1,17},{... | collective-permute-start | bytes 786440 | tf_op jit(solution)/shard_map/ppermute | solution.py:28
  5.5 1.6 %collective-permute-start.2 = (bf16[64,2048]{1,0:T(8,128)(2,1)}, bf16[64,2048]{1,0:T(8,128)(2,1)S(1)}, u32[]{:S(2)}, u32[]{:S(2)}) collective-permute-start(bf16[64,2048]{1,0:T(8,128)(2,1)} %refs_0_), channel_id=1, source_target_pairs={{0,8},{4,12},{8,0},{12,4},{16,24},{20,28},{24,16},{28,20},{1,5},{5... | collective-permute-start | bytes 786440 | tf_op jit(solution)/shard_map/ppermute | solution.py:28
  7.1 0.4 collective-permute-done.1.refs_1_
  7.5 3.5 %collective-permute-start.3 = (bf16[64,2048]{1,0:T(8,128)(2,1)S(1)}, bf16[64,2048]{1,0:T(8,128)(2,1)S(1)}, u32[]{:S(2)}, u32[]{:S(2)}) collective-permute-start(bf16[64,2048]{1,0:T(8,128)(2,1)S(1)} %collective-permute-done.1.refs_1_), channel_id=1, source_target_pairs={{0,8},{4,12},{8,0},{12,4},{16,24},{20,28},{24,16},{28,20},{1,5},{5... | collective-permute-start | bytes 786440 | tf_op jit(solution)/shard_map/ppermute | solution.py:28
  11.0 2.2 %touch.1 = bf16[8,128]{1,0:T(8,128)(2,1)} custom-call(bf16[1,2,192,2048]{3,2,1,0:T(8,128)(2,1)} %refs_4_.3, bf16[1,192,2048]{2,1,0:T(8,128)(2,1)} %refs_5_.3), custom_call_target="tpu_custom_call" | custom-call | tf_op jit(solution)/shard_map/touch/pallas_call | solution.py:40
  13.2 0.0 copy-start.2
  13.2 4.5 %collective-permute-done.refs_0_ = bf16[64,2048]{1,0:T(8,128)(2,1)S(1)} collective-permute-done((bf16[64,2048]{1,0:T(8,128)(2,1)}, bf16[64,2048]{1,0:T(8,128)(2,1)S(1)}, u32[]{:S(2)}, u32[]{:S(2)}) %collective-permute-start) | collective-permute-done | bytes 262176 | tf_op jit(solution)/shard_map/ppermute | solution.py:28
  17.7 0.0 collective-permute-done.2.refs_2_
  17.7 0.6 collective-permute-done.3.refs_3_
  18.3 1.5 %collective-permute-start.4 = (bf16[64,2048]{1,0:T(8,128)(2,1)S(1)}, bf16[64,2048]{1,0:T(8,128)(2,1)S(1)}, u32[]{:S(2)}, u32[]{:S(2)}) collective-permute-start(bf16[64,2048]{1,0:T(8,128)(2,1)S(1)} %collective-permute-done.refs_0_), channel_id=1, source_target_pairs={{0,4},{4,0},{8,12},{12,8},{16,20},{20,16},{24,28},{28,24},{1,9},{5... | collective-permute-start | bytes 786440 | tf_op jit(solution)/shard_map/ppermute | solution.py:28
  19.8 1.4 %collective-permute-start.5 = (bf16[64,2048]{1,0:T(8,128)(2,1)S(1)}, bf16[64,2048]{1,0:T(8,128)(2,1)S(1)}, u32[]{:S(2)}, u32[]{:S(2)}) collective-permute-start(bf16[64,2048]{1,0:T(8,128)(2,1)S(1)} %collective-permute-done.refs_0_), channel_id=1, source_target_pairs={{0,8},{4,12},{8,0},{12,4},{16,24},{20,28},{24,16},{28,20},{1,5},{5... | collective-permute-start | bytes 786440 | tf_op jit(solution)/shard_map/ppermute | solution.py:28
  21.2 0.6 collective-permute-start.6
  21.8 8.8 %collective-permute-done.4.refs_1_ = bf16[64,2048]{1,0:T(8,128)(2,1)S(1)} collective-permute-done((bf16[64,2048]{1,0:T(8,128)(2,1)S(1)}, bf16[64,2048]{1,0:T(8,128)(2,1)S(1)}, u32[]{:S(2)}, u32[]{:S(2)}) %collective-permute-start.4) | collective-permute-done | bytes 262176 | tf_op jit(solution)/shard_map/ppermute | solution.py:28
  30.6 0.0 collective-permute-done.5.refs_2_
  30.6 1.8 %collective-permute-done.6.refs_3_ = bf16[64,2048]{1,0:T(8,128)(2,1)S(1)} collective-permute-done((bf16[64,2048]{1,0:T(8,128)(2,1)S(1)}, bf16[64,2048]{1,0:T(8,128)(2,1)S(1)}, u32[]{:S(2)}, u32[]{:S(2)}) %collective-permute-start.6) | collective-permute-done | bytes 262176 | tf_op jit(solution)/shard_map/ppermute | solution.py:28
  32.5 0.0 copy-done
  32.5 0.0 copy-done.1
  32.5 1.4 %share.2 = (bf16[64,2048]{1,0:T(8,128)(2,1)S(1)}, bf16[64,2048]{1,0:T(8,128)(2,1)S(1)}, bf16[64,2048]{1,0:T(8,128)(2,1)S(1)}, bf16[64,2048]{1,0:T(8,128)(2,1)S(1)}) custom-call(bf16[64,2048]{1,0:T(8,128)(2,1)S(1)} %collective-permute-done.refs_0_, bf16[64,2048]{1,0:T(8,128)(2,1)S(1)} %collective-permute-done.4.refs_1_, ...), custom_call_target="tpu_custom_call" | custom-call | flops 603979776 | bytes 4456448 | tf_op jit(solution)/shard_map/share/pallas_call | solution.py:69
  33.8 1.8 %collective-permute-start.7 = (bf16[64,2048]{1,0:T(8,128)(2,1)S(1)}, bf16[64,2048]{1,0:T(8,128)(2,1)S(1)}, u32[]{:S(2)}, u32[]{:S(2)}) collective-permute-start(bf16[64,2048]{1,0:T(8,128)(2,1)S(1)} %get-tuple-element.23), channel_id=1, source_target_pairs={{0,12},{4,8},{8,4},{12,0},{16,28},{20,24},{24,20},{28,16},{1,13},{... | collective-permute-start | bytes 786440 | tf_op jit(solution)/shard_map/ppermute | solution.py:28
  35.7 0.4 collective-permute-start.12
  36.0 1.4 %collective-permute-start.11 = (bf16[64,2048]{1,0:T(8,128)(2,1)S(1)}, bf16[64,2048]{1,0:T(8,128)(2,1)S(1)}, u32[]{:S(2)}, u32[]{:S(2)}) collective-permute-start(bf16[64,2048]{1,0:T(8,128)(2,1)S(1)} %get-tuple-element.31), channel_id=1, source_target_pairs={{0,4},{4,0},{8,12},{12,8},{16,20},{20,16},{24,28},{28,24},{1,9},{5... | collective-permute-start | bytes 786440 | tf_op jit(solution)/shard_map/ppermute | solution.py:28
  37.4 0.0 copy-done.2
  37.4 2.0 %share.3 = (bf16[64,2048]{1,0:T(8,128)(2,1)S(1)}, bf16[64,2048]{1,0:T(8,128)(2,1)}, bf16[64,2048]{1,0:T(8,128)(2,1)S(1)}, bf16[64,2048]{1,0:T(8,128)(2,1)S(1)}) custom-call(bf16[64,2048]{1,0:T(8,128)(2,1)S(1)} %copy-done.2, bf16[64,2048]{1,0:T(8,128)(2,1)S(1)} %collective-permute-done.1.refs_1_, bf16[64,2048]{1,0:T(8,128)(2,1)S(1)} %collective-permute-done.2.refs_2_, ...), custom_call_target="tpu_custom_call" | custom-call | flops 603979776 | bytes 4456448 | tf_op jit(solution)/shard_map/share/pallas_call | solution.py:69
  39.4 0.0 copy-start.3
  39.4 0.0 copy-start.4
  39.4 0.0 copy-start.5
  39.4 4.7 %collective-permute-done.7 = bf16[64,2048]{1,0:T(8,128)(2,1)S(1)} collective-permute-done((bf16[64,2048]{1,0:T(8,128)(2,1)S(1)}, bf16[64,2048]{1,0:T(8,128)(2,1)S(1)}, u32[]{:S(2)}, u32[]{:S(2)}) %collective-permute-start.7) | collective-permute-done | bytes 262176 | tf_op jit(solution)/shard_map/ppermute | solution.py:28
  44.0 0.5 collective-permute-start.9
  44.6 3.7 %collective-permute-done.12 = bf16[64,2048]{1,0:T(8,128)(2,1)S(1)} collective-permute-done((bf16[64,2048]{1,0:T(8,128)(2,1)S(1)}, bf16[64,2048]{1,0:T(8,128)(2,1)S(1)}, u32[]{:S(2)}, u32[]{:S(2)}) %collective-permute-start.12) | collective-permute-done | bytes 262176 | tf_op jit(solution)/shard_map/ppermute | solution.py:28
  48.3 0.0 collective-permute-done.11
  48.3 0.1 add_convert_fusion.1
  48.4 0.1 collective-permute-start.13
  48.5 4.0 %collective-permute-start.8 = (bf16[64,2048]{1,0:T(8,128)(2,1)}, bf16[64,2048]{1,0:T(8,128)(2,1)S(1)}, u32[]{:S(2)}, u32[]{:S(2)}) collective-permute-start(bf16[64,2048]{1,0:T(8,128)(2,1)} %get-tuple-element.26), channel_id=1, source_target_pairs={{0,4},{4,0},{8,12},{12,8},{16,20},{20,16},{24,28},{28,24},{1,9},{5... | collective-permute-start | bytes 786440 | tf_op jit(solution)/shard_map/ppermute | solution.py:28
  52.5 0.0 collective-permute-done.9
  52.5 0.1 add_convert_fusion.3
  52.6 0.1 collective-permute-start.10
  52.7 0.0 copy-done.3
  52.8 0.7 %fusion.2 = (s32[1]{0:T(128)}, s32[1]{0:T(128)}) fusion(s32[2]{0:T(128)S(1)} %copy-done.3, s32[]{:T(128)S(6)} %select_n.34, s32[]{:T(128)S(6)} %select_n.31), kind=kLoop, calls=%fused_computation.8 | loop fusion | bytes 24 | tf_op jit(solution)/shard_map/jit(dynamic_index_in_dim)/dynamic_slice | solution.py:96
  53.4 0.0 copy-done.4
  53.4 0.0 copy-done.5
  53.4 1.4 %fusion = (f32[64]{0:T(128)S(1)}, f32[64]{0:T(128)S(1)}) fusion(f32[64,2]{0,1:T(2,128)S(1)} %copy-done.4, s32[64,2]{0,1:T(2,128)S(1)} %copy-done.5, s32[]{:T(128)} %bitcast, s32[]{:T(128)} %bitcast.1), kind=kLoop, calls=%fused_computation.6 | loop fusion | flops 640 | bytes 1544 | tf_op jit(solution)/shard_map/reduce_sum | solution.py:97
  54.8 6.4 %collective-permute-done.13 = bf16[64,2048]{1,0:T(8,128)(2,1)S(1)} collective-permute-done((bf16[64,2048]{1,0:T(8,128)(2,1)S(1)}, bf16[64,2048]{1,0:T(8,128)(2,1)S(1)}, u32[]{:S(2)}, u32[]{:S(2)}) %collective-permute-start.13) | collective-permute-done | bytes 262176 | tf_op jit(solution)/shard_map/ppermute | solution.py:28
  61.3 0.0 collective-permute-done.8
  61.3 0.7 %collective-permute-done.10 = bf16[64,2048]{1,0:T(8,128)(2,1)S(1)} collective-permute-done((bf16[64,2048]{1,0:T(8,128)(2,1)S(1)}, bf16[64,2048]{1,0:T(8,128)(2,1)S(1)}, u32[]{:S(2)}, u32[]{:S(2)}) %collective-permute-start.10) | collective-permute-done | bytes 262176 | tf_op jit(solution)/shard_map/ppermute | solution.py:28
  61.9 0.9 %add_convert_fusion = bf16[64,2048]{1,0:T(8,128)(2,1)} fusion(bf16[64,2048]{1,0:T(8,128)(2,1)S(1)} %collective-permute-done.13, bf16[64,2048]{1,0:T(8,128)(2,1)S(1)} %collective-permute-done.10, bf16[64,2048]{1,0:T(8,128)(2,1)S(1)} %collective-permute-done.8, bf16[64,2048]{1,0:T(8,128)(2,1)S(1)} %get-tuple-element.24, f32[64]{0:T(128)S(1)} %get-tuple-element.34, ...), kind=kLoop, calls=%fused_computation | loop fusion | flops 1572864 | bytes 1311232 | tf_op jit(solution)/shard_map/convert_element_type | solution.py:120
Async XLA Ops:
  0.0 32.5 %copy-start = (bf16[1,2,192,2048]{3,2,1,0:T(8,128)(2,1)S(1)}, bf16[1,2,192,2048]{3,2,1,0:T(8,128)(2,1)}, u32[]{:S(2)}) copy-start(bf16[1,2,192,2048]{3,2,1,0:T(8,128)(2,1)} %refs_4_.3) | copy-start | bytes 4718596
  0.0 32.5 %copy-start.1 = (bf16[1,192,2048]{2,1,0:T(8,128)(2,1)S(1)}, bf16[1,192,2048]{2,1,0:T(8,128)(2,1)}, u32[]{:S(2)}) copy-start(bf16[1,192,2048]{2,1,0:T(8,128)(2,1)} %refs_5_.3) | copy-start | bytes 2359300
  0.0 7.5 %collective-permute-start.1 = (bf16[64,2048]{1,0:T(8,128)(2,1)}, bf16[64,2048]{1,0:T(8,128)(2,1)S(1)}, u32[]{:S(2)}, u32[]{:S(2)}) collective-permute-start(bf16[64,2048]{1,0:T(8,128)(2,1)} %refs_0_), channel_id=1, source_target_pairs={{0,4},{4,0},{8,12},{12,8},{16,20},{20,16},{24,28},{28,24},{1,9},{5... | collective-permute-start | bytes 786440 | tf_op jit(solution)/shard_map/ppermute | solution.py:28
  2.9 14.7 %collective-permute-start = (bf16[64,2048]{1,0:T(8,128)(2,1)}, bf16[64,2048]{1,0:T(8,128)(2,1)S(1)}, u32[]{:S(2)}, u32[]{:S(2)}) collective-permute-start(bf16[64,2048]{1,0:T(8,128)(2,1)} %refs_0_), channel_id=1, source_target_pairs={{0,16},{4,20},{8,24},{12,28},{16,0},{20,4},{24,8},{28,12},{1,17},{... | collective-permute-start | bytes 786440 | tf_op jit(solution)/shard_map/ppermute | solution.py:28
  5.5 12.2 %collective-permute-start.2 = (bf16[64,2048]{1,0:T(8,128)(2,1)}, bf16[64,2048]{1,0:T(8,128)(2,1)S(1)}, u32[]{:S(2)}, u32[]{:S(2)}) collective-permute-start(bf16[64,2048]{1,0:T(8,128)(2,1)} %refs_0_), channel_id=1, source_target_pairs={{0,8},{4,12},{8,0},{12,4},{16,24},{20,28},{24,16},{28,20},{1,5},{5... | collective-permute-start | bytes 786440 | tf_op jit(solution)/shard_map/ppermute | solution.py:28
  7.5 10.8 %collective-permute-start.3 = (bf16[64,2048]{1,0:T(8,128)(2,1)S(1)}, bf16[64,2048]{1,0:T(8,128)(2,1)S(1)}, u32[]{:S(2)}, u32[]{:S(2)}) collective-permute-start(bf16[64,2048]{1,0:T(8,128)(2,1)S(1)} %collective-permute-done.1.refs_1_), channel_id=1, source_target_pairs={{0,8},{4,12},{8,0},{12,4},{16,24},{20,28},{24,16},{28,20},{1,5},{5... | collective-permute-start | bytes 786440 | tf_op jit(solution)/shard_map/ppermute | solution.py:28
  13.2 24.2 %copy-start.2 = (bf16[64,2048]{1,0:T(8,128)(2,1)S(1)}, bf16[64,2048]{1,0:T(8,128)(2,1)}, u32[]{:S(2)}) copy-start(bf16[64,2048]{1,0:T(8,128)(2,1)} %refs_0_) | copy-start | bytes 786436
  18.3 12.3 %collective-permute-start.4 = (bf16[64,2048]{1,0:T(8,128)(2,1)S(1)}, bf16[64,2048]{1,0:T(8,128)(2,1)S(1)}, u32[]{:S(2)}, u32[]{:S(2)}) collective-permute-start(bf16[64,2048]{1,0:T(8,128)(2,1)S(1)} %collective-permute-done.refs_0_), channel_id=1, source_target_pairs={{0,4},{4,0},{8,12},{12,8},{16,20},{20,16},{24,28},{28,24},{1,9},{5... | collective-permute-start | bytes 786440 | tf_op jit(solution)/shard_map/ppermute | solution.py:28
  19.8 10.8 %collective-permute-start.5 = (bf16[64,2048]{1,0:T(8,128)(2,1)S(1)}, bf16[64,2048]{1,0:T(8,128)(2,1)S(1)}, u32[]{:S(2)}, u32[]{:S(2)}) collective-permute-start(bf16[64,2048]{1,0:T(8,128)(2,1)S(1)} %collective-permute-done.refs_0_), channel_id=1, source_target_pairs={{0,8},{4,12},{8,0},{12,4},{16,24},{20,28},{24,16},{28,20},{1,5},{5... | collective-permute-start | bytes 786440 | tf_op jit(solution)/shard_map/ppermute | solution.py:28
  21.2 11.2 %collective-permute-start.6 = (bf16[64,2048]{1,0:T(8,128)(2,1)S(1)}, bf16[64,2048]{1,0:T(8,128)(2,1)S(1)}, u32[]{:S(2)}, u32[]{:S(2)}) collective-permute-start(bf16[64,2048]{1,0:T(8,128)(2,1)S(1)} %collective-permute-done.refs_0_), channel_id=1, source_target_pairs={{0,12},{4,8},{8,4},{12,0},{16,28},{20,24},{24,20},{28,16},{1,13},{... | collective-permute-start | bytes 786440 | tf_op jit(solution)/shard_map/ppermute | solution.py:28
  33.8 10.2 %collective-permute-start.7 = (bf16[64,2048]{1,0:T(8,128)(2,1)S(1)}, bf16[64,2048]{1,0:T(8,128)(2,1)S(1)}, u32[]{:S(2)}, u32[]{:S(2)}) collective-permute-start(bf16[64,2048]{1,0:T(8,128)(2,1)S(1)} %get-tuple-element.23), channel_id=1, source_target_pairs={{0,12},{4,8},{8,4},{12,0},{16,28},{20,24},{24,20},{28,16},{1,13},{... | collective-permute-start | bytes 786440 | tf_op jit(solution)/shard_map/ppermute | solution.py:28
  35.7 12.6 %collective-permute-start.12 = (bf16[64,2048]{1,0:T(8,128)(2,1)S(1)}, bf16[64,2048]{1,0:T(8,128)(2,1)S(1)}, u32[]{:S(2)}, u32[]{:S(2)}) collective-permute-start(bf16[64,2048]{1,0:T(8,128)(2,1)S(1)} %get-tuple-element.32), channel_id=1, source_target_pairs={{0,8},{4,12},{8,0},{12,4},{16,24},{20,28},{24,16},{28,20},{1,5},{5... | collective-permute-start | bytes 786440 | tf_op jit(solution)/shard_map/ppermute | solution.py:28
  36.0 12.3 %collective-permute-start.11 = (bf16[64,2048]{1,0:T(8,128)(2,1)S(1)}, bf16[64,2048]{1,0:T(8,128)(2,1)S(1)}, u32[]{:S(2)}, u32[]{:S(2)}) collective-permute-start(bf16[64,2048]{1,0:T(8,128)(2,1)S(1)} %get-tuple-element.31), channel_id=1, source_target_pairs={{0,4},{4,0},{8,12},{12,8},{16,20},{20,16},{24,28},{28,24},{1,9},{5... | collective-permute-start | bytes 786440 | tf_op jit(solution)/shard_map/ppermute | solution.py:28
  39.4 13.4 %copy-start.3 = (s32[2]{0:T(128)S(1)}, s32[2]{0:T(128)}, u32[]{:S(2)}) copy-start(s32[2]{0:T(128)} %param.9) | copy-start | bytes 28
  39.4 14.0 %copy-start.4 = (f32[64,2]{0,1:T(2,128)S(1)}, f32[64,2]{0,1:T(2,128)}, u32[]{:S(2)}) copy-start(f32[64,2]{0,1:T(2,128)} %param.7) | copy-start | bytes 1540
  39.4 14.0 %copy-start.5 = (s32[64,2]{0,1:T(2,128)S(1)}, s32[64,2]{0,1:T(2,128)}, u32[]{:S(2)}) copy-start(s32[64,2]{0,1:T(2,128)} %param.8) | copy-start | bytes 1540
  44.0 8.5 %collective-permute-start.9 = (bf16[64,2048]{1,0:T(8,128)(2,1)S(1)}, bf16[64,2048]{1,0:T(8,128)(2,1)S(1)}, u32[]{:S(2)}, u32[]{:S(2)}) collective-permute-start(bf16[64,2048]{1,0:T(8,128)(2,1)S(1)} %get-tuple-element.30), channel_id=1, source_target_pairs={{0,4},{4,0},{8,12},{12,8},{16,20},{20,16},{24,28},{28,24},{1,9},{5... | collective-permute-start | bytes 786440 | tf_op jit(solution)/shard_map/ppermute | solution.py:28
  48.4 12.8 %collective-permute-start.13 = (bf16[64,2048]{1,0:T(8,128)(2,1)S(1)}, bf16[64,2048]{1,0:T(8,128)(2,1)S(1)}, u32[]{:S(2)}, u32[]{:S(2)}) collective-permute-start(bf16[64,2048]{1,0:T(8,128)(2,1)S(1)} %add_convert_fusion.1), channel_id=1, source_target_pairs={{0,16},{4,20},{8,24},{12,28},{16,0},{20,4},{24,8},{28,12},{1,17},{... | collective-permute-start | bytes 786440 | tf_op jit(solution)/shard_map/ppermute | solution.py:28
  48.5 12.8 %collective-permute-start.8 = (bf16[64,2048]{1,0:T(8,128)(2,1)}, bf16[64,2048]{1,0:T(8,128)(2,1)S(1)}, u32[]{:S(2)}, u32[]{:S(2)}) collective-permute-start(bf16[64,2048]{1,0:T(8,128)(2,1)} %get-tuple-element.26), channel_id=1, source_target_pairs={{0,4},{4,0},{8,12},{12,8},{16,20},{20,16},{24,28},{28,24},{1,9},{5... | collective-permute-start | bytes 786440 | tf_op jit(solution)/shard_map/ppermute | solution.py:28
  52.6 9.3 %collective-permute-start.10 = (bf16[64,2048]{1,0:T(8,128)(2,1)S(1)}, bf16[64,2048]{1,0:T(8,128)(2,1)S(1)}, u32[]{:S(2)}, u32[]{:S(2)}) collective-permute-start(bf16[64,2048]{1,0:T(8,128)(2,1)S(1)} %add_convert_fusion.3), channel_id=1, source_target_pairs={{0,8},{4,12},{8,0},{12,4},{16,24},{20,28},{24,16},{28,20},{1,5},{5... | collective-permute-start | bytes 786440 | tf_op jit(solution)/shard_map/ppermute | solution.py:28

commit v3 on v2

--- a/solution.py
+++ b/solution.py
@@ -99,21 +99,23 @@
     ours_a = exchange(tokens, *first)
     ours_b = exchange(tokens, *second)
     ours_d = exchange(ours_a, *second)
-    theirs = after(theirs, touch(w_in, w_out), ours_a, ours_b, ours_d)
+    theirs = after(theirs, touch(w_in, w_out), ours_b)
+    theirs_d = exchange(theirs, *across)
+    theirs = after(theirs, ours_d)
     theirs_a = exchange(theirs, *first)
     theirs_b = exchange(theirs, *second)
-    theirs_d = exchange(theirs, *across)
-    away = share([theirs, theirs_a, theirs_b, theirs_d], w_in, w_out)
-    away_d = exchange(away[3], *across)
-    away_a = exchange(away[1], *first)
-    away_b = exchange(away[2], *second)
-    home = share([after(tokens, away[0]), ours_a, ours_b, ours_d], w_in, w_out)
-    away_sum = summed(away[0], away_d, away_a, away_b)
-    other = exchange(away_sum, *group)
-    home = [after(h, away_d) for h in home]
+    (away_d,) = share([theirs_d], w_in, w_out)
+    away, away_a, away_b = share([theirs, theirs_a, theirs_b], w_in, w_out)
+    back_a = exchange(away_a, *first)
+    back_b = exchange(away_b, *second)
+    back_d = exchange(away_d, *across)
+    away_sum = summed(away, back_a, back_b, back_d)
+    home = share([after(tokens, back_d), ours_a, ours_b, ours_d], w_in, w_out)
+    home = [after(h, back_d) for h in home]
     home_d = exchange(home[3], *first)
     home_a = exchange(home[1], *first)
     home_b = exchange(summed(home[2], home_d), *second)
+    other = exchange(away_sum, *group)
     own = summed(home[0], home_a, home_b)
     return (
         weights[0] * own.astype(jnp.float32) + weights[1] * other.astype(jnp.float32)

time: 63 us -> 59.5 us (0.944)
  starting transfers between devices: 22.4 us -> 17.7 us
  waiting for transfers between devices: 31.6 us -> 32.3 us
    ppermute x14, starting transfers between devices: 22.4 us -> 17.7 us  [exchange(): return lax.ppermute(block, ('ep', 'dp'), route)]
    ppermute x14, waiting for transfers between devices: 31.6 us -> 32.3 us  [exchange(): return lax.ppermute(block, ('ep', 'dp'), route)]
    pallas_call x2 -> x3, Pallas kernels: 3.36 us -> 3.94 us  [share(): pl.pallas_call(share_kernel, out_shape=[jax.ShapeDtypeStruct((rows, width...]
  transfers between devices with their start and end apart: 14 -> 14, of which waited for: 9 -> 11; matrix products, arithmetic and copies ran while one was open for 4% -> 4% of each run, Pallas kernels for 7% -> 10%
where the time goes in v3:
time: 59.5 us; the launch traced here: 59.4 us
  waiting for transfers between devices  32.3 us (54%)
  starting transfers between devices  17.7 us (30%)
  Pallas kernels  6.13 us (10%)
  other arithmetic  2.47 us (4%)
  local copies, waits for them, and re-layouts  0.69 us (1%)
    ppermute x14, waiting for transfers between devices, exchange(): return lax.ppermute(block, ('ep', 'dp'), route)  32.3 us
    ppermute x14, starting transfers between devices, exchange(): return lax.ppermute(block, ('ep', 'dp'), route)  17.7 us
    pallas_call x3, Pallas kernels, share(): pl.pallas_call(share_kernel, out_shape=[jax.ShapeDtypeStruct((rows, width...  3.94 us
    pallas_call x1, Pallas kernels, touch(): pl.pallas_call(touch_kernel, out_shape=jax.ShapeDtypeStruct((8, 128), jnp...  2.19 us
    reduce_sum x1, other arithmetic, everywhere(): jnp.sum(jnp.where(expert_ids == named, gates, 0.0), axis=1, keepdims=True)  1.39 us
  transfers between devices with their start and end apart: 14, of which 11 were waited for; matrix products, arithmetic and copies ran while one was open for 4% of the time, Pallas kernels for 10%

profile of v3, /device:TPU:0, one launch (start us, length us, event | category | flops | bytes accessed | tf_op | source)
XLA Modules:
  0.0 59.4 jit_solution(3650560625587465371)
XLA Ops:
  0.0 0.0 copy-start
  0.0 0.0 copy-start.1
  0.0 2.9 %collective-permute-start.4 = (bf16[64,2048]{1,0:T(8,128)(2,1)}, bf16[64,2048]{1,0:T(8,128)(2,1)S(1)}, u32[]{:S(2)}, u32[]{:S(2)}) collective-permute-start(bf16[64,2048]{1,0:T(8,128)(2,1)} %refs_0_), channel_id=1, source_target_pairs={{0,4},{4,0},{8,12},{12,8},{16,20},{20,16},{24,28},{28,24},{1,9},{5... | collective-permute-start | bytes 786440 | tf_op jit(solution)/shard_map/ppermute | solution.py:28
  2.9 1.6 %collective-permute-start.1 = (bf16[64,2048]{1,0:T(8,128)(2,1)}, bf16[64,2048]{1,0:T(8,128)(2,1)S(1)}, u32[]{:S(2)}, u32[]{:S(2)}) collective-permute-start(bf16[64,2048]{1,0:T(8,128)(2,1)} %refs_0_), channel_id=1, source_target_pairs={{0,8},{4,12},{8,0},{12,4},{16,24},{20,28},{24,16},{28,20},{1,5},{5... | collective-permute-start | bytes 786440 | tf_op jit(solution)/shard_map/ppermute | solution.py:28
  4.5 2.6 %collective-permute-start = (bf16[64,2048]{1,0:T(8,128)(2,1)}, bf16[64,2048]{1,0:T(8,128)(2,1)S(1)}, u32[]{:S(2)}, u32[]{:S(2)}) collective-permute-start(bf16[64,2048]{1,0:T(8,128)(2,1)} %refs_0_), channel_id=1, source_target_pairs={{0,16},{4,20},{8,24},{12,28},{16,0},{20,4},{24,8},{28,12},{1,17},{... | collective-permute-start | bytes 786440 | tf_op jit(solution)/shard_map/ppermute | solution.py:28
  7.1 2.7 %collective-permute-done.4.refs_1_ = bf16[64,2048]{1,0:T(8,128)(2,1)S(1)} collective-permute-done((bf16[64,2048]{1,0:T(8,128)(2,1)}, bf16[64,2048]{1,0:T(8,128)(2,1)S(1)}, u32[]{:S(2)}, u32[]{:S(2)}) %collective-permute-start.4) | collective-permute-done | bytes 262176 | tf_op jit(solution)/shard_map/ppermute | solution.py:28
  9.8 1.6 %collective-permute-start.5 = (bf16[64,2048]{1,0:T(8,128)(2,1)S(1)}, bf16[64,2048]{1,0:T(8,128)(2,1)S(1)}, u32[]{:S(2)}, u32[]{:S(2)}) collective-permute-start(bf16[64,2048]{1,0:T(8,128)(2,1)S(1)} %collective-permute-done.4.refs_1_), channel_id=1, source_target_pairs={{0,8},{4,12},{8,0},{12,4},{16,24},{20,28},{24,16},{28,20},{1,5},{5... | collective-permute-start | bytes 786440 | tf_op jit(solution)/shard_map/ppermute | solution.py:28
  11.4 2.2 %touch.1 = bf16[8,128]{1,0:T(8,128)(2,1)} custom-call(bf16[1,2,192,2048]{3,2,1,0:T(8,128)(2,1)} %refs_3_.1, bf16[1,192,2048]{2,1,0:T(8,128)(2,1)} %refs_4_.3), custom_call_target="tpu_custom_call" | custom-call | tf_op jit(solution)/shard_map/touch/pallas_call | solution.py:40
  13.5 0.0 collective-permute-done.1.refs_2_
  13.6 5.2 %collective-permute-done.refs_0_ = bf16[64,2048]{1,0:T(8,128)(2,1)S(1)} collective-permute-done((bf16[64,2048]{1,0:T(8,128)(2,1)}, bf16[64,2048]{1,0:T(8,128)(2,1)S(1)}, u32[]{:S(2)}, u32[]{:S(2)}) %collective-permute-start) | collective-permute-done | bytes 262176 | tf_op jit(solution)/shard_map/ppermute | solution.py:28
  18.8 0.1 collective-permute-start.2
  18.9 0.0 collective-permute-done.5.refs_3_
  18.9 2.0 %collective-permute-start.10 = (bf16[64,2048]{1,0:T(8,128)(2,1)S(1)}, bf16[64,2048]{1,0:T(8,128)(2,1)S(1)}, u32[]{:S(2)}, u32[]{:S(2)}) collective-permute-start(bf16[64,2048]{1,0:T(8,128)(2,1)S(1)} %collective-permute-done.refs_0_), channel_id=1, source_target_pairs={{0,8},{4,12},{8,0},{12,4},{16,24},{20,28},{24,16},{28,20},{1,5},{5... | collective-permute-start | bytes 786440 | tf_op jit(solution)/shard_map/ppermute | solution.py:28
  20.9 1.4 %collective-permute-start.9 = (bf16[64,2048]{1,0:T(8,128)(2,1)S(1)}, bf16[64,2048]{1,0:T(8,128)(2,1)S(1)}, u32[]{:S(2)}, u32[]{:S(2)}) collective-permute-start(bf16[64,2048]{1,0:T(8,128)(2,1)S(1)} %collective-permute-done.refs_0_), channel_id=1, source_target_pairs={{0,4},{4,0},{8,12},{12,8},{16,20},{20,16},{24,28},{28,24},{1,9},{5... | collective-permute-start | bytes 786440 | tf_op jit(solution)/shard_map/ppermute | solution.py:28
  22.3 6.7 %collective-permute-done.2.refs_0_ = bf16[64,2048]{1,0:T(8,128)(2,1)S(1)} collective-permute-done((bf16[64,2048]{1,0:T(8,128)(2,1)S(1)}, bf16[64,2048]{1,0:T(8,128)(2,1)S(1)}, u32[]{:S(2)}, u32[]{:S(2)}) %collective-permute-start.2) | collective-permute-done | bytes 262176 | tf_op jit(solution)/shard_map/ppermute | solution.py:28
  29.0 0.0 copy-done
  29.0 0.0 copy-done.1
  29.0 0.9 %share.3 = bf16[64,2048]{1,0:T(8,128)(2,1)S(1)} custom-call(bf16[64,2048]{1,0:T(8,128)(2,1)S(1)} %collective-permute-done.2.refs_0_, bf16[1,2,192,2048]{3,2,1,0:T(8,128)(2,1)S(1)} %copy-done, bf16[1,192,2048]{2,1,0:T(8,128)(2,1)S(1)} %copy-done.1), custom_call_target="tpu_custom_call" | custom-call | flops 150994944 | bytes 2883584 | tf_op jit(solution)/shard_map/share/pallas_call | solution.py:69
  29.8 0.0 copy-start.2
  29.8 0.2 collective-permute-start.3
  30.1 3.4 %collective-permute-done.10.refs_2_ = bf16[64,2048]{1,0:T(8,128)(2,1)S(1)} collective-permute-done((bf16[64,2048]{1,0:T(8,128)(2,1)S(1)}, bf16[64,2048]{1,0:T(8,128)(2,1)S(1)}, u32[]{:S(2)}, u32[]{:S(2)}) %collective-permute-start.10) | collective-permute-done | bytes 262176 | tf_op jit(solution)/shard_map/ppermute | solution.py:28
  33.4 1.1 %collective-permute-done.9.refs_1_ = bf16[64,2048]{1,0:T(8,128)(2,1)S(1)} collective-permute-done((bf16[64,2048]{1,0:T(8,128)(2,1)S(1)}, bf16[64,2048]{1,0:T(8,128)(2,1)S(1)}, u32[]{:S(2)}, u32[]{:S(2)}) %collective-permute-start.9) | collective-permute-done | bytes 262176 | tf_op jit(solution)/shard_map/ppermute | solution.py:28
  34.5 1.1 %share.5 = (bf16[64,2048]{1,0:T(8,128)(2,1)S(1)}, bf16[64,2048]{1,0:T(8,128)(2,1)S(1)}, bf16[64,2048]{1,0:T(8,128)(2,1)S(1)}) custom-call(bf16[64,2048]{1,0:T(8,128)(2,1)S(1)} %collective-permute-done.refs_0_, bf16[64,2048]{1,0:T(8,128)(2,1)S(1)} %collective-permute-done.9.refs_1_, bf16[64,2048]{1,0:T(8,128)(2,1)S(1)} %collective-permute-done.10.refs_2_, ...), custom_call_target="tpu_custom_call" | custom-call | flops 452984832 | bytes 3932160 | tf_op jit(solution)/shard_map/share/pallas_call | solution.py:69
  35.6 0.7 %collective-permute-start.11 = (bf16[64,2048]{1,0:T(8,128)(2,1)S(1)}, bf16[64,2048]{1,0:T(8,128)(2,1)S(1)}, u32[]{:S(2)}, u32[]{:S(2)}) collective-permute-start(bf16[64,2048]{1,0:T(8,128)(2,1)S(1)} %get-tuple-element.31), channel_id=1, source_target_pairs={{0,4},{4,0},{8,12},{12,8},{16,20},{20,16},{24,28},{28,24},{1,9},{5... | collective-permute-start | bytes 786440 | tf_op jit(solution)/shard_map/ppermute | solution.py:28
  36.3 0.1 collective-permute-start.12
  36.4 2.8 %collective-permute-done.3 = bf16[64,2048]{1,0:T(8,128)(2,1)S(1)} collective-permute-done((bf16[64,2048]{1,0:T(8,128)(2,1)S(1)}, bf16[64,2048]{1,0:T(8,128)(2,1)S(1)}, u32[]{:S(2)}, u32[]{:S(2)}) %collective-permute-start.3) | collective-permute-done | bytes 262176 | tf_op jit(solution)/shard_map/ppermute | solution.py:28
  39.2 0.0 copy-done.2
  39.2 2.0 %share.4 = (bf16[64,2048]{1,0:T(8,128)(2,1)S(1)}, bf16[64,2048]{1,0:T(8,128)(2,1)}, bf16[64,2048]{1,0:T(8,128)(2,1)S(1)}, bf16[64,2048]{1,0:T(8,128)(2,1)S(1)}) custom-call(bf16[64,2048]{1,0:T(8,128)(2,1)S(1)} %copy-done.2, bf16[64,2048]{1,0:T(8,128)(2,1)S(1)} %collective-permute-done.4.refs_1_, bf16[64,2048]{1,0:T(8,128)(2,1)S(1)} %collective-permute-done.1.refs_2_, ...), custom_call_target="tpu_custom_call" | custom-call | flops 603979776 | bytes 4456448 | tf_op jit(solution)/shard_map/share/pallas_call | solution.py:69
  41.2 0.0 copy-start.3
  41.2 0.0 copy-start.4
  41.2 0.0 collective-permute-start.7
  41.2 2.0 %collective-permute-start.6 = (bf16[64,2048]{1,0:T(8,128)(2,1)}, bf16[64,2048]{1,0:T(8,128)(2,1)S(1)}, u32[]{:S(2)}, u32[]{:S(2)}) collective-permute-start(bf16[64,2048]{1,0:T(8,128)(2,1)} %get-tuple-element.24), channel_id=1, source_target_pairs={{0,4},{4,0},{8,12},{12,8},{16,20},{20,16},{24,28},{28,24},{1,9},{5... | collective-permute-start | bytes 786440 | tf_op jit(solution)/shard_map/ppermute | solution.py:28
  43.2 0.7 %collective-permute-done.11 = bf16[64,2048]{1,0:T(8,128)(2,1)S(1)} collective-permute-done((bf16[64,2048]{1,0:T(8,128)(2,1)S(1)}, bf16[64,2048]{1,0:T(8,128)(2,1)S(1)}, u32[]{:S(2)}, u32[]{:S(2)}) %collective-permute-start.11) | collective-permute-done | bytes 262176 | tf_op jit(solution)/shard_map/ppermute | solution.py:28
  44.0 1.6 %collective-permute-done.12 = bf16[64,2048]{1,0:T(8,128)(2,1)S(1)} collective-permute-done((bf16[64,2048]{1,0:T(8,128)(2,1)S(1)}, bf16[64,2048]{1,0:T(8,128)(2,1)S(1)}, u32[]{:S(2)}, u32[]{:S(2)}) %collective-permute-start.12) | collective-permute-done | bytes 262176 | tf_op jit(solution)/shard_map/ppermute | solution.py:28
  45.6 0.1 add_convert_fusion.1
  45.7 1.1 %collective-permute-start.13 = (bf16[64,2048]{1,0:T(8,128)(2,1)S(1)}, bf16[64,2048]{1,0:T(8,128)(2,1)S(1)}, u32[]{:S(2)}, u32[]{:S(2)}) collective-permute-start(bf16[64,2048]{1,0:T(8,128)(2,1)S(1)} %add_convert_fusion.1), channel_id=1, source_target_pairs={{0,16},{4,20},{8,24},{12,28},{16,0},{20,4},{24,8},{28,12},{1,17},{... | collective-permute-start | bytes 786440 | tf_op jit(solution)/shard_map/ppermute | solution.py:28
  46.8 0.7 %collective-permute-done.7 = bf16[64,2048]{1,0:T(8,128)(2,1)S(1)} collective-permute-done((bf16[64,2048]{1,0:T(8,128)(2,1)S(1)}, bf16[64,2048]{1,0:T(8,128)(2,1)S(1)}, u32[]{:S(2)}, u32[]{:S(2)}) %collective-permute-start.7) | collective-permute-done | bytes 262176 | tf_op jit(solution)/shard_map/ppermute | solution.py:28
  47.6 0.1 add_convert_fusion.3
  47.6 1.4 %collective-permute-start.8 = (bf16[64,2048]{1,0:T(8,128)(2,1)S(1)}, bf16[64,2048]{1,0:T(8,128)(2,1)S(1)}, u32[]{:S(2)}, u32[]{:S(2)}) collective-permute-start(bf16[64,2048]{1,0:T(8,128)(2,1)S(1)} %add_convert_fusion.3), channel_id=1, source_target_pairs={{0,8},{4,12},{8,0},{12,4},{16,24},{20,28},{24,16},{28,20},{1,5},{5... | collective-permute-start | bytes 786440 | tf_op jit(solution)/shard_map/ppermute | solution.py:28
  49.0 0.0 copy-done.3
  49.0 0.7 %fusion.2 = (s32[1]{0:T(128)}, s32[1]{0:T(128)}) fusion(s32[2]{0:T(128)S(1)} %copy-done.3, s32[]{:T(128)S(6)} %select_n.34, s32[]{:T(128)S(6)} %select_n.31), kind=kLoop, calls=%fused_computation.8 | loop fusion | bytes 24 | tf_op jit(solution)/shard_map/jit(dynamic_index_in_dim)/dynamic_slice | solution.py:96
  49.7 0.0 copy-done.4
  49.7 0.0 copy-done.5
  49.7 1.4 %fusion = (f32[64]{0:T(128)S(1)}, f32[64]{0:T(128)S(1)}) fusion(f32[64,2]{0,1:T(2,128)S(1)} %copy-done.4, s32[64,2]{0,1:T(2,128)S(1)} %copy-done.5, s32[]{:T(128)} %bitcast, s32[]{:T(128)} %bitcast.1), kind=kLoop, calls=%fused_computation.6 | loop fusion | flops 640 | bytes 1544 | tf_op jit(solution)/shard_map/reduce_sum | solution.py:97
  51.1 1.0 %collective-permute-done.6 = bf16[64,2048]{1,0:T(8,128)(2,1)S(1)} collective-permute-done((bf16[64,2048]{1,0:T(8,128)(2,1)}, bf16[64,2048]{1,0:T(8,128)(2,1)S(1)}, u32[]{:S(2)}, u32[]{:S(2)}) %collective-permute-start.6) | collective-permute-done | bytes 262176 | tf_op jit(solution)/shard_map/ppermute | solution.py:28
  52.1 6.4 %collective-permute-done.13 = bf16[64,2048]{1,0:T(8,128)(2,1)S(1)} collective-permute-done((bf16[64,2048]{1,0:T(8,128)(2,1)S(1)}, bf16[64,2048]{1,0:T(8,128)(2,1)S(1)}, u32[]{:S(2)}, u32[]{:S(2)}) %collective-permute-start.13) | collective-permute-done | bytes 262176 | tf_op jit(solution)/shard_map/ppermute | solution.py:28
  58.5 0.0 collective-permute-done.8
  58.5 0.9 %add_convert_fusion = bf16[64,2048]{1,0:T(8,128)(2,1)} fusion(bf16[64,2048]{1,0:T(8,128)(2,1)S(1)} %collective-permute-done.13, bf16[64,2048]{1,0:T(8,128)(2,1)S(1)} %collective-permute-done.8, bf16[64,2048]{1,0:T(8,128)(2,1)S(1)} %collective-permute-done.6, bf16[64,2048]{1,0:T(8,128)(2,1)S(1)} %get-tuple-element.22, f32[64]{0:T(128)S(1)} %get-tuple-element.34, ...), kind=kLoop, calls=%fused_computation | loop fusion | flops 1572864 | bytes 1311232 | tf_op jit(solution)/shard_map/convert_element_type | solution.py:122
  (1 shorter events, 0.0 us)
Async XLA Ops:
  0.0 29.0 %copy-start = (bf16[1,2,192,2048]{3,2,1,0:T(8,128)(2,1)S(1)}, bf16[1,2,192,2048]{3,2,1,0:T(8,128)(2,1)}, u32[]{:S(2)}) copy-start(bf16[1,2,192,2048]{3,2,1,0:T(8,128)(2,1)} %refs_3_.1) | copy-start | bytes 4718596
  0.0 29.0 %copy-start.1 = (bf16[1,192,2048]{2,1,0:T(8,128)(2,1)S(1)}, bf16[1,192,2048]{2,1,0:T(8,128)(2,1)}, u32[]{:S(2)}) copy-start(bf16[1,192,2048]{2,1,0:T(8,128)(2,1)} %refs_4_.3) | copy-start | bytes 2359300
  0.0 9.8 %collective-permute-start.4 = (bf16[64,2048]{1,0:T(8,128)(2,1)}, bf16[64,2048]{1,0:T(8,128)(2,1)S(1)}, u32[]{:S(2)}, u32[]{:S(2)}) collective-permute-start(bf16[64,2048]{1,0:T(8,128)(2,1)} %refs_0_), channel_id=1, source_target_pairs={{0,4},{4,0},{8,12},{12,8},{16,20},{20,16},{24,28},{28,24},{1,9},{5... | collective-permute-start | bytes 786440 | tf_op jit(solution)/shard_map/ppermute | solution.py:28
  2.9 10.6 %collective-permute-start.1 = (bf16[64,2048]{1,0:T(8,128)(2,1)}, bf16[64,2048]{1,0:T(8,128)(2,1)S(1)}, u32[]{:S(2)}, u32[]{:S(2)}) collective-permute-start(bf16[64,2048]{1,0:T(8,128)(2,1)} %refs_0_), channel_id=1, source_target_pairs={{0,8},{4,12},{8,0},{12,4},{16,24},{20,28},{24,16},{28,20},{1,5},{5... | collective-permute-start | bytes 786440 | tf_op jit(solution)/shard_map/ppermute | solution.py:28
  4.5 14.3 %collective-permute-start = (bf16[64,2048]{1,0:T(8,128)(2,1)}, bf16[64,2048]{1,0:T(8,128)(2,1)S(1)}, u32[]{:S(2)}, u32[]{:S(2)}) collective-permute-start(bf16[64,2048]{1,0:T(8,128)(2,1)} %refs_0_), channel_id=1, source_target_pairs={{0,16},{4,20},{8,24},{12,28},{16,0},{20,4},{24,8},{28,12},{1,17},{... | collective-permute-start | bytes 786440 | tf_op jit(solution)/shard_map/ppermute | solution.py:28
  9.8 9.2 %collective-permute-start.5 = (bf16[64,2048]{1,0:T(8,128)(2,1)S(1)}, bf16[64,2048]{1,0:T(8,128)(2,1)S(1)}, u32[]{:S(2)}, u32[]{:S(2)}) collective-permute-start(bf16[64,2048]{1,0:T(8,128)(2,1)S(1)} %collective-permute-done.4.refs_1_), channel_id=1, source_target_pairs={{0,8},{4,12},{8,0},{12,4},{16,24},{20,28},{24,16},{28,20},{1,5},{5... | collective-permute-start | bytes 786440 | tf_op jit(solution)/shard_map/ppermute | solution.py:28
  18.8 10.2 %collective-permute-start.2 = (bf16[64,2048]{1,0:T(8,128)(2,1)S(1)}, bf16[64,2048]{1,0:T(8,128)(2,1)S(1)}, u32[]{:S(2)}, u32[]{:S(2)}) collective-permute-start(bf16[64,2048]{1,0:T(8,128)(2,1)S(1)} %collective-permute-done.refs_0_), channel_id=1, source_target_pairs={{0,12},{4,8},{8,4},{12,0},{16,28},{20,24},{24,20},{28,16},{1,13},{... | collective-permute-start | bytes 786440 | tf_op jit(solution)/shard_map/ppermute | solution.py:28
  18.9 14.5 %collective-permute-start.10 = (bf16[64,2048]{1,0:T(8,128)(2,1)S(1)}, bf16[64,2048]{1,0:T(8,128)(2,1)S(1)}, u32[]{:S(2)}, u32[]{:S(2)}) collective-permute-start(bf16[64,2048]{1,0:T(8,128)(2,1)S(1)} %collective-permute-done.refs_0_), channel_id=1, source_target_pairs={{0,8},{4,12},{8,0},{12,4},{16,24},{20,28},{24,16},{28,20},{1,5},{5... | collective-permute-start | bytes 786440 | tf_op jit(solution)/shard_map/ppermute | solution.py:28
  20.9 13.6 %collective-permute-start.9 = (bf16[64,2048]{1,0:T(8,128)(2,1)S(1)}, bf16[64,2048]{1,0:T(8,128)(2,1)S(1)}, u32[]{:S(2)}, u32[]{:S(2)}) collective-permute-start(bf16[64,2048]{1,0:T(8,128)(2,1)S(1)} %collective-permute-done.refs_0_), channel_id=1, source_target_pairs={{0,4},{4,0},{8,12},{12,8},{16,20},{20,16},{24,28},{28,24},{1,9},{5... | collective-permute-start | bytes 786440 | tf_op jit(solution)/shard_map/ppermute | solution.py:28
  29.8 9.4 %copy-start.2 = (bf16[64,2048]{1,0:T(8,128)(2,1)S(1)}, bf16[64,2048]{1,0:T(8,128)(2,1)}, u32[]{:S(2)}) copy-start(bf16[64,2048]{1,0:T(8,128)(2,1)} %refs_0_) | copy-start | bytes 786436
  29.8 9.4 %collective-permute-start.3 = (bf16[64,2048]{1,0:T(8,128)(2,1)S(1)}, bf16[64,2048]{1,0:T(8,128)(2,1)S(1)}, u32[]{:S(2)}, u32[]{:S(2)}) collective-permute-start(bf16[64,2048]{1,0:T(8,128)(2,1)S(1)} %share.3), channel_id=1, source_target_pairs={{0,12},{4,8},{8,4},{12,0},{16,28},{20,24},{24,20},{28,16},{1,13},{... | collective-permute-start | bytes 786440 | tf_op jit(solution)/shard_map/ppermute | solution.py:28
  35.6 8.4 %collective-permute-start.11 = (bf16[64,2048]{1,0:T(8,128)(2,1)S(1)}, bf16[64,2048]{1,0:T(8,128)(2,1)S(1)}, u32[]{:S(2)}, u32[]{:S(2)}) collective-permute-start(bf16[64,2048]{1,0:T(8,128)(2,1)S(1)} %get-tuple-element.31), channel_id=1, source_target_pairs={{0,4},{4,0},{8,12},{12,8},{16,20},{20,16},{24,28},{28,24},{1,9},{5... | collective-permute-start | bytes 786440 | tf_op jit(solution)/shard_map/ppermute | solution.py:28
  36.3 9.2 %collective-permute-start.12 = (bf16[64,2048]{1,0:T(8,128)(2,1)S(1)}, bf16[64,2048]{1,0:T(8,128)(2,1)S(1)}, u32[]{:S(2)}, u32[]{:S(2)}) collective-permute-start(bf16[64,2048]{1,0:T(8,128)(2,1)S(1)} %get-tuple-element.32), channel_id=1, source_target_pairs={{0,8},{4,12},{8,0},{12,4},{16,24},{20,28},{24,16},{28,20},{1,5},{5... | collective-permute-start | bytes 786440 | tf_op jit(solution)/shard_map/ppermute | solution.py:28
  41.2 7.8 %copy-start.3 = (s32[2]{0:T(128)S(1)}, s32[2]{0:T(128)}, u32[]{:S(2)}) copy-start(s32[2]{0:T(128)} %param.9) | copy-start | bytes 28
  41.2 8.5 %copy-start.4 = (f32[64,2]{0,1:T(2,128)S(1)}, f32[64,2]{0,1:T(2,128)}, u32[]{:S(2)}) copy-start(f32[64,2]{0,1:T(2,128)} %param.7) | copy-start | bytes 1540
  41.2 8.5 %copy-start.5 = (s32[64,2]{0,1:T(2,128)S(1)}, s32[64,2]{0,1:T(2,128)}, u32[]{:S(2)}) copy-start(s32[64,2]{0,1:T(2,128)} %param.8) | copy-start | bytes 1540
  41.2 6.4 %collective-permute-start.7 = (bf16[64,2048]{1,0:T(8,128)(2,1)S(1)}, bf16[64,2048]{1,0:T(8,128)(2,1)S(1)}, u32[]{:S(2)}, u32[]{:S(2)}) collective-permute-start(bf16[64,2048]{1,0:T(8,128)(2,1)S(1)} %get-tuple-element.28), channel_id=1, source_target_pairs={{0,4},{4,0},{8,12},{12,8},{16,20},{20,16},{24,28},{28,24},{1,9},{5... | collective-permute-start | bytes 786440 | tf_op jit(solution)/shard_map/ppermute | solution.py:28
  41.2 10.9 %collective-permute-start.6 = (bf16[64,2048]{1,0:T(8,128)(2,1)}, bf16[64,2048]{1,0:T(8,128)(2,1)S(1)}, u32[]{:S(2)}, u32[]{:S(2)}) collective-permute-start(bf16[64,2048]{1,0:T(8,128)(2,1)} %get-tuple-element.24), channel_id=1, source_target_pairs={{0,4},{4,0},{8,12},{12,8},{16,20},{20,16},{24,28},{28,24},{1,9},{5... | collective-permute-start | bytes 786440 | tf_op jit(solution)/shard_map/ppermute | solution.py:28
  45.7 12.8 %collective-permute-start.13 = (bf16[64,2048]{1,0:T(8,128)(2,1)S(1)}, bf16[64,2048]{1,0:T(8,128)(2,1)S(1)}, u32[]{:S(2)}, u32[]{:S(2)}) collective-permute-start(bf16[64,2048]{1,0:T(8,128)(2,1)S(1)} %add_convert_fusion.1), channel_id=1, source_target_pairs={{0,16},{4,20},{8,24},{12,28},{16,0},{20,4},{24,8},{28,12},{1,17},{... | collective-permute-start | bytes 786440 | tf_op jit(solution)/shard_map/ppermute | solution.py:28
  47.6 10.9 %collective-permute-start.8 = (bf16[64,2048]{1,0:T(8,128)(2,1)S(1)}, bf16[64,2048]{1,0:T(8,128)(2,1)S(1)}, u32[]{:S(2)}, u32[]{:S(2)}) collective-permute-start(bf16[64,2048]{1,0:T(8,128)(2,1)S(1)} %add_convert_fusion.3), channel_id=1, source_target_pairs={{0,8},{4,12},{8,0},{12,4},{16,24},{20,28},{24,16},{28,20},{1,5},{5... | collective-permute-start | bytes 786440 | tf_op jit(solution)/shard_map/ppermute | solution.py:28

commit v4 on v3

--- a/solution.py
+++ b/solution.py
@@ -68,7 +68,7 @@
     n = len(blocks)
     return pl.pallas_call(
         share_kernel,
-        out_shape=[jax.ShapeDtypeStruct((rows, width), jnp.bfloat16)] * n,
+        out_shape=[pltpu.VMEM((rows, width), jnp.bfloat16)] * n,
         in_specs=[pl.BlockSpec(memory_space=pltpu.VMEM)] * (n + 2),
         out_specs=[pl.BlockSpec(memory_space=pltpu.VMEM)] * n,
         compiler_params=pltpu.CompilerParams(vmem_limit_bytes=32 << 20),
@@ -106,15 +106,15 @@
     theirs_b = exchange(theirs, *second)
     (away_d,) = share([theirs_d], w_in, w_out)
     away, away_a, away_b = share([theirs, theirs_a, theirs_b], w_in, w_out)
+    back_d = exchange(away_d, *first)
     back_a = exchange(away_a, *first)
-    back_b = exchange(away_b, *second)
-    back_d = exchange(away_d, *across)
-    away_sum = summed(away, back_a, back_b, back_d)
+    back_b = exchange(summed(away_b, back_d), *second)
+    away_sum = summed(away, back_a, back_b)
     home = share([after(tokens, back_d), ours_a, ours_b, ours_d], w_in, w_out)
     home = [after(h, back_d) for h in home]
-    home_d = exchange(home[3], *first)
-    home_a = exchange(home[1], *first)
-    home_b = exchange(summed(home[2], home_d), *second)
+    home_d = exchange(home[3], *second)
+    home_b = exchange(home[2], *second)
+    home_a = exchange(summed(home[1], home_d), *first)
     other = exchange(away_sum, *group)
     own = summed(home[0], home_a, home_b)
     return (

time: 59.5 us -> 58.5 us (0.983)
  waiting for transfers between devices: 32.3 us -> 29.9 us
  starting transfers between devices: 17.7 us -> 19 us
    ppermute x14, waiting for transfers between devices: 32.3 us -> 29.9 us  [exchange(): return lax.ppermute(block, ('ep', 'dp'), route)]
    ppermute x14, starting transfers between devices: 17.7 us -> 19 us  [exchange(): return lax.ppermute(block, ('ep', 'dp'), route)]
  transfers between devices with their start and end apart: 14 -> 14, of which waited for: 11 -> 8; matrix products, arithmetic and copies ran while one was open for 4% -> 4% of each run, Pallas kernels for 10% -> 11%
where the time goes in v4:
time: 58.5 us; the launch traced here: 58.3 us
  waiting for transfers between devices  29.9 us (51%)
  starting transfers between devices  19 us (32%)
  Pallas kernels  6.13 us (10%)
  other arithmetic  2.5 us (4%)
  local copies, waits for them, and re-layouts  0.69 us (1%)
    ppermute x14, waiting for transfers between devices, exchange(): return lax.ppermute(block, ('ep', 'dp'), route)  29.9 us
    ppermute x14, starting transfers between devices, exchange(): return lax.ppermute(block, ('ep', 'dp'), route)  19 us
    pallas_call x3, Pallas kernels, share(): pl.pallas_call(share_kernel, out_shape=[pltpu.VMEM((rows, width), jnp.bfl...  3.95 us
    pallas_call x1, Pallas kernels, touch(): pl.pallas_call(touch_kernel, out_shape=jax.ShapeDtypeStruct((8, 128), jnp...  2.19 us
    reduce_sum x1, other arithmetic, everywhere(): jnp.sum(jnp.where(expert_ids == named, gates, 0.0), axis=1, keepdims=True)  1.39 us
  transfers between devices with their start and end apart: 14, of which 8 were waited for; matrix products, arithmetic and copies ran while one was open for 4% of the time, Pallas kernels for 11%

profile of v4, /device:TPU:0, one launch (start us, length us, event | category | flops | bytes accessed | tf_op | source)
XLA Modules:
  0.0 58.3 jit_solution(17943238789204472873)
XLA Ops:
  0.0 0.0 copy-start
  0.0 0.0 copy-start.1
  0.0 2.9 %collective-permute-start.4 = (bf16[64,2048]{1,0:T(8,128)(2,1)}, bf16[64,2048]{1,0:T(8,128)(2,1)S(1)}, u32[]{:S(2)}, u32[]{:S(2)}) collective-permute-start(bf16[64,2048]{1,0:T(8,128)(2,1)} %refs_0_), channel_id=1, source_target_pairs={{0,4},{4,0},{8,12},{12,8},{16,20},{20,16},{24,28},{28,24},{1,9},{5... | collective-permute-start | bytes 786440 | tf_op jit(solution)/shard_map/ppermute | solution.py:28
  2.9 1.6 %collective-permute-start.1 = (bf16[64,2048]{1,0:T(8,128)(2,1)}, bf16[64,2048]{1,0:T(8,128)(2,1)S(1)}, u32[]{:S(2)}, u32[]{:S(2)}) collective-permute-start(bf16[64,2048]{1,0:T(8,128)(2,1)} %refs_0_), channel_id=1, source_target_pairs={{0,8},{4,12},{8,0},{12,4},{16,24},{20,28},{24,16},{28,20},{1,5},{5... | collective-permute-start | bytes 786440 | tf_op jit(solution)/shard_map/ppermute | solution.py:28
  4.5 2.6 %collective-permute-start = (bf16[64,2048]{1,0:T(8,128)(2,1)}, bf16[64,2048]{1,0:T(8,128)(2,1)S(1)}, u32[]{:S(2)}, u32[]{:S(2)}) collective-permute-start(bf16[64,2048]{1,0:T(8,128)(2,1)} %refs_0_), channel_id=1, source_target_pairs={{0,16},{4,20},{8,24},{12,28},{16,0},{20,4},{24,8},{28,12},{1,17},{... | collective-permute-start | bytes 786440 | tf_op jit(solution)/shard_map/ppermute | solution.py:28
  7.1 2.7 %collective-permute-done.4.refs_1_ = bf16[64,2048]{1,0:T(8,128)(2,1)S(1)} collective-permute-done((bf16[64,2048]{1,0:T(8,128)(2,1)}, bf16[64,2048]{1,0:T(8,128)(2,1)S(1)}, u32[]{:S(2)}, u32[]{:S(2)}) %collective-permute-start.4) | collective-permute-done | bytes 262176 | tf_op jit(solution)/shard_map/ppermute | solution.py:28
  9.8 1.6 %collective-permute-start.5 = (bf16[64,2048]{1,0:T(8,128)(2,1)S(1)}, bf16[64,2048]{1,0:T(8,128)(2,1)S(1)}, u32[]{:S(2)}, u32[]{:S(2)}) collective-permute-start(bf16[64,2048]{1,0:T(8,128)(2,1)S(1)} %collective-permute-done.4.refs_1_), channel_id=1, source_target_pairs={{0,8},{4,12},{8,0},{12,4},{16,24},{20,28},{24,16},{28,20},{1,5},{5... | collective-permute-start | bytes 786440 | tf_op jit(solution)/shard_map/ppermute | solution.py:28
  11.4 2.2 %touch.1 = bf16[8,128]{1,0:T(8,128)(2,1)} custom-call(bf16[1,2,192,2048]{3,2,1,0:T(8,128)(2,1)} %refs_3_.1, bf16[1,192,2048]{2,1,0:T(8,128)(2,1)} %refs_4_.3), custom_call_target="tpu_custom_call" | custom-call | tf_op jit(solution)/shard_map/touch/pallas_call | solution.py:40
  13.5 0.0 collective-permute-done.1.refs_2_
  13.6 5.2 %collective-permute-done.refs_0_ = bf16[64,2048]{1,0:T(8,128)(2,1)S(1)} collective-permute-done((bf16[64,2048]{1,0:T(8,128)(2,1)}, bf16[64,2048]{1,0:T(8,128)(2,1)S(1)}, u32[]{:S(2)}, u32[]{:S(2)}) %collective-permute-start) | collective-permute-done | bytes 262176 | tf_op jit(solution)/shard_map/ppermute | solution.py:28
  18.8 0.1 collective-permute-start.2
  18.9 0.0 collective-permute-done.5.refs_3_
  18.9 2.0 %collective-permute-start.10 = (bf16[64,2048]{1,0:T(8,128)(2,1)S(1)}, bf16[64,2048]{1,0:T(8,128)(2,1)S(1)}, u32[]{:S(2)}, u32[]{:S(2)}) collective-permute-start(bf16[64,2048]{1,0:T(8,128)(2,1)S(1)} %collective-permute-done.refs_0_), channel_id=1, source_target_pairs={{0,8},{4,12},{8,0},{12,4},{16,24},{20,28},{24,16},{28,20},{1,5},{5... | collective-permute-start | bytes 786440 | tf_op jit(solution)/shard_map/ppermute | solution.py:28
  20.9 1.4 %collective-permute-start.9 = (bf16[64,2048]{1,0:T(8,128)(2,1)S(1)}, bf16[64,2048]{1,0:T(8,128)(2,1)S(1)}, u32[]{:S(2)}, u32[]{:S(2)}) collective-permute-start(bf16[64,2048]{1,0:T(8,128)(2,1)S(1)} %collective-permute-done.refs_0_), channel_id=1, source_target_pairs={{0,4},{4,0},{8,12},{12,8},{16,20},{20,16},{24,28},{28,24},{1,9},{5... | collective-permute-start | bytes 786440 | tf_op jit(solution)/shard_map/ppermute | solution.py:28
  22.3 6.7 %collective-permute-done.2.refs_0_ = bf16[64,2048]{1,0:T(8,128)(2,1)S(1)} collective-permute-done((bf16[64,2048]{1,0:T(8,128)(2,1)S(1)}, bf16[64,2048]{1,0:T(8,128)(2,1)S(1)}, u32[]{:S(2)}, u32[]{:S(2)}) %collective-permute-start.2) | collective-permute-done | bytes 262176 | tf_op jit(solution)/shard_map/ppermute | solution.py:28
  29.0 0.0 copy-done
  29.0 0.0 copy-done.1
  29.0 0.9 %share.3 = bf16[64,2048]{1,0:T(8,128)(2,1)S(1)} custom-call(bf16[64,2048]{1,0:T(8,128)(2,1)S(1)} %collective-permute-done.2.refs_0_, bf16[1,2,192,2048]{3,2,1,0:T(8,128)(2,1)S(1)} %copy-done, bf16[1,192,2048]{2,1,0:T(8,128)(2,1)S(1)} %copy-done.1), custom_call_target="tpu_custom_call" | custom-call | flops 150994944 | bytes 2883584 | tf_op jit(solution)/shard_map/share/pallas_call | solution.py:69
  29.8 0.0 copy-start.2
  29.8 0.4 collective-permute-start.3
  30.2 3.2 %collective-permute-done.10.refs_2_ = bf16[64,2048]{1,0:T(8,128)(2,1)S(1)} collective-permute-done((bf16[64,2048]{1,0:T(8,128)(2,1)S(1)}, bf16[64,2048]{1,0:T(8,128)(2,1)S(1)}, u32[]{:S(2)}, u32[]{:S(2)}) %collective-permute-start.10) | collective-permute-done | bytes 262176 | tf_op jit(solution)/shard_map/ppermute | solution.py:28
  33.4 0.0 collective-permute-done.9.refs_1_
  33.4 1.1 %share.5 = (bf16[64,2048]{1,0:T(8,128)(2,1)S(1)}, bf16[64,2048]{1,0:T(8,128)(2,1)S(1)}, bf16[64,2048]{1,0:T(8,128)(2,1)S(1)}) custom-call(bf16[64,2048]{1,0:T(8,128)(2,1)S(1)} %collective-permute-done.refs_0_, bf16[64,2048]{1,0:T(8,128)(2,1)S(1)} %collective-permute-done.9.refs_1_, bf16[64,2048]{1,0:T(8,128)(2,1)S(1)} %collective-permute-done.10.refs_2_, ...), custom_call_target="tpu_custom_call" | custom-call | flops 452984832 | bytes 3932160 | tf_op jit(solution)/shard_map/share/pallas_call | solution.py:69
  34.5 1.8 %collective-permute-done.3 = bf16[64,2048]{1,0:T(8,128)(2,1)S(1)} collective-permute-done((bf16[64,2048]{1,0:T(8,128)(2,1)S(1)}, bf16[64,2048]{1,0:T(8,128)(2,1)S(1)}, u32[]{:S(2)}, u32[]{:S(2)}) %collective-permute-start.3) | collective-permute-done | bytes 262176 | tf_op jit(solution)/shard_map/ppermute | solution.py:28
  36.3 0.1 add_convert_fusion.2
  36.3 0.1 collective-permute-start.12
  36.4 0.7 %collective-permute-start.11 = (bf16[64,2048]{1,0:T(8,128)(2,1)S(1)}, bf16[64,2048]{1,0:T(8,128)(2,1)S(1)}, u32[]{:S(2)}, u32[]{:S(2)}) collective-permute-start(bf16[64,2048]{1,0:T(8,128)(2,1)S(1)} %get-tuple-element.31), channel_id=1, source_target_pairs={{0,4},{4,0},{8,12},{12,8},{16,20},{20,16},{24,28},{28,24},{1,9},{5... | collective-permute-start | bytes 786440 | tf_op jit(solution)/shard_map/ppermute | solution.py:28
  37.1 0.0 copy-done.2
  37.1 2.0 %share.4 = (bf16[64,2048]{1,0:T(8,128)(2,1)S(1)}, bf16[64,2048]{1,0:T(8,128)(2,1)S(1)}, bf16[64,2048]{1,0:T(8,128)(2,1)}, bf16[64,2048]{1,0:T(8,128)(2,1)S(1)}) custom-call(bf16[64,2048]{1,0:T(8,128)(2,1)S(1)} %copy-done.2, bf16[64,2048]{1,0:T(8,128)(2,1)S(1)} %collective-permute-done.4.refs_1_, bf16[64,2048]{1,0:T(8,128)(2,1)S(1)} %collective-permute-done.1.refs_2_, ...), custom_call_target="tpu_custom_call" | custom-call | flops 603979776 | bytes 4456448 | tf_op jit(solution)/shard_map/share/pallas_call | solution.py:69
  39.1 0.0 copy-start.3
  39.1 1.6 %collective-permute-start.6 = (bf16[64,2048]{1,0:T(8,128)(2,1)S(1)}, bf16[64,2048]{1,0:T(8,128)(2,1)S(1)}, u32[]{:S(2)}, u32[]{:S(2)}) collective-permute-start(bf16[64,2048]{1,0:T(8,128)(2,1)S(1)} %get-tuple-element.26), channel_id=1, source_target_pairs={{0,8},{4,12},{8,0},{12,4},{16,24},{20,28},{24,16},{28,20},{1,5},{5... | collective-permute-start | bytes 786440 | tf_op jit(solution)/shard_map/ppermute | solution.py:28
  40.7 0.4 collective-permute-start.8
  41.2 2.3 %collective-permute-done.12 = bf16[64,2048]{1,0:T(8,128)(2,1)S(1)} collective-permute-done((bf16[64,2048]{1,0:T(8,128)(2,1)S(1)}, bf16[64,2048]{1,0:T(8,128)(2,1)S(1)}, u32[]{:S(2)}, u32[]{:S(2)}) %collective-permute-start.12) | collective-permute-done | bytes 262176 | tf_op jit(solution)/shard_map/ppermute | solution.py:28
  43.5 2.2 %collective-permute-done.11 = bf16[64,2048]{1,0:T(8,128)(2,1)S(1)} collective-permute-done((bf16[64,2048]{1,0:T(8,128)(2,1)S(1)}, bf16[64,2048]{1,0:T(8,128)(2,1)S(1)}, u32[]{:S(2)}, u32[]{:S(2)}) %collective-permute-start.11) | collective-permute-done | bytes 262176 | tf_op jit(solution)/shard_map/ppermute | solution.py:28
  45.7 0.1 add_convert_fusion.1
  45.8 3.1 %collective-permute-start.13 = (bf16[64,2048]{1,0:T(8,128)(2,1)S(1)}, bf16[64,2048]{1,0:T(8,128)(2,1)S(1)}, u32[]{:S(2)}, u32[]{:S(2)}) collective-permute-start(bf16[64,2048]{1,0:T(8,128)(2,1)S(1)} %add_convert_fusion.1), channel_id=1, source_target_pairs={{0,16},{4,20},{8,24},{12,28},{16,0},{20,4},{24,8},{28,12},{1,17},{... | collective-permute-start | bytes 786440 | tf_op jit(solution)/shard_map/ppermute | solution.py:28
  48.9 0.0 collective-permute-done.6
  48.9 0.1 add_convert_fusion.4
  48.9 0.6 %collective-permute-start.7 = (bf16[64,2048]{1,0:T(8,128)(2,1)S(1)}, bf16[64,2048]{1,0:T(8,128)(2,1)S(1)}, u32[]{:S(2)}, u32[]{:S(2)}) collective-permute-start(bf16[64,2048]{1,0:T(8,128)(2,1)S(1)} %add_convert_fusion.4), channel_id=1, source_target_pairs={{0,4},{4,0},{8,12},{12,8},{16,20},{20,16},{24,28},{28,24},{1,9},{5... | collective-permute-start | bytes 786440 | tf_op jit(solution)/shard_map/ppermute | solution.py:28
  49.5 0.0 copy-done.3
  49.5 0.7 %fusion.2 = (s32[1]{0:T(128)}, s32[1]{0:T(128)}) fusion(s32[2]{0:T(128)S(1)} %copy-done.3, s32[]{:T(128)S(6)} %select_n.34, s32[]{:T(128)S(6)} %select_n.31), kind=kLoop, calls=%fused_computation.9 | loop fusion | bytes 24 | tf_op jit(solution)/shard_map/jit(dynamic_index_in_dim)/dynamic_slice | solution.py:96
  50.2 0.0 copy-done.4
  50.2 0.0 copy-done.5
  50.2 1.4 %fusion = (f32[64]{0:T(128)S(1)}, f32[64]{0:T(128)S(1)}) fusion(f32[64,2]{0,1:T(2,128)S(1)} %copy-done.4, s32[64,2]{0,1:T(2,128)S(1)} %copy-done.5, s32[]{:T(128)} %bitcast, s32[]{:T(128)} %bitcast.1), kind=kLoop, calls=%fused_computation.7 | loop fusion | flops 640 | bytes 1544 | tf_op jit(solution)/shard_map/reduce_sum | solution.py:97
  51.6 5.8 %collective-permute-done.8 = bf16[64,2048]{1,0:T(8,128)(2,1)S(1)} collective-permute-done((bf16[64,2048]{1,0:T(8,128)(2,1)}, bf16[64,2048]{1,0:T(8,128)(2,1)S(1)}, u32[]{:S(2)}, u32[]{:S(2)}) %collective-permute-start.8) | collective-permute-done | bytes 262176 | tf_op jit(solution)/shard_map/ppermute | solution.py:28
  57.4 0.0 collective-permute-done.13
  57.4 0.0 collective-permute-done.7
  57.4 0.9 %add_convert_fusion = bf16[64,2048]{1,0:T(8,128)(2,1)} fusion(bf16[64,2048]{1,0:T(8,128)(2,1)S(1)} %collective-permute-done.13, bf16[64,2048]{1,0:T(8,128)(2,1)S(1)} %collective-permute-done.8, bf16[64,2048]{1,0:T(8,128)(2,1)S(1)} %collective-permute-done.7, bf16[64,2048]{1,0:T(8,128)(2,1)S(1)} %get-tuple-element.22, f32[64]{0:T(128)S(1)} %get-tuple-element.34, ...), kind=kLoop, calls=%fused_computation | loop fusion | flops 1572864 | bytes 1311232 | tf_op jit(solution)/shard_map/convert_element_type | solution.py:122
  (2 shorter events, 0.0 us)
Async XLA Ops:
  0.0 29.0 %copy-start = (bf16[1,2,192,2048]{3,2,1,0:T(8,128)(2,1)S(1)}, bf16[1,2,192,2048]{3,2,1,0:T(8,128)(2,1)}, u32[]{:S(2)}) copy-start(bf16[1,2,192,2048]{3,2,1,0:T(8,128)(2,1)} %refs_3_.1) | copy-start | bytes 4718596
  0.0 29.0 %copy-start.1 = (bf16[1,192,2048]{2,1,0:T(8,128)(2,1)S(1)}, bf16[1,192,2048]{2,1,0:T(8,128)(2,1)}, u32[]{:S(2)}) copy-start(bf16[1,192,2048]{2,1,0:T(8,128)(2,1)} %refs_4_.3) | copy-start | bytes 2359300
  0.0 9.8 %collective-permute-start.4 = (bf16[64,2048]{1,0:T(8,128)(2,1)}, bf16[64,2048]{1,0:T(8,128)(2,1)S(1)}, u32[]{:S(2)}, u32[]{:S(2)}) collective-permute-start(bf16[64,2048]{1,0:T(8,128)(2,1)} %refs_0_), channel_id=1, source_target_pairs={{0,4},{4,0},{8,12},{12,8},{16,20},{20,16},{24,28},{28,24},{1,9},{5... | collective-permute-start | bytes 786440 | tf_op jit(solution)/shard_map/ppermute | solution.py:28
  2.9 10.6 %collective-permute-start.1 = (bf16[64,2048]{1,0:T(8,128)(2,1)}, bf16[64,2048]{1,0:T(8,128)(2,1)S(1)}, u32[]{:S(2)}, u32[]{:S(2)}) collective-permute-start(bf16[64,2048]{1,0:T(8,128)(2,1)} %refs_0_), channel_id=1, source_target_pairs={{0,8},{4,12},{8,0},{12,4},{16,24},{20,28},{24,16},{28,20},{1,5},{5... | collective-permute-start | bytes 786440 | tf_op jit(solution)/shard_map/ppermute | solution.py:28
  4.5 14.3 %collective-permute-start = (bf16[64,2048]{1,0:T(8,128)(2,1)}, bf16[64,2048]{1,0:T(8,128)(2,1)S(1)}, u32[]{:S(2)}, u32[]{:S(2)}) collective-permute-start(bf16[64,2048]{1,0:T(8,128)(2,1)} %refs_0_), channel_id=1, source_target_pairs={{0,16},{4,20},{8,24},{12,28},{16,0},{20,4},{24,8},{28,12},{1,17},{... | collective-permute-start | bytes 786440 | tf_op jit(solution)/shard_map/ppermute | solution.py:28
  9.8 9.2 %collective-permute-start.5 = (bf16[64,2048]{1,0:T(8,128)(2,1)S(1)}, bf16[64,2048]{1,0:T(8,128)(2,1)S(1)}, u32[]{:S(2)}, u32[]{:S(2)}) collective-permute-start(bf16[64,2048]{1,0:T(8,128)(2,1)S(1)} %collective-permute-done.4.refs_1_), channel_id=1, source_target_pairs={{0,8},{4,12},{8,0},{12,4},{16,24},{20,28},{24,16},{28,20},{1,5},{5... | collective-permute-start | bytes 786440 | tf_op jit(solution)/shard_map/ppermute | solution.py:28
  18.8 10.2 %collective-permute-start.2 = (bf16[64,2048]{1,0:T(8,128)(2,1)S(1)}, bf16[64,2048]{1,0:T(8,128)(2,1)S(1)}, u32[]{:S(2)}, u32[]{:S(2)}) collective-permute-start(bf16[64,2048]{1,0:T(8,128)(2,1)S(1)} %collective-permute-done.refs_0_), channel_id=1, source_target_pairs={{0,12},{4,8},{8,4},{12,0},{16,28},{20,24},{24,20},{28,16},{1,13},{... | collective-permute-start | bytes 786440 | tf_op jit(solution)/shard_map/ppermute | solution.py:28
  18.9 14.5 %collective-permute-start.10 = (bf16[64,2048]{1,0:T(8,128)(2,1)S(1)}, bf16[64,2048]{1,0:T(8,128)(2,1)S(1)}, u32[]{:S(2)}, u32[]{:S(2)}) collective-permute-start(bf16[64,2048]{1,0:T(8,128)(2,1)S(1)} %collective-permute-done.refs_0_), channel_id=1, source_target_pairs={{0,8},{4,12},{8,0},{12,4},{16,24},{20,28},{24,16},{28,20},{1,5},{5... | collective-permute-start | bytes 786440 | tf_op jit(solution)/shard_map/ppermute | solution.py:28
  20.9 12.5 %collective-permute-start.9 = (bf16[64,2048]{1,0:T(8,128)(2,1)S(1)}, bf16[64,2048]{1,0:T(8,128)(2,1)S(1)}, u32[]{:S(2)}, u32[]{:S(2)}) collective-permute-start(bf16[64,2048]{1,0:T(8,128)(2,1)S(1)} %collective-permute-done.refs_0_), channel_id=1, source_target_pairs={{0,4},{4,0},{8,12},{12,8},{16,20},{20,16},{24,28},{28,24},{1,9},{5... | collective-permute-start | bytes 786440 | tf_op jit(solution)/shard_map/ppermute | solution.py:28
  29.8 7.3 %copy-start.2 = (bf16[64,2048]{1,0:T(8,128)(2,1)S(1)}, bf16[64,2048]{1,0:T(8,128)(2,1)}, u32[]{:S(2)}) copy-start(bf16[64,2048]{1,0:T(8,128)(2,1)} %refs_0_) | copy-start | bytes 786436
  29.8 6.4 %collective-permute-start.3 = (bf16[64,2048]{1,0:T(8,128)(2,1)S(1)}, bf16[64,2048]{1,0:T(8,128)(2,1)S(1)}, u32[]{:S(2)}, u32[]{:S(2)}) collective-permute-start(bf16[64,2048]{1,0:T(8,128)(2,1)S(1)} %share.3), channel_id=1, source_target_pairs={{0,4},{4,0},{8,12},{12,8},{16,20},{20,16},{24,28},{28,24},{1,9},{5... | collective-permute-start | bytes 786440 | tf_op jit(solution)/shard_map/ppermute | solution.py:28
  36.3 7.1 %collective-permute-start.12 = (bf16[64,2048]{1,0:T(8,128)(2,1)S(1)}, bf16[64,2048]{1,0:T(8,128)(2,1)S(1)}, u32[]{:S(2)}, u32[]{:S(2)}) collective-permute-start(bf16[64,2048]{1,0:T(8,128)(2,1)S(1)} %add_convert_fusion.2), channel_id=1, source_target_pairs={{0,8},{4,12},{8,0},{12,4},{16,24},{20,28},{24,16},{28,20},{1,5},{5... | collective-permute-start | bytes 786440 | tf_op jit(solution)/shard_map/ppermute | solution.py:28
  36.4 9.2 %collective-permute-start.11 = (bf16[64,2048]{1,0:T(8,128)(2,1)S(1)}, bf16[64,2048]{1,0:T(8,128)(2,1)S(1)}, u32[]{:S(2)}, u32[]{:S(2)}) collective-permute-start(bf16[64,2048]{1,0:T(8,128)(2,1)S(1)} %get-tuple-element.31), channel_id=1, source_target_pairs={{0,4},{4,0},{8,12},{12,8},{16,20},{20,16},{24,28},{28,24},{1,9},{5... | collective-permute-start | bytes 786440 | tf_op jit(solution)/shard_map/ppermute | solution.py:28
  39.1 10.4 %copy-start.3 = (s32[2]{0:T(128)S(1)}, s32[2]{0:T(128)}, u32[]{:S(2)}) copy-start(s32[2]{0:T(128)} %param.9) | copy-start | bytes 28
  39.1 11.1 %copy-start.4 = (f32[64,2]{0,1:T(2,128)S(1)}, f32[64,2]{0,1:T(2,128)}, u32[]{:S(2)}) copy-start(f32[64,2]{0,1:T(2,128)} %param.7) | copy-start | bytes 1540
  39.1 11.1 %copy-start.5 = (s32[64,2]{0,1:T(2,128)S(1)}, s32[64,2]{0,1:T(2,128)}, u32[]{:S(2)}) copy-start(s32[64,2]{0,1:T(2,128)} %param.8) | copy-start | bytes 1540
  39.1 9.7 %collective-permute-start.6 = (bf16[64,2048]{1,0:T(8,128)(2,1)S(1)}, bf16[64,2048]{1,0:T(8,128)(2,1)S(1)}, u32[]{:S(2)}, u32[]{:S(2)}) collective-permute-start(bf16[64,2048]{1,0:T(8,128)(2,1)S(1)} %get-tuple-element.26), channel_id=1, source_target_pairs={{0,8},{4,12},{8,0},{12,4},{16,24},{20,28},{24,16},{28,20},{1,5},{5... | collective-permute-start | bytes 786440 | tf_op jit(solution)/shard_map/ppermute | solution.py:28
  40.7 16.7 %collective-permute-start.8 = (bf16[64,2048]{1,0:T(8,128)(2,1)}, bf16[64,2048]{1,0:T(8,128)(2,1)S(1)}, u32[]{:S(2)}, u32[]{:S(2)}) collective-permute-start(bf16[64,2048]{1,0:T(8,128)(2,1)} %get-tuple-element.28), channel_id=1, source_target_pairs={{0,8},{4,12},{8,0},{12,4},{16,24},{20,28},{24,16},{28,20},{1,5},{5... | collective-permute-start | bytes 786440 | tf_op jit(solution)/shard_map/ppermute | solution.py:28
  45.8 11.6 %collective-permute-start.13 = (bf16[64,2048]{1,0:T(8,128)(2,1)S(1)}, bf16[64,2048]{1,0:T(8,128)(2,1)S(1)}, u32[]{:S(2)}, u32[]{:S(2)}) collective-permute-start(bf16[64,2048]{1,0:T(8,128)(2,1)S(1)} %add_convert_fusion.1), channel_id=1, source_target_pairs={{0,16},{4,20},{8,24},{12,28},{16,0},{20,4},{24,8},{28,12},{1,17},{... | collective-permute-start | bytes 786440 | tf_op jit(solution)/shard_map/ppermute | solution.py:28
  48.9 8.5 %collective-permute-start.7 = (bf16[64,2048]{1,0:T(8,128)(2,1)S(1)}, bf16[64,2048]{1,0:T(8,128)(2,1)S(1)}, u32[]{:S(2)}, u32[]{:S(2)}) collective-permute-start(bf16[64,2048]{1,0:T(8,128)(2,1)S(1)} %add_convert_fusion.4), channel_id=1, source_target_pairs={{0,4},{4,0},{8,12},{12,8},{16,20},{20,16},{24,28},{28,24},{1,9},{5... | collective-permute-start | bytes 786440 | tf_op jit(solution)/shard_map/ppermute | solution.py:28

commit v5 on v4

--- a/solution.py
+++ b/solution.py
@@ -62,7 +62,7 @@
         ).astype(jnp.bfloat16)
 
 
-def share(blocks, w_in, w_out):
+def share(blocks, w_in, w_out, load=1):
     rows, width = blocks[0].shape
     units = w_out.shape[1]
     n = len(blocks)
@@ -73,7 +73,7 @@
         out_specs=[pl.BlockSpec(memory_space=pltpu.VMEM)] * n,
         compiler_params=pltpu.CompilerParams(vmem_limit_bytes=32 << 20),
         cost_estimate=pl.CostEstimate(
-            flops=6 * n * rows * width * units,
+            flops=load * 6 * n * rows * width * units,
             bytes_accessed=2 * (2 * n * rows * width + 3 * units * width),
             transcendentals=n * rows * units,
         ),
@@ -104,7 +104,7 @@
     theirs = after(theirs, ours_d)
     theirs_a = exchange(theirs, *first)
     theirs_b = exchange(theirs, *second)
-    (away_d,) = share([theirs_d], w_in, w_out)
+    (away_d,) = share([theirs_d], w_in, w_out, load=8)
     away, away_a, away_b = share([theirs, theirs_a, theirs_b], w_in, w_out)
     back_d = exchange(away_d, *first)
     back_a = exchange(away_a, *first)

time: 58.5 us -> 57.8 us (0.988)
  waiting for transfers between devices: 29.9 us -> 28 us
  starting transfers between devices: 19 us -> 20.4 us
  Pallas kernels: 6.13 us -> 5.51 us
    ppermute x14, waiting for transfers between devices: 29.9 us -> 28 us  [exchange(): return lax.ppermute(block, ('ep', 'dp'), route)]
    ppermute x14, starting transfers between devices: 19 us -> 20.4 us  [exchange(): return lax.ppermute(block, ('ep', 'dp'), route)]
    pallas_call x3, Pallas kernels: 3.95 us -> 3.33 us  [share(): pl.pallas_call(share_kernel, out_shape=[pltpu.VMEM((rows, width), jnp.bfl...]
  transfers between devices with their start and end apart: 14 -> 14, of which waited for: 8 -> 10; matrix products, arithmetic and copies ran while one was open for 4% -> 4% of each run, Pallas kernels for 11% -> 10%
where the time goes in v5:
time: 57.8 us; the launch traced here: 57.1 us
  waiting for transfers between devices  28 us (48%)
  starting transfers between devices  20.4 us (35%)
  Pallas kernels  5.51 us (10%)
  other arithmetic  2.46 us (4%)
  local copies, waits for them, and re-layouts  0.7 us (1%)
    ppermute x14, waiting for transfers between devices, exchange(): return lax.ppermute(block, ('ep', 'dp'), route)  28 us
    ppermute x14, starting transfers between devices, exchange(): return lax.ppermute(block, ('ep', 'dp'), route)  20.4 us
    pallas_call x3, Pallas kernels, share(): pl.pallas_call(share_kernel, out_shape=[pltpu.VMEM((rows, width), jnp.bfl...  3.33 us
    pallas_call x1, Pallas kernels, touch(): pl.pallas_call(touch_kernel, out_shape=jax.ShapeDtypeStruct((8, 128), jnp...  2.19 us
    reduce_sum x1, other arithmetic, everywhere(): jnp.sum(jnp.where(expert_ids == named, gates, 0.0), axis=1, keepdims=True)  1.35 us
  transfers between devices with their start and end apart: 14, of which 10 were waited for; matrix products, arithmetic and copies ran while one was open for 4% of the time, Pallas kernels for 10%

profile of v5, /device:TPU:0, one launch (start us, length us, event | category | flops | bytes accessed | tf_op | source)
XLA Modules:
  0.0 57.1 jit_solution(9485584887826299619)
XLA Ops:
  0.0 2.9 %collective-permute-start.4 = (bf16[64,2048]{1,0:T(8,128)(2,1)}, bf16[64,2048]{1,0:T(8,128)(2,1)S(1)}, u32[]{:S(2)}, u32[]{:S(2)}) collective-permute-start(bf16[64,2048]{1,0:T(8,128)(2,1)} %refs_0_), channel_id=1, source_target_pairs={{0,4},{4,0},{8,12},{12,8},{16,20},{20,16},{24,28},{28,24},{1,9},{5... | collective-permute-start | bytes 786440 | tf_op jit(solution)/shard_map/ppermute | solution.py:28
  2.9 1.6 %collective-permute-start.1 = (bf16[64,2048]{1,0:T(8,128)(2,1)}, bf16[64,2048]{1,0:T(8,128)(2,1)S(1)}, u32[]{:S(2)}, u32[]{:S(2)}) collective-permute-start(bf16[64,2048]{1,0:T(8,128)(2,1)} %refs_0_), channel_id=1, source_target_pairs={{0,8},{4,12},{8,0},{12,4},{16,24},{20,28},{24,16},{28,20},{1,5},{5... | collective-permute-start | bytes 786440 | tf_op jit(solution)/shard_map/ppermute | solution.py:28
  4.5 2.6 %collective-permute-start = (bf16[64,2048]{1,0:T(8,128)(2,1)}, bf16[64,2048]{1,0:T(8,128)(2,1)S(1)}, u32[]{:S(2)}, u32[]{:S(2)}) collective-permute-start(bf16[64,2048]{1,0:T(8,128)(2,1)} %refs_0_), channel_id=1, source_target_pairs={{0,16},{4,20},{8,24},{12,28},{16,0},{20,4},{24,8},{28,12},{1,17},{... | collective-permute-start | bytes 786440 | tf_op jit(solution)/shard_map/ppermute | solution.py:28
  7.1 2.2 %touch.1 = bf16[8,128]{1,0:T(8,128)(2,1)} custom-call(bf16[1,2,192,2048]{3,2,1,0:T(8,128)(2,1)} %refs_3_.1, bf16[1,192,2048]{2,1,0:T(8,128)(2,1)} %refs_4_.3), custom_call_target="tpu_custom_call" | custom-call | tf_op jit(solution)/shard_map/touch/pallas_call | solution.py:40
  9.3 0.5 collective-permute-done.4.refs_1_
  9.8 1.6 %collective-permute-start.5 = (bf16[64,2048]{1,0:T(8,128)(2,1)S(1)}, bf16[64,2048]{1,0:T(8,128)(2,1)S(1)}, u32[]{:S(2)}, u32[]{:S(2)}) collective-permute-start(bf16[64,2048]{1,0:T(8,128)(2,1)S(1)} %collective-permute-done.4.refs_1_), channel_id=1, source_target_pairs={{0,8},{4,12},{8,0},{12,4},{16,24},{20,28},{24,16},{28,20},{1,5},{5... | collective-permute-start | bytes 786440 | tf_op jit(solution)/shard_map/ppermute | solution.py:28
  11.4 1.6 %collective-permute-done.1.refs_2_ = bf16[64,2048]{1,0:T(8,128)(2,1)S(1)} collective-permute-done((bf16[64,2048]{1,0:T(8,128)(2,1)}, bf16[64,2048]{1,0:T(8,128)(2,1)S(1)}, u32[]{:S(2)}, u32[]{:S(2)}) %collective-permute-start.1) | collective-permute-done | bytes 262176 | tf_op jit(solution)/shard_map/ppermute | solution.py:28
  13.0 5.9 %collective-permute-done.refs_0_ = bf16[64,2048]{1,0:T(8,128)(2,1)S(1)} collective-permute-done((bf16[64,2048]{1,0:T(8,128)(2,1)}, bf16[64,2048]{1,0:T(8,128)(2,1)S(1)}, u32[]{:S(2)}, u32[]{:S(2)}) %collective-permute-start) | collective-permute-done | bytes 262176 | tf_op jit(solution)/shard_map/ppermute | solution.py:28
  18.9 0.1 collective-permute-start.2
  18.9 0.0 collective-permute-done.5.refs_3_
  18.9 2.0 %collective-permute-start.10 = (bf16[64,2048]{1,0:T(8,128)(2,1)S(1)}, bf16[64,2048]{1,0:T(8,128)(2,1)S(1)}, u32[]{:S(2)}, u32[]{:S(2)}) collective-permute-start(bf16[64,2048]{1,0:T(8,128)(2,1)S(1)} %collective-permute-done.refs_0_), channel_id=1, source_target_pairs={{0,8},{4,12},{8,0},{12,4},{16,24},{20,28},{24,16},{28,20},{1,5},{5... | collective-permute-start | bytes 786440 | tf_op jit(solution)/shard_map/ppermute | solution.py:28
  20.9 1.5 %collective-permute-start.9 = (bf16[64,2048]{1,0:T(8,128)(2,1)S(1)}, bf16[64,2048]{1,0:T(8,128)(2,1)S(1)}, u32[]{:S(2)}, u32[]{:S(2)}) collective-permute-start(bf16[64,2048]{1,0:T(8,128)(2,1)S(1)} %collective-permute-done.refs_0_), channel_id=1, source_target_pairs={{0,4},{4,0},{8,12},{12,8},{16,20},{20,16},{24,28},{28,24},{1,9},{5... | collective-permute-start | bytes 786440 | tf_op jit(solution)/shard_map/ppermute | solution.py:28
  22.4 4.5 %collective-permute-done.2.refs_0_ = bf16[64,2048]{1,0:T(8,128)(2,1)S(1)} collective-permute-done((bf16[64,2048]{1,0:T(8,128)(2,1)S(1)}, bf16[64,2048]{1,0:T(8,128)(2,1)S(1)}, u32[]{:S(2)}, u32[]{:S(2)}) %collective-permute-start.2) | collective-permute-done | bytes 262176 | tf_op jit(solution)/shard_map/ppermute | solution.py:28
  26.9 0.0 copy-done
  26.9 0.0 copy-done.1
  26.9 0.9 %share.3 = bf16[64,2048]{1,0:T(8,128)(2,1)S(1)} custom-call(bf16[64,2048]{1,0:T(8,128)(2,1)S(1)} %collective-permute-done.2.refs_0_, bf16[1,2,192,2048]{3,2,1,0:T(8,128)(2,1)S(1)} %copy-done, bf16[1,192,2048]{2,1,0:T(8,128)(2,1)S(1)} %copy-done.1), custom_call_target="tpu_custom_call" | custom-call | flops 1207959552 | bytes 2883584 | tf_op jit(solution)/shard_map/share/pallas_call | solution.py:69
  27.8 0.0 copy-start.2
  27.8 0.1 collective-permute-start.3
  27.8 2.6 %collective-permute-done.10.refs_2_ = bf16[64,2048]{1,0:T(8,128)(2,1)S(1)} collective-permute-done((bf16[64,2048]{1,0:T(8,128)(2,1)S(1)}, bf16[64,2048]{1,0:T(8,128)(2,1)S(1)}, u32[]{:S(2)}, u32[]{:S(2)}) %collective-permute-start.10) | collective-permute-done | bytes 262176 | tf_op jit(solution)/shard_map/ppermute | solution.py:28
  30.4 1.3 %collective-permute-done.9.refs_1_ = bf16[64,2048]{1,0:T(8,128)(2,1)S(1)} collective-permute-done((bf16[64,2048]{1,0:T(8,128)(2,1)S(1)}, bf16[64,2048]{1,0:T(8,128)(2,1)S(1)}, u32[]{:S(2)}, u32[]{:S(2)}) %collective-permute-start.9) | collective-permute-done | bytes 262176 | tf_op jit(solution)/shard_map/ppermute | solution.py:28
  31.8 1.1 %share.5 = (bf16[64,2048]{1,0:T(8,128)(2,1)S(1)}, bf16[64,2048]{1,0:T(8,128)(2,1)S(1)}, bf16[64,2048]{1,0:T(8,128)(2,1)S(1)}) custom-call(bf16[64,2048]{1,0:T(8,128)(2,1)S(1)} %collective-permute-done.refs_0_, bf16[64,2048]{1,0:T(8,128)(2,1)S(1)} %collective-permute-done.9.refs_1_, bf16[64,2048]{1,0:T(8,128)(2,1)S(1)} %collective-permute-done.10.refs_2_, ...), custom_call_target="tpu_custom_call" | custom-call | flops 452984832 | bytes 3932160 | tf_op jit(solution)/shard_map/share/pallas_call | solution.py:69
  32.9 1.7 %collective-permute-done.3 = bf16[64,2048]{1,0:T(8,128)(2,1)S(1)} collective-permute-done((bf16[64,2048]{1,0:T(8,128)(2,1)S(1)}, bf16[64,2048]{1,0:T(8,128)(2,1)S(1)}, u32[]{:S(2)}, u32[]{:S(2)}) %collective-permute-start.3) | collective-permute-done | bytes 262176 | tf_op jit(solution)/shard_map/ppermute | solution.py:28
  34.6 0.1 add_convert_fusion.2
  34.6 0.3 collective-permute-start.12
  34.9 0.6 %collective-permute-start.11 = (bf16[64,2048]{1,0:T(8,128)(2,1)S(1)}, bf16[64,2048]{1,0:T(8,128)(2,1)S(1)}, u32[]{:S(2)}, u32[]{:S(2)}) collective-permute-start(bf16[64,2048]{1,0:T(8,128)(2,1)S(1)} %get-tuple-element.31), channel_id=1, source_target_pairs={{0,4},{4,0},{8,12},{12,8},{16,20},{20,16},{24,28},{28,24},{1,9},{5... | collective-permute-start | bytes 786440 | tf_op jit(solution)/shard_map/ppermute | solution.py:28
  35.5 0.0 copy-done.2
  35.5 1.4 %share.4 = (bf16[64,2048]{1,0:T(8,128)(2,1)S(1)}, bf16[64,2048]{1,0:T(8,128)(2,1)S(1)}, bf16[64,2048]{1,0:T(8,128)(2,1)S(1)}, bf16[64,2048]{1,0:T(8,128)(2,1)S(1)}) custom-call(bf16[64,2048]{1,0:T(8,128)(2,1)S(1)} %copy-done.2, bf16[64,2048]{1,0:T(8,128)(2,1)S(1)} %collective-permute-done.4.refs_1_, bf16[64,2048]{1,0:T(8,128)(2,1)S(1)} %collective-permute-done.1.refs_2_, ...), custom_call_target="tpu_custom_call" | custom-call | flops 603979776 | bytes 4456448 | tf_op jit(solution)/shard_map/share/pallas_call | solution.py:69
  36.9 0.0 copy-start.3
  36.9 0.0 copy-start.4
  36.9 0.0 copy-start.5
  36.9 1.9 %collective-permute-start.6 = (bf16[64,2048]{1,0:T(8,128)(2,1)S(1)}, bf16[64,2048]{1,0:T(8,128)(2,1)S(1)}, u32[]{:S(2)}, u32[]{:S(2)}) collective-permute-start(bf16[64,2048]{1,0:T(8,128)(2,1)S(1)} %get-tuple-element.26), channel_id=1, source_target_pairs={{0,8},{4,12},{8,0},{12,4},{16,24},{20,28},{24,16},{28,20},{1,5},{5... | collective-permute-start | bytes 786440 | tf_op jit(solution)/shard_map/ppermute | solution.py:28
  38.8 0.2 collective-permute-start.8
  39.0 4.3 %collective-permute-done.12 = bf16[64,2048]{1,0:T(8,128)(2,1)S(1)} collective-permute-done((bf16[64,2048]{1,0:T(8,128)(2,1)S(1)}, bf16[64,2048]{1,0:T(8,128)(2,1)S(1)}, u32[]{:S(2)}, u32[]{:S(2)}) %collective-permute-start.12) | collective-permute-done | bytes 262176 | tf_op jit(solution)/shard_map/ppermute | solution.py:28
  43.3 0.8 %collective-permute-done.11 = bf16[64,2048]{1,0:T(8,128)(2,1)S(1)} collective-permute-done((bf16[64,2048]{1,0:T(8,128)(2,1)S(1)}, bf16[64,2048]{1,0:T(8,128)(2,1)S(1)}, u32[]{:S(2)}, u32[]{:S(2)}) %collective-permute-start.11) | collective-permute-done | bytes 262176 | tf_op jit(solution)/shard_map/ppermute | solution.py:28
  44.2 0.1 add_convert_fusion.1
  44.3 4.5 %collective-permute-start.13 = (bf16[64,2048]{1,0:T(8,128)(2,1)S(1)}, bf16[64,2048]{1,0:T(8,128)(2,1)S(1)}, u32[]{:S(2)}, u32[]{:S(2)}) collective-permute-start(bf16[64,2048]{1,0:T(8,128)(2,1)S(1)} %add_convert_fusion.1), channel_id=1, source_target_pairs={{0,16},{4,20},{8,24},{12,28},{16,0},{20,4},{24,8},{28,12},{1,17},{... | collective-permute-start | bytes 786440 | tf_op jit(solution)/shard_map/ppermute | solution.py:28
  48.8 0.0 collective-permute-done.6
  48.8 0.1 add_convert_fusion.4
  48.9 0.6 %collective-permute-start.7 = (bf16[64,2048]{1,0:T(8,128)(2,1)S(1)}, bf16[64,2048]{1,0:T(8,128)(2,1)S(1)}, u32[]{:S(2)}, u32[]{:S(2)}) collective-permute-start(bf16[64,2048]{1,0:T(8,128)(2,1)S(1)} %add_convert_fusion.4), channel_id=1, source_target_pairs={{0,4},{4,0},{8,12},{12,8},{16,20},{20,16},{24,28},{28,24},{1,9},{5... | collective-permute-start | bytes 786440 | tf_op jit(solution)/shard_map/ppermute | solution.py:28
  49.5 0.0 copy-done.3
  49.5 0.7 %fusion.2 = (s32[1]{0:T(128)}, s32[1]{0:T(128)}) fusion(s32[2]{0:T(128)S(1)} %copy-done.3, s32[]{:T(128)S(6)} %select_n.34, s32[]{:T(128)S(6)} %select_n.31), kind=kLoop, calls=%fused_computation.9 | loop fusion | bytes 24 | tf_op jit(solution)/shard_map/jit(dynamic_index_in_dim)/dynamic_slice | solution.py:96
  50.2 0.0 copy-done.4
  50.2 0.0 copy-done.5
  50.2 1.4 %fusion = (f32[64]{0:T(128)S(1)}, f32[64]{0:T(128)S(1)}) fusion(f32[64,2]{0,1:T(2,128)S(1)} %copy-done.4, s32[64,2]{0,1:T(2,128)S(1)} %copy-done.5, s32[]{:T(128)} %bitcast, s32[]{:T(128)} %bitcast.1), kind=kLoop, calls=%fused_computation.7 | loop fusion | flops 640 | bytes 1544 | tf_op jit(solution)/shard_map/reduce_sum | solution.py:97
  51.5 4.7 %collective-permute-done.8 = bf16[64,2048]{1,0:T(8,128)(2,1)S(1)} collective-permute-done((bf16[64,2048]{1,0:T(8,128)(2,1)S(1)}, bf16[64,2048]{1,0:T(8,128)(2,1)S(1)}, u32[]{:S(2)}, u32[]{:S(2)}) %collective-permute-start.8) | collective-permute-done | bytes 262176 | tf_op jit(solution)/shard_map/ppermute | solution.py:28
  56.2 0.0 collective-permute-done.13
  56.3 0.0 collective-permute-done.7
  56.3 0.9 %add_convert_fusion = bf16[64,2048]{1,0:T(8,128)(2,1)} fusion(bf16[64,2048]{1,0:T(8,128)(2,1)S(1)} %collective-permute-done.13, bf16[64,2048]{1,0:T(8,128)(2,1)S(1)} %collective-permute-done.8, bf16[64,2048]{1,0:T(8,128)(2,1)S(1)} %collective-permute-done.7, bf16[64,2048]{1,0:T(8,128)(2,1)S(1)} %get-tuple-element.22, f32[64]{0:T(128)S(1)} %get-tuple-element.34, ...), kind=kLoop, calls=%fused_computation | loop fusion | flops 1572864 | bytes 1311232 | tf_op jit(solution)/shard_map/convert_element_type | solution.py:122
  (2 shorter events, 0.0 us)
Async XLA Ops:
  0.0 26.9 %copy-start = (bf16[1,2,192,2048]{3,2,1,0:T(8,128)(2,1)S(1)}, bf16[1,2,192,2048]{3,2,1,0:T(8,128)(2,1)}, u32[]{:S(2)}) copy-start(bf16[1,2,192,2048]{3,2,1,0:T(8,128)(2,1)} %refs_3_.1) | copy-start | bytes 4718596
  0.0 26.9 %copy-start.1 = (bf16[1,192,2048]{2,1,0:T(8,128)(2,1)S(1)}, bf16[1,192,2048]{2,1,0:T(8,128)(2,1)}, u32[]{:S(2)}) copy-start(bf16[1,192,2048]{2,1,0:T(8,128)(2,1)} %refs_4_.3) | copy-start | bytes 2359300
  0.0 9.8 %collective-permute-start.4 = (bf16[64,2048]{1,0:T(8,128)(2,1)}, bf16[64,2048]{1,0:T(8,128)(2,1)S(1)}, u32[]{:S(2)}, u32[]{:S(2)}) collective-permute-start(bf16[64,2048]{1,0:T(8,128)(2,1)} %refs_0_), channel_id=1, source_target_pairs={{0,4},{4,0},{8,12},{12,8},{16,20},{20,16},{24,28},{28,24},{1,9},{5... | collective-permute-start | bytes 786440 | tf_op jit(solution)/shard_map/ppermute | solution.py:28
  2.9 10.1 %collective-permute-start.1 = (bf16[64,2048]{1,0:T(8,128)(2,1)}, bf16[64,2048]{1,0:T(8,128)(2,1)S(1)}, u32[]{:S(2)}, u32[]{:S(2)}) collective-permute-start(bf16[64,2048]{1,0:T(8,128)(2,1)} %refs_0_), channel_id=1, source_target_pairs={{0,8},{4,12},{8,0},{12,4},{16,24},{20,28},{24,16},{28,20},{1,5},{5... | collective-permute-start | bytes 786440 | tf_op jit(solution)/shard_map/ppermute | solution.py:28
  4.5 14.3 %collective-permute-start = (bf16[64,2048]{1,0:T(8,128)(2,1)}, bf16[64,2048]{1,0:T(8,128)(2,1)S(1)}, u32[]{:S(2)}, u32[]{:S(2)}) collective-permute-start(bf16[64,2048]{1,0:T(8,128)(2,1)} %refs_0_), channel_id=1, source_target_pairs={{0,16},{4,20},{8,24},{12,28},{16,0},{20,4},{24,8},{28,12},{1,17},{... | collective-permute-start | bytes 786440 | tf_op jit(solution)/shard_map/ppermute | solution.py:28
  9.8 9.2 %collective-permute-start.5 = (bf16[64,2048]{1,0:T(8,128)(2,1)S(1)}, bf16[64,2048]{1,0:T(8,128)(2,1)S(1)}, u32[]{:S(2)}, u32[]{:S(2)}) collective-permute-start(bf16[64,2048]{1,0:T(8,128)(2,1)S(1)} %collective-permute-done.4.refs_1_), channel_id=1, source_target_pairs={{0,8},{4,12},{8,0},{12,4},{16,24},{20,28},{24,16},{28,20},{1,5},{5... | collective-permute-start | bytes 786440 | tf_op jit(solution)/shard_map/ppermute | solution.py:28
  18.9 8.0 %collective-permute-start.2 = (bf16[64,2048]{1,0:T(8,128)(2,1)S(1)}, bf16[64,2048]{1,0:T(8,128)(2,1)S(1)}, u32[]{:S(2)}, u32[]{:S(2)}) collective-permute-start(bf16[64,2048]{1,0:T(8,128)(2,1)S(1)} %collective-permute-done.refs_0_), channel_id=1, source_target_pairs={{0,12},{4,8},{8,4},{12,0},{16,28},{20,24},{24,20},{28,16},{1,13},{... | collective-permute-start | bytes 786440 | tf_op jit(solution)/shard_map/ppermute | solution.py:28
  18.9 11.5 %collective-permute-start.10 = (bf16[64,2048]{1,0:T(8,128)(2,1)S(1)}, bf16[64,2048]{1,0:T(8,128)(2,1)S(1)}, u32[]{:S(2)}, u32[]{:S(2)}) collective-permute-start(bf16[64,2048]{1,0:T(8,128)(2,1)S(1)} %collective-permute-done.refs_0_), channel_id=1, source_target_pairs={{0,8},{4,12},{8,0},{12,4},{16,24},{20,28},{24,16},{28,20},{1,5},{5... | collective-permute-start | bytes 786440 | tf_op jit(solution)/shard_map/ppermute | solution.py:28
  20.9 10.8 %collective-permute-start.9 = (bf16[64,2048]{1,0:T(8,128)(2,1)S(1)}, bf16[64,2048]{1,0:T(8,128)(2,1)S(1)}, u32[]{:S(2)}, u32[]{:S(2)}) collective-permute-start(bf16[64,2048]{1,0:T(8,128)(2,1)S(1)} %collective-permute-done.refs_0_), channel_id=1, source_target_pairs={{0,4},{4,0},{8,12},{12,8},{16,20},{20,16},{24,28},{28,24},{1,9},{5... | collective-permute-start | bytes 786440 | tf_op jit(solution)/shard_map/ppermute | solution.py:28
  27.8 7.7 %copy-start.2 = (bf16[64,2048]{1,0:T(8,128)(2,1)S(1)}, bf16[64,2048]{1,0:T(8,128)(2,1)}, u32[]{:S(2)}) copy-start(bf16[64,2048]{1,0:T(8,128)(2,1)} %refs_0_) | copy-start | bytes 786436
  27.8 6.8 %collective-permute-start.3 = (bf16[64,2048]{1,0:T(8,128)(2,1)S(1)}, bf16[64,2048]{1,0:T(8,128)(2,1)S(1)}, u32[]{:S(2)}, u32[]{:S(2)}) collective-permute-start(bf16[64,2048]{1,0:T(8,128)(2,1)S(1)} %share.3), channel_id=1, source_target_pairs={{0,4},{4,0},{8,12},{12,8},{16,20},{20,16},{24,28},{28,24},{1,9},{5... | collective-permute-start | bytes 786440 | tf_op jit(solution)/shard_map/ppermute | solution.py:28
  34.6 8.7 %collective-permute-start.12 = (bf16[64,2048]{1,0:T(8,128)(2,1)S(1)}, bf16[64,2048]{1,0:T(8,128)(2,1)S(1)}, u32[]{:S(2)}, u32[]{:S(2)}) collective-permute-start(bf16[64,2048]{1,0:T(8,128)(2,1)S(1)} %add_convert_fusion.2), channel_id=1, source_target_pairs={{0,8},{4,12},{8,0},{12,4},{16,24},{20,28},{24,16},{28,20},{1,5},{5... | collective-permute-start | bytes 786440 | tf_op jit(solution)/shard_map/ppermute | solution.py:28
  34.9 9.2 %collective-permute-start.11 = (bf16[64,2048]{1,0:T(8,128)(2,1)S(1)}, bf16[64,2048]{1,0:T(8,128)(2,1)S(1)}, u32[]{:S(2)}, u32[]{:S(2)}) collective-permute-start(bf16[64,2048]{1,0:T(8,128)(2,1)S(1)} %get-tuple-element.31), channel_id=1, source_target_pairs={{0,4},{4,0},{8,12},{12,8},{16,20},{20,16},{24,28},{28,24},{1,9},{5... | collective-permute-start | bytes 786440 | tf_op jit(solution)/shard_map/ppermute | solution.py:28
  36.9 12.6 %copy-start.3 = (s32[2]{0:T(128)S(1)}, s32[2]{0:T(128)}, u32[]{:S(2)}) copy-start(s32[2]{0:T(128)} %param.9) | copy-start | bytes 28
  36.9 13.3 %copy-start.4 = (f32[64,2]{0,1:T(2,128)S(1)}, f32[64,2]{0,1:T(2,128)}, u32[]{:S(2)}) copy-start(f32[64,2]{0,1:T(2,128)} %param.7) | copy-start | bytes 1540
  36.9 13.3 %copy-start.5 = (s32[64,2]{0,1:T(2,128)S(1)}, s32[64,2]{0,1:T(2,128)}, u32[]{:S(2)}) copy-start(s32[64,2]{0,1:T(2,128)} %param.8) | copy-start | bytes 1540
  36.9 11.9 %collective-permute-start.6 = (bf16[64,2048]{1,0:T(8,128)(2,1)S(1)}, bf16[64,2048]{1,0:T(8,128)(2,1)S(1)}, u32[]{:S(2)}, u32[]{:S(2)}) collective-permute-start(bf16[64,2048]{1,0:T(8,128)(2,1)S(1)} %get-tuple-element.26), channel_id=1, source_target_pairs={{0,8},{4,12},{8,0},{12,4},{16,24},{20,28},{24,16},{28,20},{1,5},{5... | collective-permute-start | bytes 786440 | tf_op jit(solution)/shard_map/ppermute | solution.py:28
  38.8 17.5 %collective-permute-start.8 = (bf16[64,2048]{1,0:T(8,128)(2,1)S(1)}, bf16[64,2048]{1,0:T(8,128)(2,1)S(1)}, u32[]{:S(2)}, u32[]{:S(2)}) collective-permute-start(bf16[64,2048]{1,0:T(8,128)(2,1)S(1)} %get-tuple-element.28), channel_id=1, source_target_pairs={{0,8},{4,12},{8,0},{12,4},{16,24},{20,28},{24,16},{28,20},{1,5},{5... | collective-permute-start | bytes 786440 | tf_op jit(solution)/shard_map/ppermute | solution.py:28
  44.3 12.0 %collective-permute-start.13 = (bf16[64,2048]{1,0:T(8,128)(2,1)S(1)}, bf16[64,2048]{1,0:T(8,128)(2,1)S(1)}, u32[]{:S(2)}, u32[]{:S(2)}) collective-permute-start(bf16[64,2048]{1,0:T(8,128)(2,1)S(1)} %add_convert_fusion.1), channel_id=1, source_target_pairs={{0,16},{4,20},{8,24},{12,28},{16,0},{20,4},{24,8},{28,12},{1,17},{... | collective-permute-start | bytes 786440 | tf_op jit(solution)/shard_map/ppermute | solution.py:28
  48.9 7.4 %collective-permute-start.7 = (bf16[64,2048]{1,0:T(8,128)(2,1)S(1)}, bf16[64,2048]{1,0:T(8,128)(2,1)S(1)}, u32[]{:S(2)}, u32[]{:S(2)}) collective-permute-start(bf16[64,2048]{1,0:T(8,128)(2,1)S(1)} %add_convert_fusion.4), channel_id=1, source_target_pairs={{0,4},{4,0},{8,12},{12,8},{16,20},{20,16},{24,28},{28,24},{1,9},{5... | collective-permute-start | bytes 786440 | tf_op jit(solution)/shard_map/ppermute | solution.py:28

commit v6 on v5

--- a/solution.py
+++ b/solution.py
@@ -99,18 +99,18 @@
     ours_a = exchange(tokens, *first)
     ours_b = exchange(tokens, *second)
     ours_d = exchange(ours_a, *second)
-    theirs = after(theirs, touch(w_in, w_out), ours_b)
+    theirs = after(theirs, touch(w_in, w_out), ours_a, ours_b)
     theirs_d = exchange(theirs, *across)
     theirs = after(theirs, ours_d)
     theirs_a = exchange(theirs, *first)
     theirs_b = exchange(theirs, *second)
-    (away_d,) = share([theirs_d], w_in, w_out, load=8)
-    away, away_a, away_b = share([theirs, theirs_a, theirs_b], w_in, w_out)
+    (away_d,) = share([theirs_d], w_in, w_out, load=16)
+    away, away_a, away_b = share([theirs, theirs_a, theirs_b], w_in, w_out, load=4)
     back_d = exchange(away_d, *first)
     back_a = exchange(away_a, *first)
     back_b = exchange(summed(away_b, back_d), *second)
     away_sum = summed(away, back_a, back_b)
-    home = share([after(tokens, back_d), ours_a, ours_b, ours_d], w_in, w_out)
+    home = share([tokens, ours_a, ours_b, ours_d], w_in, w_out, load=8)
     home = [after(h, back_d) for h in home]
     home_d = exchange(home[3], *second)
     home_b = exchange(home[2], *second)

time: 57.8 us -> 57.8 us (level)
  no operation moved by 1% of the time
where the time goes in v6:
time: 57.8 us; the launch traced here: 57.1 us
  waiting for transfers between devices  28 us (48%)
  starting transfers between devices  20.4 us (35%)
  Pallas kernels  5.51 us (10%)
  other arithmetic  2.46 us (4%)
  local copies, waits for them, and re-layouts  0.7 us (1%)
    ppermute x14, waiting for transfers between devices, exchange(): return lax.ppermute(block, ('ep', 'dp'), route)  28 us
    ppermute x14, starting transfers between devices, exchange(): return lax.ppermute(block, ('ep', 'dp'), route)  20.4 us
    pallas_call x3, Pallas kernels, share(): pl.pallas_call(share_kernel, out_shape=[pltpu.VMEM((rows, width), jnp.bfl...  3.33 us
    pallas_call x1, Pallas kernels, touch(): pl.pallas_call(touch_kernel, out_shape=jax.ShapeDtypeStruct((8, 128), jnp...  2.19 us
    reduce_sum x1, other arithmetic, everywhere(): jnp.sum(jnp.where(expert_ids == named, gates, 0.0), axis=1, keepdims=True)  1.35 us
  transfers between devices with their start and end apart: 14, of which 10 were waited for; matrix products, arithmetic and copies ran while one was open for 4% of the time, Pallas kernels for 10%

profile of v6, /device:TPU:0, one launch (start us, length us, event | category | flops | bytes accessed | tf_op | source)
XLA Modules:
  0.0 57.1 jit_solution(9910449382404699285)
XLA Ops:
  0.0 2.9 %collective-permute-start = (bf16[64,2048]{1,0:T(8,128)(2,1)}, bf16[64,2048]{1,0:T(8,128)(2,1)S(1)}, u32[]{:S(2)}, u32[]{:S(2)}) collective-permute-start(bf16[64,2048]{1,0:T(8,128)(2,1)} %refs_0_.1), channel_id=1, source_target_pairs={{0,4},{4,0},{8,12},{12,8},{16,20},{20,16},{24,28},{28,24},{1,9},{5... | collective-permute-start | bytes 786440 | tf_op jit(solution)/shard_map/ppermute | solution.py:28
  2.9 1.6 %collective-permute-start.1 = (bf16[64,2048]{1,0:T(8,128)(2,1)}, bf16[64,2048]{1,0:T(8,128)(2,1)S(1)}, u32[]{:S(2)}, u32[]{:S(2)}) collective-permute-start(bf16[64,2048]{1,0:T(8,128)(2,1)} %refs_0_.1), channel_id=1, source_target_pairs={{0,8},{4,12},{8,0},{12,4},{16,24},{20,28},{24,16},{28,20},{1,5},{5... | collective-permute-start | bytes 786440 | tf_op jit(solution)/shard_map/ppermute | solution.py:28
  4.5 2.6 %collective-permute-start.3 = (bf16[64,2048]{1,0:T(8,128)(2,1)}, bf16[64,2048]{1,0:T(8,128)(2,1)S(1)}, u32[]{:S(2)}, u32[]{:S(2)}) collective-permute-start(bf16[64,2048]{1,0:T(8,128)(2,1)} %refs_0_.1), channel_id=1, source_target_pairs={{0,16},{4,20},{8,24},{12,28},{16,0},{20,4},{24,8},{28,12},{1,17},{... | collective-permute-start | bytes 786440 | tf_op jit(solution)/shard_map/ppermute | solution.py:28
  7.1 2.2 %touch.1 = bf16[8,128]{1,0:T(8,128)(2,1)} custom-call(bf16[1,2,192,2048]{3,2,1,0:T(8,128)(2,1)} %refs_3_.1, bf16[1,192,2048]{2,1,0:T(8,128)(2,1)} %refs_4_.3), custom_call_target="tpu_custom_call" | custom-call | tf_op jit(solution)/shard_map/touch/pallas_call | solution.py:40
  9.3 0.5 collective-permute-done.refs_1_
  9.8 1.6 %collective-permute-start.2 = (bf16[64,2048]{1,0:T(8,128)(2,1)S(1)}, bf16[64,2048]{1,0:T(8,128)(2,1)S(1)}, u32[]{:S(2)}, u32[]{:S(2)}) collective-permute-start(bf16[64,2048]{1,0:T(8,128)(2,1)S(1)} %collective-permute-done.refs_1_), channel_id=1, source_target_pairs={{0,8},{4,12},{8,0},{12,4},{16,24},{20,28},{24,16},{28,20},{1,5},{5... | collective-permute-start | bytes 786440 | tf_op jit(solution)/shard_map/ppermute | solution.py:28
  11.4 1.6 %collective-permute-done.1.refs_2_ = bf16[64,2048]{1,0:T(8,128)(2,1)S(1)} collective-permute-done((bf16[64,2048]{1,0:T(8,128)(2,1)}, bf16[64,2048]{1,0:T(8,128)(2,1)S(1)}, u32[]{:S(2)}, u32[]{:S(2)}) %collective-permute-start.1) | collective-permute-done | bytes 262176 | tf_op jit(solution)/shard_map/ppermute | solution.py:28
  13.0 5.9 %collective-permute-done.3.refs_0_ = bf16[64,2048]{1,0:T(8,128)(2,1)S(1)} collective-permute-done((bf16[64,2048]{1,0:T(8,128)(2,1)}, bf16[64,2048]{1,0:T(8,128)(2,1)S(1)}, u32[]{:S(2)}, u32[]{:S(2)}) %collective-permute-start.3) | collective-permute-done | bytes 262176 | tf_op jit(solution)/shard_map/ppermute | solution.py:28
  18.9 0.1 collective-permute-start.4
  18.9 0.0 collective-permute-done.2.refs_3_
  18.9 2.0 %collective-permute-start.10 = (bf16[64,2048]{1,0:T(8,128)(2,1)S(1)}, bf16[64,2048]{1,0:T(8,128)(2,1)S(1)}, u32[]{:S(2)}, u32[]{:S(2)}) collective-permute-start(bf16[64,2048]{1,0:T(8,128)(2,1)S(1)} %collective-permute-done.3.refs_0_), channel_id=1, source_target_pairs={{0,8},{4,12},{8,0},{12,4},{16,24},{20,28},{24,16},{28,20},{1,5},{5... | collective-permute-start | bytes 786440 | tf_op jit(solution)/shard_map/ppermute | solution.py:28
  20.9 1.5 %collective-permute-start.9 = (bf16[64,2048]{1,0:T(8,128)(2,1)S(1)}, bf16[64,2048]{1,0:T(8,128)(2,1)S(1)}, u32[]{:S(2)}, u32[]{:S(2)}) collective-permute-start(bf16[64,2048]{1,0:T(8,128)(2,1)S(1)} %collective-permute-done.3.refs_0_), channel_id=1, source_target_pairs={{0,4},{4,0},{8,12},{12,8},{16,20},{20,16},{24,28},{28,24},{1,9},{5... | collective-permute-start | bytes 786440 | tf_op jit(solution)/shard_map/ppermute | solution.py:28
  22.4 4.5 %collective-permute-done.4.refs_0_ = bf16[64,2048]{1,0:T(8,128)(2,1)S(1)} collective-permute-done((bf16[64,2048]{1,0:T(8,128)(2,1)S(1)}, bf16[64,2048]{1,0:T(8,128)(2,1)S(1)}, u32[]{:S(2)}, u32[]{:S(2)}) %collective-permute-start.4) | collective-permute-done | bytes 262176 | tf_op jit(solution)/shard_map/ppermute | solution.py:28
  26.9 0.0 copy-done
  26.9 0.0 copy-done.1
  26.9 0.9 %share.4 = bf16[64,2048]{1,0:T(8,128)(2,1)S(1)} custom-call(bf16[64,2048]{1,0:T(8,128)(2,1)S(1)} %collective-permute-done.4.refs_0_, bf16[1,2,192,2048]{3,2,1,0:T(8,128)(2,1)S(1)} %copy-done, bf16[1,192,2048]{2,1,0:T(8,128)(2,1)S(1)} %copy-done.1), custom_call_target="tpu_custom_call" | custom-call | flops 2415919104 | bytes 2883584 | tf_op jit(solution)/shard_map/share/pallas_call | solution.py:69
  27.8 0.0 copy-start.2
  27.8 0.1 collective-permute-start.5
  27.8 2.6 %collective-permute-done.10.refs_2_ = bf16[64,2048]{1,0:T(8,128)(2,1)S(1)} collective-permute-done((bf16[64,2048]{1,0:T(8,128)(2,1)S(1)}, bf16[64,2048]{1,0:T(8,128)(2,1)S(1)}, u32[]{:S(2)}, u32[]{:S(2)}) %collective-permute-start.10) | collective-permute-done | bytes 262176 | tf_op jit(solution)/shard_map/ppermute | solution.py:28
  30.4 1.3 %collective-permute-done.9.refs_1_ = bf16[64,2048]{1,0:T(8,128)(2,1)S(1)} collective-permute-done((bf16[64,2048]{1,0:T(8,128)(2,1)S(1)}, bf16[64,2048]{1,0:T(8,128)(2,1)S(1)}, u32[]{:S(2)}, u32[]{:S(2)}) %collective-permute-start.9) | collective-permute-done | bytes 262176 | tf_op jit(solution)/shard_map/ppermute | solution.py:28
  31.8 1.1 %share.5 = (bf16[64,2048]{1,0:T(8,128)(2,1)S(1)}, bf16[64,2048]{1,0:T(8,128)(2,1)S(1)}, bf16[64,2048]{1,0:T(8,128)(2,1)S(1)}) custom-call(bf16[64,2048]{1,0:T(8,128)(2,1)S(1)} %collective-permute-done.3.refs_0_, bf16[64,2048]{1,0:T(8,128)(2,1)S(1)} %collective-permute-done.9.refs_1_, bf16[64,2048]{1,0:T(8,128)(2,1)S(1)} %collective-permute-done.10.refs_2_, ...), custom_call_target="tpu_custom_call" | custom-call | flops 1811939328 | bytes 3932160 | tf_op jit(solution)/shard_map/share/pallas_call | solution.py:69
  32.9 1.7 %collective-permute-done.5 = bf16[64,2048]{1,0:T(8,128)(2,1)S(1)} collective-permute-done((bf16[64,2048]{1,0:T(8,128)(2,1)S(1)}, bf16[64,2048]{1,0:T(8,128)(2,1)S(1)}, u32[]{:S(2)}, u32[]{:S(2)}) %collective-permute-start.5) | collective-permute-done | bytes 262176 | tf_op jit(solution)/shard_map/ppermute | solution.py:28
  34.6 0.1 add_convert_fusion.2
  34.6 0.3 collective-permute-start.12
  34.9 0.6 %collective-permute-start.11 = (bf16[64,2048]{1,0:T(8,128)(2,1)S(1)}, bf16[64,2048]{1,0:T(8,128)(2,1)S(1)}, u32[]{:S(2)}, u32[]{:S(2)}) collective-permute-start(bf16[64,2048]{1,0:T(8,128)(2,1)S(1)} %get-tuple-element.29), channel_id=1, source_target_pairs={{0,4},{4,0},{8,12},{12,8},{16,20},{20,16},{24,28},{28,24},{1,9},{5... | collective-permute-start | bytes 786440 | tf_op jit(solution)/shard_map/ppermute | solution.py:28
  35.5 0.0 copy-done.2
  35.5 1.4 %share.3 = (bf16[64,2048]{1,0:T(8,128)(2,1)S(1)}, bf16[64,2048]{1,0:T(8,128)(2,1)S(1)}, bf16[64,2048]{1,0:T(8,128)(2,1)S(1)}, bf16[64,2048]{1,0:T(8,128)(2,1)S(1)}) custom-call(bf16[64,2048]{1,0:T(8,128)(2,1)S(1)} %copy-done.2, bf16[64,2048]{1,0:T(8,128)(2,1)S(1)} %collective-permute-done.refs_1_, bf16[64,2048]{1,0:T(8,128)(2,1)S(1)} %collective-permute-done.1.refs_2_, ...), custom_call_target="tpu_custom_call" | custom-call | flops 4831838208 | bytes 4456448 | tf_op jit(solution)/shard_map/share/pallas_call | solution.py:69
  36.9 0.0 copy-start.3
  36.9 0.0 copy-start.4
  36.9 0.0 copy-start.5
  36.9 1.9 %collective-permute-start.6 = (bf16[64,2048]{1,0:T(8,128)(2,1)S(1)}, bf16[64,2048]{1,0:T(8,128)(2,1)S(1)}, u32[]{:S(2)}, u32[]{:S(2)}) collective-permute-start(bf16[64,2048]{1,0:T(8,128)(2,1)S(1)} %get-tuple-element.24), channel_id=1, source_target_pairs={{0,8},{4,12},{8,0},{12,4},{16,24},{20,28},{24,16},{28,20},{1,5},{5... | collective-permute-start | bytes 786440 | tf_op jit(solution)/shard_map/ppermute | solution.py:28
  38.8 0.2 collective-permute-start.8
  39.0 4.3 %collective-permute-done.12 = bf16[64,2048]{1,0:T(8,128)(2,1)S(1)} collective-permute-done((bf16[64,2048]{1,0:T(8,128)(2,1)S(1)}, bf16[64,2048]{1,0:T(8,128)(2,1)S(1)}, u32[]{:S(2)}, u32[]{:S(2)}) %collective-permute-start.12) | collective-permute-done | bytes 262176 | tf_op jit(solution)/shard_map/ppermute | solution.py:28
  43.3 0.8 %collective-permute-done.11 = bf16[64,2048]{1,0:T(8,128)(2,1)S(1)} collective-permute-done((bf16[64,2048]{1,0:T(8,128)(2,1)S(1)}, bf16[64,2048]{1,0:T(8,128)(2,1)S(1)}, u32[]{:S(2)}, u32[]{:S(2)}) %collective-permute-start.11) | collective-permute-done | bytes 262176 | tf_op jit(solution)/shard_map/ppermute | solution.py:28
  44.2 0.1 add_convert_fusion.1
  44.3 4.5 %collective-permute-start.13 = (bf16[64,2048]{1,0:T(8,128)(2,1)S(1)}, bf16[64,2048]{1,0:T(8,128)(2,1)S(1)}, u32[]{:S(2)}, u32[]{:S(2)}) collective-permute-start(bf16[64,2048]{1,0:T(8,128)(2,1)S(1)} %add_convert_fusion.1), channel_id=1, source_target_pairs={{0,16},{4,20},{8,24},{12,28},{16,0},{20,4},{24,8},{28,12},{1,17},{... | collective-permute-start | bytes 786440 | tf_op jit(solution)/shard_map/ppermute | solution.py:28
  48.8 0.0 collective-permute-done.6
  48.8 0.1 add_convert_fusion.4
  48.9 0.6 %collective-permute-start.7 = (bf16[64,2048]{1,0:T(8,128)(2,1)S(1)}, bf16[64,2048]{1,0:T(8,128)(2,1)S(1)}, u32[]{:S(2)}, u32[]{:S(2)}) collective-permute-start(bf16[64,2048]{1,0:T(8,128)(2,1)S(1)} %add_convert_fusion.4), channel_id=1, source_target_pairs={{0,4},{4,0},{8,12},{12,8},{16,20},{20,16},{24,28},{28,24},{1,9},{5... | collective-permute-start | bytes 786440 | tf_op jit(solution)/shard_map/ppermute | solution.py:28
  49.5 0.0 copy-done.3
  49.5 0.7 %fusion.2 = (s32[1]{0:T(128)}, s32[1]{0:T(128)}) fusion(s32[2]{0:T(128)S(1)} %copy-done.3, s32[]{:T(128)S(6)} %select_n.34, s32[]{:T(128)S(6)} %select_n.31), kind=kLoop, calls=%fused_computation.9 | loop fusion | bytes 24 | tf_op jit(solution)/shard_map/jit(dynamic_index_in_dim)/dynamic_slice | solution.py:96
  50.2 0.0 copy-done.4
  50.2 0.0 copy-done.5
  50.2 1.4 %fusion = (f32[64]{0:T(128)S(1)}, f32[64]{0:T(128)S(1)}) fusion(f32[64,2]{0,1:T(2,128)S(1)} %copy-done.4, s32[64,2]{0,1:T(2,128)S(1)} %copy-done.5, s32[]{:T(128)} %bitcast, s32[]{:T(128)} %bitcast.1), kind=kLoop, calls=%fused_computation.7 | loop fusion | flops 640 | bytes 1544 | tf_op jit(solution)/shard_map/reduce_sum | solution.py:97
  51.5 4.7 %collective-permute-done.8 = bf16[64,2048]{1,0:T(8,128)(2,1)S(1)} collective-permute-done((bf16[64,2048]{1,0:T(8,128)(2,1)S(1)}, bf16[64,2048]{1,0:T(8,128)(2,1)S(1)}, u32[]{:S(2)}, u32[]{:S(2)}) %collective-permute-start.8) | collective-permute-done | bytes 262176 | tf_op jit(solution)/shard_map/ppermute | solution.py:28
  56.2 0.0 collective-permute-done.13
  56.3 0.0 collective-permute-done.7
  56.3 0.9 %add_convert_fusion = bf16[64,2048]{1,0:T(8,128)(2,1)} fusion(bf16[64,2048]{1,0:T(8,128)(2,1)S(1)} %collective-permute-done.13, bf16[64,2048]{1,0:T(8,128)(2,1)S(1)} %collective-permute-done.8, bf16[64,2048]{1,0:T(8,128)(2,1)S(1)} %collective-permute-done.7, bf16[64,2048]{1,0:T(8,128)(2,1)S(1)} %get-tuple-element.20, f32[64]{0:T(128)S(1)} %get-tuple-element.32, ...), kind=kLoop, calls=%fused_computation | loop fusion | flops 1572864 | bytes 1311232 | tf_op jit(solution)/shard_map/convert_element_type | solution.py:122
  (2 shorter events, 0.0 us)
Async XLA Ops:
  0.0 26.9 %copy-start = (bf16[1,2,192,2048]{3,2,1,0:T(8,128)(2,1)S(1)}, bf16[1,2,192,2048]{3,2,1,0:T(8,128)(2,1)}, u32[]{:S(2)}) copy-start(bf16[1,2,192,2048]{3,2,1,0:T(8,128)(2,1)} %refs_3_.1) | copy-start | bytes 4718596
  0.0 26.9 %copy-start.1 = (bf16[1,192,2048]{2,1,0:T(8,128)(2,1)S(1)}, bf16[1,192,2048]{2,1,0:T(8,128)(2,1)}, u32[]{:S(2)}) copy-start(bf16[1,192,2048]{2,1,0:T(8,128)(2,1)} %refs_4_.3) | copy-start | bytes 2359300
  0.0 9.8 %collective-permute-start = (bf16[64,2048]{1,0:T(8,128)(2,1)}, bf16[64,2048]{1,0:T(8,128)(2,1)S(1)}, u32[]{:S(2)}, u32[]{:S(2)}) collective-permute-start(bf16[64,2048]{1,0:T(8,128)(2,1)} %refs_0_.1), channel_id=1, source_target_pairs={{0,4},{4,0},{8,12},{12,8},{16,20},{20,16},{24,28},{28,24},{1,9},{5... | collective-permute-start | bytes 786440 | tf_op jit(solution)/shard_map/ppermute | solution.py:28
  2.9 10.1 %collective-permute-start.1 = (bf16[64,2048]{1,0:T(8,128)(2,1)}, bf16[64,2048]{1,0:T(8,128)(2,1)S(1)}, u32[]{:S(2)}, u32[]{:S(2)}) collective-permute-start(bf16[64,2048]{1,0:T(8,128)(2,1)} %refs_0_.1), channel_id=1, source_target_pairs={{0,8},{4,12},{8,0},{12,4},{16,24},{20,28},{24,16},{28,20},{1,5},{5... | collective-permute-start | bytes 786440 | tf_op jit(solution)/shard_map/ppermute | solution.py:28
  4.5 14.3 %collective-permute-start.3 = (bf16[64,2048]{1,0:T(8,128)(2,1)}, bf16[64,2048]{1,0:T(8,128)(2,1)S(1)}, u32[]{:S(2)}, u32[]{:S(2)}) collective-permute-start(bf16[64,2048]{1,0:T(8,128)(2,1)} %refs_0_.1), channel_id=1, source_target_pairs={{0,16},{4,20},{8,24},{12,28},{16,0},{20,4},{24,8},{28,12},{1,17},{... | collective-permute-start | bytes 786440 | tf_op jit(solution)/shard_map/ppermute | solution.py:28
  9.8 9.2 %collective-permute-start.2 = (bf16[64,2048]{1,0:T(8,128)(2,1)S(1)}, bf16[64,2048]{1,0:T(8,128)(2,1)S(1)}, u32[]{:S(2)}, u32[]{:S(2)}) collective-permute-start(bf16[64,2048]{1,0:T(8,128)(2,1)S(1)} %collective-permute-done.refs_1_), channel_id=1, source_target_pairs={{0,8},{4,12},{8,0},{12,4},{16,24},{20,28},{24,16},{28,20},{1,5},{5... | collective-permute-start | bytes 786440 | tf_op jit(solution)/shard_map/ppermute | solution.py:28
  18.9 8.0 %collective-permute-start.4 = (bf16[64,2048]{1,0:T(8,128)(2,1)S(1)}, bf16[64,2048]{1,0:T(8,128)(2,1)S(1)}, u32[]{:S(2)}, u32[]{:S(2)}) collective-permute-start(bf16[64,2048]{1,0:T(8,128)(2,1)S(1)} %collective-permute-done.3.refs_0_), channel_id=1, source_target_pairs={{0,12},{4,8},{8,4},{12,0},{16,28},{20,24},{24,20},{28,16},{1,13},{... | collective-permute-start | bytes 786440 | tf_op jit(solution)/shard_map/ppermute | solution.py:28
  18.9 11.5 %collective-permute-start.10 = (bf16[64,2048]{1,0:T(8,128)(2,1)S(1)}, bf16[64,2048]{1,0:T(8,128)(2,1)S(1)}, u32[]{:S(2)}, u32[]{:S(2)}) collective-permute-start(bf16[64,2048]{1,0:T(8,128)(2,1)S(1)} %collective-permute-done.3.refs_0_), channel_id=1, source_target_pairs={{0,8},{4,12},{8,0},{12,4},{16,24},{20,28},{24,16},{28,20},{1,5},{5... | collective-permute-start | bytes 786440 | tf_op jit(solution)/shard_map/ppermute | solution.py:28
  20.9 10.8 %collective-permute-start.9 = (bf16[64,2048]{1,0:T(8,128)(2,1)S(1)}, bf16[64,2048]{1,0:T(8,128)(2,1)S(1)}, u32[]{:S(2)}, u32[]{:S(2)}) collective-permute-start(bf16[64,2048]{1,0:T(8,128)(2,1)S(1)} %collective-permute-done.3.refs_0_), channel_id=1, source_target_pairs={{0,4},{4,0},{8,12},{12,8},{16,20},{20,16},{24,28},{28,24},{1,9},{5... | collective-permute-start | bytes 786440 | tf_op jit(solution)/shard_map/ppermute | solution.py:28
  27.8 7.7 %copy-start.2 = (bf16[64,2048]{1,0:T(8,128)(2,1)S(1)}, bf16[64,2048]{1,0:T(8,128)(2,1)}, u32[]{:S(2)}) copy-start(bf16[64,2048]{1,0:T(8,128)(2,1)} %refs_0_.1) | copy-start | bytes 786436
  27.8 6.8 %collective-permute-start.5 = (bf16[64,2048]{1,0:T(8,128)(2,1)S(1)}, bf16[64,2048]{1,0:T(8,128)(2,1)S(1)}, u32[]{:S(2)}, u32[]{:S(2)}) collective-permute-start(bf16[64,2048]{1,0:T(8,128)(2,1)S(1)} %share.4), channel_id=1, source_target_pairs={{0,4},{4,0},{8,12},{12,8},{16,20},{20,16},{24,28},{28,24},{1,9},{5... | collective-permute-start | bytes 786440 | tf_op jit(solution)/shard_map/ppermute | solution.py:28
  34.6 8.7 %collective-permute-start.12 = (bf16[64,2048]{1,0:T(8,128)(2,1)S(1)}, bf16[64,2048]{1,0:T(8,128)(2,1)S(1)}, u32[]{:S(2)}, u32[]{:S(2)}) collective-permute-start(bf16[64,2048]{1,0:T(8,128)(2,1)S(1)} %add_convert_fusion.2), channel_id=1, source_target_pairs={{0,8},{4,12},{8,0},{12,4},{16,24},{20,28},{24,16},{28,20},{1,5},{5... | collective-permute-start | bytes 786440 | tf_op jit(solution)/shard_map/ppermute | solution.py:28
  34.9 9.2 %collective-permute-start.11 = (bf16[64,2048]{1,0:T(8,128)(2,1)S(1)}, bf16[64,2048]{1,0:T(8,128)(2,1)S(1)}, u32[]{:S(2)}, u32[]{:S(2)}) collective-permute-start(bf16[64,2048]{1,0:T(8,128)(2,1)S(1)} %get-tuple-element.29), channel_id=1, source_target_pairs={{0,4},{4,0},{8,12},{12,8},{16,20},{20,16},{24,28},{28,24},{1,9},{5... | collective-permute-start | bytes 786440 | tf_op jit(solution)/shard_map/ppermute | solution.py:28
  36.9 12.6 %copy-start.3 = (s32[2]{0:T(128)S(1)}, s32[2]{0:T(128)}, u32[]{:S(2)}) copy-start(s32[2]{0:T(128)} %param.9) | copy-start | bytes 28
  36.9 13.3 %copy-start.4 = (f32[64,2]{0,1:T(2,128)S(1)}, f32[64,2]{0,1:T(2,128)}, u32[]{:S(2)}) copy-start(f32[64,2]{0,1:T(2,128)} %param.7) | copy-start | bytes 1540
  36.9 13.3 %copy-start.5 = (s32[64,2]{0,1:T(2,128)S(1)}, s32[64,2]{0,1:T(2,128)}, u32[]{:S(2)}) copy-start(s32[64,2]{0,1:T(2,128)} %param.8) | copy-start | bytes 1540
  36.9 11.9 %collective-permute-start.6 = (bf16[64,2048]{1,0:T(8,128)(2,1)S(1)}, bf16[64,2048]{1,0:T(8,128)(2,1)S(1)}, u32[]{:S(2)}, u32[]{:S(2)}) collective-permute-start(bf16[64,2048]{1,0:T(8,128)(2,1)S(1)} %get-tuple-element.24), channel_id=1, source_target_pairs={{0,8},{4,12},{8,0},{12,4},{16,24},{20,28},{24,16},{28,20},{1,5},{5... | collective-permute-start | bytes 786440 | tf_op jit(solution)/shard_map/ppermute | solution.py:28
  38.8 17.5 %collective-permute-start.8 = (bf16[64,2048]{1,0:T(8,128)(2,1)S(1)}, bf16[64,2048]{1,0:T(8,128)(2,1)S(1)}, u32[]{:S(2)}, u32[]{:S(2)}) collective-permute-start(bf16[64,2048]{1,0:T(8,128)(2,1)S(1)} %get-tuple-element.26), channel_id=1, source_target_pairs={{0,8},{4,12},{8,0},{12,4},{16,24},{20,28},{24,16},{28,20},{1,5},{5... | collective-permute-start | bytes 786440 | tf_op jit(solution)/shard_map/ppermute | solution.py:28
  44.3 12.0 %collective-permute-start.13 = (bf16[64,2048]{1,0:T(8,128)(2,1)S(1)}, bf16[64,2048]{1,0:T(8,128)(2,1)S(1)}, u32[]{:S(2)}, u32[]{:S(2)}) collective-permute-start(bf16[64,2048]{1,0:T(8,128)(2,1)S(1)} %add_convert_fusion.1), channel_id=1, source_target_pairs={{0,16},{4,20},{8,24},{12,28},{16,0},{20,4},{24,8},{28,12},{1,17},{... | collective-permute-start | bytes 786440 | tf_op jit(solution)/shard_map/ppermute | solution.py:28
  48.9 7.4 %collective-permute-start.7 = (bf16[64,2048]{1,0:T(8,128)(2,1)S(1)}, bf16[64,2048]{1,0:T(8,128)(2,1)S(1)}, u32[]{:S(2)}, u32[]{:S(2)}) collective-permute-start(bf16[64,2048]{1,0:T(8,128)(2,1)S(1)} %add_convert_fusion.4), channel_id=1, source_target_pairs={{0,4},{4,0},{8,12},{12,8},{16,20},{20,16},{24,28},{28,24},{1,9},{5... | collective-permute-start | bytes 786440 | tf_op jit(solution)/shard_map/ppermute | solution.py:28

commit v7 on v6

--- a/solution.py
+++ b/solution.py
@@ -112,8 +112,8 @@
     away_sum = summed(away, back_a, back_b)
     home = share([tokens, ours_a, ours_b, ours_d], w_in, w_out, load=8)
     home = [after(h, back_d) for h in home]
-    home_d = exchange(home[3], *second)
-    home_b = exchange(home[2], *second)
+    both = exchange(jnp.concatenate([home[3], home[2]]), *second)
+    home_d, home_b = jnp.split(both, 2)
     home_a = exchange(summed(home[1], home_d), *first)
     other = exchange(away_sum, *group)
     own = summed(home[0], home_a, home_b)

time: 57.8 us -> 63.9 us (1.11)
  the two profiles are of different devices: /device:TPU:0 before, /device:TPU:4 now
where the time goes in v7:
time: 63.9 us; the launch traced here: 63.7 us
  waiting for transfers between devices  40.6 us (64%)
  starting transfers between devices  14.5 us (23%)
  Pallas kernels  5.51 us (9%)
  other arithmetic  2.35 us (4%)
    ppermute x13, waiting for transfers between devices, exchange(): return lax.ppermute(block, ('ep', 'dp'), route)  40.6 us
    ppermute x13, starting transfers between devices, exchange(): return lax.ppermute(block, ('ep', 'dp'), route)  14.5 us
    pallas_call x3, Pallas kernels, share(): pl.pallas_call(share_kernel, out_shape=[pltpu.VMEM((rows, width), jnp.bfl...  3.33 us
    pallas_call x1, Pallas kernels, touch(): pl.pallas_call(touch_kernel, out_shape=jax.ShapeDtypeStruct((8, 128), jnp...  2.19 us
  transfers between devices with their start and end apart: 13, of which 10 were waited for; matrix products, arithmetic and copies ran while one was open for 3% of the time, Pallas kernels for 9%

profile of v7, /device:TPU:4, one launch (start us, length us, event | category | flops | bytes accessed | tf_op | source)
XLA Modules:
  0.0 63.7 jit_solution(12880392719198979151)
XLA Ops:
  0.0 0.0 copy-start
  0.0 0.0 copy-start.1
  0.0 1.5 %collective-permute-start = (bf16[64,2048]{1,0:T(8,128)(2,1)}, bf16[64,2048]{1,0:T(8,128)(2,1)S(1)}, u32[]{:S(2)}, u32[]{:S(2)}) collective-permute-start(bf16[64,2048]{1,0:T(8,128)(2,1)} %refs_0_.1), channel_id=1, source_target_pairs={{0,4},{4,0},{8,12},{12,8},{16,20},{20,16},{24,28},{28,24},{1,9},{5... | collective-permute-start | bytes 786440 | tf_op jit(solution)/shard_map/ppermute | solution.py:28
  1.5 1.6 %collective-permute-start.1 = (bf16[64,2048]{1,0:T(8,128)(2,1)}, bf16[64,2048]{1,0:T(8,128)(2,1)S(1)}, u32[]{:S(2)}, u32[]{:S(2)}) collective-permute-start(bf16[64,2048]{1,0:T(8,128)(2,1)} %refs_0_.1), channel_id=1, source_target_pairs={{0,8},{4,12},{8,0},{12,4},{16,24},{20,28},{24,16},{28,20},{1,5},{5... | collective-permute-start | bytes 786440 | tf_op jit(solution)/shard_map/ppermute | solution.py:28
  3.1 2.6 %collective-permute-start.3 = (bf16[64,2048]{1,0:T(8,128)(2,1)}, bf16[64,2048]{1,0:T(8,128)(2,1)S(1)}, u32[]{:S(2)}, u32[]{:S(2)}) collective-permute-start(bf16[64,2048]{1,0:T(8,128)(2,1)} %refs_0_.1), channel_id=1, source_target_pairs={{0,16},{4,20},{8,24},{12,28},{16,0},{20,4},{24,8},{28,12},{1,17},{... | collective-permute-start | bytes 786440 | tf_op jit(solution)/shard_map/ppermute | solution.py:28
  5.7 2.2 %touch.1 = bf16[8,128]{1,0:T(8,128)(2,1)} custom-call(bf16[1,2,192,2048]{3,2,1,0:T(8,128)(2,1)} %refs_3_.1, bf16[1,192,2048]{2,1,0:T(8,128)(2,1)} %refs_4_.3), custom_call_target="tpu_custom_call" | custom-call | tf_op jit(solution)/shard_map/touch/pallas_call | solution.py:40
  7.8 0.0 copy-start.2
  7.9 1.4 %collective-permute-done.refs_1_ = bf16[64,2048]{1,0:T(8,128)(2,1)S(1)} collective-permute-done((bf16[64,2048]{1,0:T(8,128)(2,1)}, bf16[64,2048]{1,0:T(8,128)(2,1)S(1)}, u32[]{:S(2)}, u32[]{:S(2)}) %collective-permute-start) | collective-permute-done | bytes 262176 | tf_op jit(solution)/shard_map/ppermute | solution.py:28
  9.2 0.8 %collective-permute-start.2 = (bf16[64,2048]{1,0:T(8,128)(2,1)S(1)}, bf16[64,2048]{1,0:T(8,128)(2,1)S(1)}, u32[]{:S(2)}, u32[]{:S(2)}) collective-permute-start(bf16[64,2048]{1,0:T(8,128)(2,1)S(1)} %collective-permute-done.refs_1_), channel_id=1, source_target_pairs={{0,8},{4,12},{8,0},{12,4},{16,24},{20,28},{24,16},{28,20},{1,5},{5... | collective-permute-start | bytes 786440 | tf_op jit(solution)/shard_map/ppermute | solution.py:28
  10.0 1.9 %collective-permute-done.1.refs_2_ = bf16[64,2048]{1,0:T(8,128)(2,1)S(1)} collective-permute-done((bf16[64,2048]{1,0:T(8,128)(2,1)}, bf16[64,2048]{1,0:T(8,128)(2,1)S(1)}, u32[]{:S(2)}, u32[]{:S(2)}) %collective-permute-start.1) | collective-permute-done | bytes 262176 | tf_op jit(solution)/shard_map/ppermute | solution.py:28
  11.9 5.5 %collective-permute-done.3.refs_0_ = bf16[64,2048]{1,0:T(8,128)(2,1)S(1)} collective-permute-done((bf16[64,2048]{1,0:T(8,128)(2,1)}, bf16[64,2048]{1,0:T(8,128)(2,1)S(1)}, u32[]{:S(2)}, u32[]{:S(2)}) %collective-permute-start.3) | collective-permute-done | bytes 262176 | tf_op jit(solution)/shard_map/ppermute | solution.py:28
  17.4 0.1 collective-permute-start.4
  17.5 0.0 collective-permute-done.2.refs_3_
  17.5 1.2 %collective-permute-start.8 = (bf16[64,2048]{1,0:T(8,128)(2,1)S(1)}, bf16[64,2048]{1,0:T(8,128)(2,1)S(1)}, u32[]{:S(2)}, u32[]{:S(2)}) collective-permute-start(bf16[64,2048]{1,0:T(8,128)(2,1)S(1)} %collective-permute-done.3.refs_0_), channel_id=1, source_target_pairs={{0,4},{4,0},{8,12},{12,8},{16,20},{20,16},{24,28},{28,24},{1,9},{5... | collective-permute-start | bytes 786440 | tf_op jit(solution)/shard_map/ppermute | solution.py:28
  18.7 2.2 %collective-permute-start.9 = (bf16[64,2048]{1,0:T(8,128)(2,1)S(1)}, bf16[64,2048]{1,0:T(8,128)(2,1)S(1)}, u32[]{:S(2)}, u32[]{:S(2)}) collective-permute-start(bf16[64,2048]{1,0:T(8,128)(2,1)S(1)} %collective-permute-done.3.refs_0_), channel_id=1, source_target_pairs={{0,8},{4,12},{8,0},{12,4},{16,24},{20,28},{24,16},{28,20},{1,5},{5... | collective-permute-start | bytes 786440 | tf_op jit(solution)/shard_map/ppermute | solution.py:28
  20.9 6.6 %collective-permute-done.4.refs_0_ = bf16[64,2048]{1,0:T(8,128)(2,1)S(1)} collective-permute-done((bf16[64,2048]{1,0:T(8,128)(2,1)S(1)}, bf16[64,2048]{1,0:T(8,128)(2,1)S(1)}, u32[]{:S(2)}, u32[]{:S(2)}) %collective-permute-start.4) | collective-permute-done | bytes 262176 | tf_op jit(solution)/shard_map/ppermute | solution.py:28
  27.6 0.0 copy-done
  27.6 0.0 copy-done.1
  27.6 0.9 %share.4 = bf16[64,2048]{1,0:T(8,128)(2,1)S(1)} custom-call(bf16[64,2048]{1,0:T(8,128)(2,1)S(1)} %collective-permute-done.4.refs_0_, bf16[1,2,192,2048]{3,2,1,0:T(8,128)(2,1)S(1)} %copy-done, bf16[1,192,2048]{2,1,0:T(8,128)(2,1)S(1)} %copy-done.1), custom_call_target="tpu_custom_call" | custom-call | flops 2415919104 | bytes 2883584 | tf_op jit(solution)/shard_map/share/pallas_call | solution.py:69
  28.4 0.6 collective-permute-start.5
  29.1 0.0 copy-done.2
  29.1 1.4 %share.3 = (bf16[64,2048]{1,0:T(8,128)(2,1)S(1)}, bf16[64,2048]{1,0:T(8,128)(2,1)S(1)}, bf16[64,2048]{1,0:T(8,128)(2,1)S(1)}, bf16[64,2048]{1,0:T(8,128)(2,1)S(1)}) custom-call(bf16[64,2048]{1,0:T(8,128)(2,1)S(1)} %copy-done.2, bf16[64,2048]{1,0:T(8,128)(2,1)S(1)} %collective-permute-done.refs_1_, bf16[64,2048]{1,0:T(8,128)(2,1)S(1)} %collective-permute-done.1.refs_2_, ...), custom_call_target="tpu_custom_call" | custom-call | flops 4831838208 | bytes 4456448 | tf_op jit(solution)/shard_map/share/pallas_call | solution.py:69
  30.4 0.0 collective-permute-done.8.refs_1_
  30.5 0.9 %collective-permute-done.9.refs_2_ = bf16[64,2048]{1,0:T(8,128)(2,1)S(1)} collective-permute-done((bf16[64,2048]{1,0:T(8,128)(2,1)S(1)}, bf16[64,2048]{1,0:T(8,128)(2,1)S(1)}, u32[]{:S(2)}, u32[]{:S(2)}) %collective-permute-start.9) | collective-permute-done | bytes 262176 | tf_op jit(solution)/shard_map/ppermute | solution.py:28
  31.4 1.1 %share.5 = (bf16[64,2048]{1,0:T(8,128)(2,1)S(1)}, bf16[64,2048]{1,0:T(8,128)(2,1)S(1)}, bf16[64,2048]{1,0:T(8,128)(2,1)S(1)}) custom-call(bf16[64,2048]{1,0:T(8,128)(2,1)S(1)} %collective-permute-done.3.refs_0_, bf16[64,2048]{1,0:T(8,128)(2,1)S(1)} %collective-permute-done.8.refs_1_, bf16[64,2048]{1,0:T(8,128)(2,1)S(1)} %collective-permute-done.9.refs_2_, ...), custom_call_target="tpu_custom_call" | custom-call | flops 1811939328 | bytes 3932160 | tf_op jit(solution)/shard_map/share/pallas_call | solution.py:69
  32.5 3.8 %collective-permute-done.5 = bf16[64,2048]{1,0:T(8,128)(2,1)S(1)} collective-permute-done((bf16[64,2048]{1,0:T(8,128)(2,1)S(1)}, bf16[64,2048]{1,0:T(8,128)(2,1)S(1)}, u32[]{:S(2)}, u32[]{:S(2)}) %collective-permute-start.5) | collective-permute-done | bytes 262176 | tf_op jit(solution)/shard_map/ppermute | solution.py:28
  36.3 0.1 add_convert_fusion.2
  36.4 0.0 copy-start.3
  36.4 0.0 copy-start.4
  36.4 0.0 copy-start.5
  36.4 0.1 collective-permute-start.11
  36.5 0.1 collective-permute-start.10
  36.7 2.0 %collective-permute-start.6 = (bf16[128,2048]{1,0:T(8,128)(2,1)S(1)}, bf16[128,2048]{1,0:T(8,128)(2,1)S(1)}, u32[]{:S(2)}, u32[]{:S(2)}) collective-permute-start(bf16[128,2048]{1,0:T(8,128)(2,1)S(1)} %pad_maximum_fusion), channel_id=1, source_target_pairs={{0,8},{4,12},{8,0},{12,4},{16,24},{20,28},{24,16},{28,20},{1,5},{5... | collective-permute-start | bytes 1572872 | tf_op jit(solution)/shard_map/ppermute | solution.py:28
  38.7 4.2 %collective-permute-done.11 = bf16[64,2048]{1,0:T(8,128)(2,1)S(1)} collective-permute-done((bf16[64,2048]{1,0:T(8,128)(2,1)S(1)}, bf16[64,2048]{1,0:T(8,128)(2,1)S(1)}, u32[]{:S(2)}, u32[]{:S(2)}) %collective-permute-start.11) | collective-permute-done | bytes 262176 | tf_op jit(solution)/shard_map/ppermute | solution.py:28
  42.9 2.9 %collective-permute-done.10 = bf16[64,2048]{1,0:T(8,128)(2,1)S(1)} collective-permute-done((bf16[64,2048]{1,0:T(8,128)(2,1)S(1)}, bf16[64,2048]{1,0:T(8,128)(2,1)S(1)}, u32[]{:S(2)}, u32[]{:S(2)}) %collective-permute-start.10) | collective-permute-done | bytes 262176 | tf_op jit(solution)/shard_map/ppermute | solution.py:28
  45.8 0.1 add_convert_fusion.1
  45.9 1.6 %collective-permute-start.12 = (bf16[64,2048]{1,0:T(8,128)(2,1)S(1)}, bf16[64,2048]{1,0:T(8,128)(2,1)S(1)}, u32[]{:S(2)}, u32[]{:S(2)}) collective-permute-start(bf16[64,2048]{1,0:T(8,128)(2,1)S(1)} %add_convert_fusion.1), channel_id=1, source_target_pairs={{0,16},{4,20},{8,24},{12,28},{16,0},{20,4},{24,8},{28,12},{1,17},{... | collective-permute-start | bytes 786440 | tf_op jit(solution)/shard_map/ppermute | solution.py:28
  47.5 8.8 %collective-permute-done.6 = bf16[128,2048]{1,0:T(8,128)(2,1)S(1)} collective-permute-done((bf16[128,2048]{1,0:T(8,128)(2,1)S(1)}, bf16[128,2048]{1,0:T(8,128)(2,1)S(1)}, u32[]{:S(2)}, u32[]{:S(2)}) %collective-permute-start.6) | collective-permute-done | bytes 524320 | tf_op jit(solution)/shard_map/ppermute | solution.py:28
  56.4 0.1 add_convert_fusion.4
  56.4 0.1 collective-permute-start.7
  56.6 0.0 copy-done.3
  56.6 0.6 fusion.2
  57.2 0.0 copy-done.4
  57.2 0.0 copy-done.5
  57.2 1.2 %fusion = (f32[64]{0:T(128)S(1)}, f32[64]{0:T(128)S(1)}) fusion(f32[64,2]{0,1:T(2,128)S(1)} %copy-done.4, s32[64,2]{0,1:T(2,128)S(1)} %copy-done.5, s32[]{:T(128)} %bitcast, s32[]{:T(128)} %bitcast.1), kind=kLoop, calls=%fused_computation.8 | loop fusion | flops 640 | bytes 1544 | tf_op jit(solution)/shard_map/reduce_sum | solution.py:97
  58.4 0.0 collective-permute-done.12
  58.4 4.5 %collective-permute-done.7 = bf16[64,2048]{1,0:T(8,128)(2,1)S(1)} collective-permute-done((bf16[64,2048]{1,0:T(8,128)(2,1)S(1)}, bf16[64,2048]{1,0:T(8,128)(2,1)S(1)}, u32[]{:S(2)}, u32[]{:S(2)}) %collective-permute-start.7) | collective-permute-done | bytes 262176 | tf_op jit(solution)/shard_map/ppermute | solution.py:28
  62.9 0.9 %add_convert_fusion = bf16[64,2048]{1,0:T(8,128)(2,1)} fusion(bf16[64,2048]{1,0:T(8,128)(2,1)S(1)} %collective-permute-done.12, bf16[64,2048]{1,0:T(8,128)(2,1)S(1)} %collective-permute-done.7, bf16[64,2048]{1,0:T(8,128)(2,1)S(1)} %get-tuple-element.20, bf16[128,2048]{1,0:T(8,128)(2,1)S(1)} %collective-permute-done.6, f32[64]{0:T(128)S(1)} %get-tuple-element.32, ...), kind=kLoop, calls=%fused_computation.1 | loop fusion | flops 1572864 | bytes 1311232 | tf_op jit(solution)/shard_map/convert_element_type | solution.py:122
  (1 shorter events, 0.0 us)
Async XLA Ops:
  0.0 27.6 %copy-start = (bf16[1,2,192,2048]{3,2,1,0:T(8,128)(2,1)S(1)}, bf16[1,2,192,2048]{3,2,1,0:T(8,128)(2,1)}, u32[]{:S(2)}) copy-start(bf16[1,2,192,2048]{3,2,1,0:T(8,128)(2,1)} %refs_3_.1) | copy-start | bytes 4718596
  0.0 27.6 %copy-start.1 = (bf16[1,192,2048]{2,1,0:T(8,128)(2,1)S(1)}, bf16[1,192,2048]{2,1,0:T(8,128)(2,1)}, u32[]{:S(2)}) copy-start(bf16[1,192,2048]{2,1,0:T(8,128)(2,1)} %refs_4_.3) | copy-start | bytes 2359300
  0.0 9.2 %collective-permute-start = (bf16[64,2048]{1,0:T(8,128)(2,1)}, bf16[64,2048]{1,0:T(8,128)(2,1)S(1)}, u32[]{:S(2)}, u32[]{:S(2)}) collective-permute-start(bf16[64,2048]{1,0:T(8,128)(2,1)} %refs_0_.1), channel_id=1, source_target_pairs={{0,4},{4,0},{8,12},{12,8},{16,20},{20,16},{24,28},{28,24},{1,9},{5... | collective-permute-start | bytes 786440 | tf_op jit(solution)/shard_map/ppermute | solution.py:28
  1.5 10.4 %collective-permute-start.1 = (bf16[64,2048]{1,0:T(8,128)(2,1)}, bf16[64,2048]{1,0:T(8,128)(2,1)S(1)}, u32[]{:S(2)}, u32[]{:S(2)}) collective-permute-start(bf16[64,2048]{1,0:T(8,128)(2,1)} %refs_0_.1), channel_id=1, source_target_pairs={{0,8},{4,12},{8,0},{12,4},{16,24},{20,28},{24,16},{28,20},{1,5},{5... | collective-permute-start | bytes 786440 | tf_op jit(solution)/shard_map/ppermute | solution.py:28
  3.1 14.3 %collective-permute-start.3 = (bf16[64,2048]{1,0:T(8,128)(2,1)}, bf16[64,2048]{1,0:T(8,128)(2,1)S(1)}, u32[]{:S(2)}, u32[]{:S(2)}) collective-permute-start(bf16[64,2048]{1,0:T(8,128)(2,1)} %refs_0_.1), channel_id=1, source_target_pairs={{0,16},{4,20},{8,24},{12,28},{16,0},{20,4},{24,8},{28,12},{1,17},{... | collective-permute-start | bytes 786440 | tf_op jit(solution)/shard_map/ppermute | solution.py:28
  7.8 21.2 %copy-start.2 = (bf16[64,2048]{1,0:T(8,128)(2,1)S(1)}, bf16[64,2048]{1,0:T(8,128)(2,1)}, u32[]{:S(2)}) copy-start(bf16[64,2048]{1,0:T(8,128)(2,1)} %refs_0_.1) | copy-start | bytes 786436
  9.2 8.3 %collective-permute-start.2 = (bf16[64,2048]{1,0:T(8,128)(2,1)S(1)}, bf16[64,2048]{1,0:T(8,128)(2,1)S(1)}, u32[]{:S(2)}, u32[]{:S(2)}) collective-permute-start(bf16[64,2048]{1,0:T(8,128)(2,1)S(1)} %collective-permute-done.refs_1_), channel_id=1, source_target_pairs={{0,8},{4,12},{8,0},{12,4},{16,24},{20,28},{24,16},{28,20},{1,5},{5... | collective-permute-start | bytes 786440 | tf_op jit(solution)/shard_map/ppermute | solution.py:28
  17.4 10.1 %collective-permute-start.4 = (bf16[64,2048]{1,0:T(8,128)(2,1)S(1)}, bf16[64,2048]{1,0:T(8,128)(2,1)S(1)}, u32[]{:S(2)}, u32[]{:S(2)}) collective-permute-start(bf16[64,2048]{1,0:T(8,128)(2,1)S(1)} %collective-permute-done.3.refs_0_), channel_id=1, source_target_pairs={{0,12},{4,8},{8,4},{12,0},{16,28},{20,24},{24,20},{28,16},{1,13},{... | collective-permute-start | bytes 786440 | tf_op jit(solution)/shard_map/ppermute | solution.py:28
  17.5 12.9 %collective-permute-start.8 = (bf16[64,2048]{1,0:T(8,128)(2,1)S(1)}, bf16[64,2048]{1,0:T(8,128)(2,1)S(1)}, u32[]{:S(2)}, u32[]{:S(2)}) collective-permute-start(bf16[64,2048]{1,0:T(8,128)(2,1)S(1)} %collective-permute-done.3.refs_0_), channel_id=1, source_target_pairs={{0,4},{4,0},{8,12},{12,8},{16,20},{20,16},{24,28},{28,24},{1,9},{5... | collective-permute-start | bytes 786440 | tf_op jit(solution)/shard_map/ppermute | solution.py:28
  18.7 12.7 %collective-permute-start.9 = (bf16[64,2048]{1,0:T(8,128)(2,1)S(1)}, bf16[64,2048]{1,0:T(8,128)(2,1)S(1)}, u32[]{:S(2)}, u32[]{:S(2)}) collective-permute-start(bf16[64,2048]{1,0:T(8,128)(2,1)S(1)} %collective-permute-done.3.refs_0_), channel_id=1, source_target_pairs={{0,8},{4,12},{8,0},{12,4},{16,24},{20,28},{24,16},{28,20},{1,5},{5... | collective-permute-start | bytes 786440 | tf_op jit(solution)/shard_map/ppermute | solution.py:28
  28.4 7.9 %collective-permute-start.5 = (bf16[64,2048]{1,0:T(8,128)(2,1)S(1)}, bf16[64,2048]{1,0:T(8,128)(2,1)S(1)}, u32[]{:S(2)}, u32[]{:S(2)}) collective-permute-start(bf16[64,2048]{1,0:T(8,128)(2,1)S(1)} %share.4), channel_id=1, source_target_pairs={{0,4},{4,0},{8,12},{12,8},{16,20},{20,16},{24,28},{28,24},{1,9},{5... | collective-permute-start | bytes 786440 | tf_op jit(solution)/shard_map/ppermute | solution.py:28
  36.4 20.2 %copy-start.3 = (s32[2]{0:T(128)S(1)}, s32[2]{0:T(128)}, u32[]{:S(2)}) copy-start(s32[2]{0:T(128)} %param.9) | copy-start | bytes 28
  36.4 20.8 %copy-start.4 = (f32[64,2]{0,1:T(2,128)S(1)}, f32[64,2]{0,1:T(2,128)}, u32[]{:S(2)}) copy-start(f32[64,2]{0,1:T(2,128)} %param.7) | copy-start | bytes 1540
  36.4 20.8 %copy-start.5 = (s32[64,2]{0,1:T(2,128)S(1)}, s32[64,2]{0,1:T(2,128)}, u32[]{:S(2)}) copy-start(s32[64,2]{0,1:T(2,128)} %param.8) | copy-start | bytes 1540
  36.4 6.4 %collective-permute-start.11 = (bf16[64,2048]{1,0:T(8,128)(2,1)S(1)}, bf16[64,2048]{1,0:T(8,128)(2,1)S(1)}, u32[]{:S(2)}, u32[]{:S(2)}) collective-permute-start(bf16[64,2048]{1,0:T(8,128)(2,1)S(1)} %add_convert_fusion.2), channel_id=1, source_target_pairs={{0,8},{4,12},{8,0},{12,4},{16,24},{20,28},{24,16},{28,20},{1,5},{5... | collective-permute-start | bytes 786440 | tf_op jit(solution)/shard_map/ppermute | solution.py:28
  36.5 9.3 %collective-permute-start.10 = (bf16[64,2048]{1,0:T(8,128)(2,1)S(1)}, bf16[64,2048]{1,0:T(8,128)(2,1)S(1)}, u32[]{:S(2)}, u32[]{:S(2)}) collective-permute-start(bf16[64,2048]{1,0:T(8,128)(2,1)S(1)} %get-tuple-element.29), channel_id=1, source_target_pairs={{0,4},{4,0},{8,12},{12,8},{16,20},{20,16},{24,28},{28,24},{1,9},{5... | collective-permute-start | bytes 786440 | tf_op jit(solution)/shard_map/ppermute | solution.py:28
  36.7 19.7 %collective-permute-start.6 = (bf16[128,2048]{1,0:T(8,128)(2,1)S(1)}, bf16[128,2048]{1,0:T(8,128)(2,1)S(1)}, u32[]{:S(2)}, u32[]{:S(2)}) collective-permute-start(bf16[128,2048]{1,0:T(8,128)(2,1)S(1)} %pad_maximum_fusion), channel_id=1, source_target_pairs={{0,8},{4,12},{8,0},{12,4},{16,24},{20,28},{24,16},{28,20},{1,5},{5... | collective-permute-start | bytes 1572872 | tf_op jit(solution)/shard_map/ppermute | solution.py:28
  45.9 12.5 %collective-permute-start.12 = (bf16[64,2048]{1,0:T(8,128)(2,1)S(1)}, bf16[64,2048]{1,0:T(8,128)(2,1)S(1)}, u32[]{:S(2)}, u32[]{:S(2)}) collective-permute-start(bf16[64,2048]{1,0:T(8,128)(2,1)S(1)} %add_convert_fusion.1), channel_id=1, source_target_pairs={{0,16},{4,20},{8,24},{12,28},{16,0},{20,4},{24,8},{28,12},{1,17},{... | collective-permute-start | bytes 786440 | tf_op jit(solution)/shard_map/ppermute | solution.py:28
  56.4 6.4 %collective-permute-start.7 = (bf16[64,2048]{1,0:T(8,128)(2,1)S(1)}, bf16[64,2048]{1,0:T(8,128)(2,1)S(1)}, u32[]{:S(2)}, u32[]{:S(2)}) collective-permute-start(bf16[64,2048]{1,0:T(8,128)(2,1)S(1)} %add_convert_fusion.4), channel_id=1, source_target_pairs={{0,4},{4,0},{8,12},{12,8},{16,20},{20,16},{24,28},{28,24},{1,9},{5... | collective-permute-start | bytes 786440 | tf_op jit(solution)/shard_map/ppermute | solution.py:28
